TPU v7x, 256 devices: a whole 4x4x8 slice. The times are simulated.
256 devices in a mesh: mem: 8 (over z_hi, core), patch: 32 (over z_lo, y, x).
Axes of the slice: x: 4, y: 4, z: 8 (z_hi: 4, z_lo: 2; z = z_hi * 2 + z_lo), core: 2. Of those that a mesh axis runs over, the one named last changes fastest.
Arguments:
- ensemble: float32 [8, 2, 55, 65536], P('mem', None, None, 'patch'), may hold values from -6 to 6
- field: float32 [2, 55, 65536], P(None, None, 'patch'), may hold values from -12 to 12
- diffusivity: float32 [65536], P('patch'), may hold values from 0.08 to 0.16
- neighbours: int32 [7, 65536], P(None, 'patch'), may hold values from 0 to 65535, as said below
- vertical_root: float32 [55, 55], replicated, may hold values from -3 to 3
Outputs:
- covariance_product: float32 [2, 55, 65536], P(None, None, 'patch')
- quadratic: float32 [], replicated
Inputs may be any that keep to these rules, and one draw needn't show every extreme that they name: Each neighbours[s, i] is a cell fewer than 128 positions from i in the cyclic order of the 65536 cells, or i itself in unused slots; the relation is symmetric, and no cell other than i appears twice among i's slots.
All inputs are finite; a program needn't handle non-finite values.
Results may differ from a plain program's by a relative error of at most 0.00011.
Values sent between devices are 32-bit elements; how exact they have to be, the bound alone decides.
No kernel may reach another device: no remote copies, remote signals or barrier semaphores. Data moves between devices by JAX's collectives and lax.ppermute only.
A program may use at most 192 MiB of HBM per device.

v0:
```python
import math

import jax
import jax.numpy as jnp
from jax import lax
from jax.sharding import PartitionSpec as P

STEPS = 4
ROW = 128


def with_halo(cells, sides, width):
    for axis, dim in sides:
        count = lax.axis_size(axis)
        head = lax.slice_in_dim(cells, 0, width, axis=dim)
        tail = lax.slice_in_dim(cells, cells.shape[dim] - width, cells.shape[dim], axis=dim)
        cells = jnp.concatenate(
            [
                lax.ppermute(tail, axis, [(i, (i + 1) % count) for i in range(count)]),
                cells,
                lax.ppermute(head, axis, [((i + 1) % count, i) for i in range(count)]),
            ],
            axis=dim,
        )
    return cells


def build_tiles(position, edge_rate, reach, block):
    count = position.shape[1]
    blocks = count // block
    starts = (jnp.arange(blocks, dtype=jnp.int32) * block)[None, :, None]
    local = position.reshape(7, blocks, block) - starts
    rates = edge_rate.reshape(7, blocks, block)
    window = jnp.arange(block + 2 * reach, dtype=jnp.int32)[None, :, None]
    tiles = jnp.zeros((blocks, block + 2 * reach, block), jnp.float32)
    for slot in range(7):
        tiles = tiles + jnp.where(local[slot][:, None, :] == window, rates[slot][:, None, :], 0.0)
    own_spot = (jnp.arange(block, dtype=jnp.int32) + reach)[None, None, :]
    keep_rate = 1.0 - jnp.sum(rates, axis=0)
    tiles = tiles + jnp.where(own_spot == window, keep_rate[:, None, :], 0.0)
    return tiles


def apply_tiles(padded, tiles, reach, block):
    blocks = tiles.shape[0]
    windows = jnp.stack(
        [padded[:, :, b * block : b * block + block + 2 * reach] for b in range(blocks)], axis=2
    )
    result = jnp.einsum("xlbj,bji->xlbi", windows, tiles, precision=lax.Precision.HIGHEST)
    return result.reshape(padded.shape[0], padded.shape[1], blocks * block)


def on_device(ensemble, field, diffusivity, neighbours, vertical_root):
    own_cells = diffusivity.shape[0]
    all_cells = own_cells * lax.axis_size("patch")
    offset = lax.axis_index("patch") * own_cells
    coeff_span = ROW
    coeff_wide = with_halo(diffusivity, (("patch", 0),), coeff_span)
    block = math.gcd(own_cells, 512)
    position = jnp.mod(neighbours - offset + ROW, all_cells)
    edge_rate = 0.5 * (
        coeff_wide[ROW : ROW + own_cells][None, :] + jnp.take(coeff_wide, position, axis=0)
    )
    tiles = build_tiles(position, edge_rate, ROW, block)

    def diffuse(state):
        for repeat in range(STEPS):
            padded = with_halo(state, (("patch", 2),), ROW)
            state = apply_tiles(padded, tiles, ROW, block)
        return state

    weighted = ensemble[:, 0] * field[0][None] + ensemble[:, 1] * field[1][None]
    spread = diffuse(weighted)
    lowered = jnp.einsum("lk,mlc->mkc", vertical_root, spread, precision=lax.Precision.HIGHEST)
    raised = jnp.einsum("kl,mlc->mkc", vertical_root, lowered, precision=lax.Precision.HIGHEST)
    smoothed = diffuse(raised)
    members_all = ensemble.shape[0] * lax.axis_size("mem")
    summand = jnp.sum(ensemble * smoothed[:, None], axis=0) / (members_all - 1.0)
    count_all = field.shape[0] * field.shape[1] * all_cells
    covariance_product = lax.psum(summand, "mem")
    quadratic = lax.psum(jnp.sum(field * covariance_product), "patch") / count_all
    return (covariance_product, quadratic)


def solution(mesh):
    return jax.shard_map(
        on_device,
        mesh=mesh,
        in_specs=(
            P("mem", None, None, "patch"),
            P(None, None, "patch"),
            P("patch"),
            P(None, "patch"),
            P(),
        ),
        out_specs=(P(None, None, "patch"), P()),
        check_vma=False,
    )
```

profile of v0, /device:TPU:32, one launch (start us, length us, event | category | flops | bytes accessed | tf_op | source)
XLA Modules:
  0.0 431.5 jit_solution(4133925059474241601)
XLA Ops:
  7.2 2.4 fusion.75
  9.7 0.7 fusion.76
  10.4 0.7 fusion.48
  11.2 1.6 collective-permute-start.2
  12.7 4.8 %collective-permute-start.3 = (f32[1,55,128]{2,1,0:T(8,128)S(1)}, f32[1,55,128]{2,1,0:T(8,128)S(1)}, u32[]{:S(2)}, u32[]{:S(2)}) collective-permute-start(f32[1,55,128]{2,1,0:T(8,128)S(1)} %get-tuple-element.64), channel_id=1, source_target_pairs={{1,0},{2,1},{3,2},{4,3},{5,4},{6,5},{7,6},{8,7},{9,8},{10,9},{11,1... | collective-permute-start | bytes 84488 | tf_op jit(solution)/shard_map/ppermute | solution.py:21
  17.5 6.5 %collective-permute-start.1 = (f32[128]{0:T(128)S(1)}, f32[128]{0:T(128)S(1)}, u32[]{:S(2)}, u32[]{:S(2)}) collective-permute-start(f32[128]{0:T(128)S(1)} %get-tuple-element.73), channel_id=1, source_target_pairs={{1,0},{2,1},{3,2},{4,3},{5,4},{6,5},{7,6},{8,7},{9,8},{10,9},{11,1... | collective-permute-start | bytes 1544 | tf_op jit(solution)/shard_map/ppermute | solution.py:21
  24.2 0.3 iota_compare_fusion.7
  24.5 0.7 collective-permute-done
  25.3 79.3 %gather_fusion = f32[14336]{0:T(1024)S(1)} fusion(f32[2304]{0:T(1024)S(1)} %pad_maximum_fusion.16, s32[14336]{0:T(1024)S(1)} %broadcast_clamp_fusion), kind=kCustom, calls=%fused_computation | custom fusion | bytes 172032 | tf_op jit(solution)/shard_map/jit(_take)/gather | solution.py:62
  104.7 0.2 slice_reduce_fusion.6
  105.0 10.4 %convolution_bitcast_fusion.9 = f32[1,55,4,512]{3,1,2,0:T(8,128)S(1)} fusion(f32[1,55,1,768]{3,1,2,0:T(8,128)S(1)} %get-tuple-element.62, f32[1,55,1,768]{3,1,2,0:T(8,128)S(1)} %get-tuple-element.60, f32[1,55,1,768]{3,1,2,0:T(8,128)S(1)} %get-tuple-element.61, f32[1,55,1,768]{3,1,2,0:T(8,128)S(1)} %get-tuple-element.59, f32[4,512]{1,0:T(4,128)S(1)} %sub.33, ...), kind=kOutput, calls=%fused_computation.19 | convolution fusion | flops 1073200128 | bytes 1642496 | tf_op jit(solution)/shard_map/xlbj,bji->xlbi/dot_general | solution.py:49
  115.5 0.3 copy.15
  115.8 0.3 reshape.154
  116.1 0.1 collective-permute-start.4
  116.2 7.1 %collective-permute-start.5 = (f32[1,55,128]{2,1,0:T(8,128)S(1)}, f32[1,55,128]{2,1,0:T(8,128)S(1)}, u32[]{:S(2)}, u32[]{:S(2)}) collective-permute-start(f32[1,55,128]{2,1,0:T(8,128)S(1)} %get-tuple-element.58), channel_id=1, source_target_pairs={{1,0},{2,1},{3,2},{4,3},{5,4},{6,5},{7,6},{8,7},{9,8},{10,9},{11,1... | collective-permute-start | bytes 84488 | tf_op jit(solution)/shard_map/ppermute | solution.py:21
  123.3 1.2 collective-permute-done.4
  124.5 0.3 collective-permute-done.5
  124.9 10.4 %convolution_bitcast_fusion.8 = f32[1,55,4,512]{3,1,2,0:T(8,128)S(1)} fusion(f32[1,55,1,768]{3,1,2,0:T(8,128)S(1)} %get-tuple-element.56, f32[1,55,1,768]{3,1,2,0:T(8,128)S(1)} %get-tuple-element.54, f32[1,55,1,768]{3,1,2,0:T(8,128)S(1)} %get-tuple-element.55, f32[1,55,1,768]{3,1,2,0:T(8,128)S(1)} %get-tuple-element.53, f32[4,512]{1,0:T(4,128)S(1)} %sub.33, ...), kind=kOutput, calls=%fused_computation.18 | convolution fusion | flops 1073200128 | bytes 1642496 | tf_op jit(solution)/shard_map/xlbj,bji->xlbi/dot_general | solution.py:49
  135.3 0.3 copy.16
  135.6 0.3 reshape.156
  136.0 0.1 collective-permute-start.6
  136.0 6.8 %collective-permute-start.7 = (f32[1,55,128]{2,1,0:T(8,128)S(1)}, f32[1,55,128]{2,1,0:T(8,128)S(1)}, u32[]{:S(2)}, u32[]{:S(2)}) collective-permute-start(f32[1,55,128]{2,1,0:T(8,128)S(1)} %get-tuple-element.52), channel_id=1, source_target_pairs={{1,0},{2,1},{3,2},{4,3},{5,4},{6,5},{7,6},{8,7},{9,8},{10,9},{11,1... | collective-permute-start | bytes 84488 | tf_op jit(solution)/shard_map/ppermute | solution.py:21
  142.8 1.6 collective-permute-done.6
  144.5 10.4 %convolution_bitcast_fusion.7 = f32[1,55,4,512]{3,1,2,0:T(8,128)S(1)} fusion(f32[1,55,1,768]{3,1,2,0:T(8,128)S(1)} %get-tuple-element.50, f32[1,55,1,768]{3,1,2,0:T(8,128)S(1)} %get-tuple-element.48, f32[1,55,1,768]{3,1,2,0:T(8,128)S(1)} %get-tuple-element.49, f32[1,55,1,768]{3,1,2,0:T(8,128)S(1)} %get-tuple-element.47, f32[4,512]{1,0:T(4,128)S(1)} %sub.33, ...), kind=kOutput, calls=%fused_computation.17 | convolution fusion | flops 1073200128 | bytes 1642496 | tf_op jit(solution)/shard_map/xlbj,bji->xlbi/dot_general | solution.py:49
  154.9 0.3 copy.17
  155.2 0.3 reshape.158
  155.5 0.1 collective-permute-start.8
  155.6 6.8 %collective-permute-start.9 = (f32[1,55,128]{2,1,0:T(8,128)S(1)}, f32[1,55,128]{2,1,0:T(8,128)S(1)}, u32[]{:S(2)}, u32[]{:S(2)}) collective-permute-start(f32[1,55,128]{2,1,0:T(8,128)S(1)} %get-tuple-element.46), channel_id=1, source_target_pairs={{1,0},{2,1},{3,2},{4,3},{5,4},{6,5},{7,6},{8,7},{9,8},{10,9},{11,1... | collective-permute-start | bytes 84488 | tf_op jit(solution)/shard_map/ppermute | solution.py:21
  162.4 1.5 collective-permute-done.8
  164.0 10.4 %convolution_bitcast_fusion.6 = f32[1,55,4,512]{3,1,2,0:T(8,128)S(1)} fusion(f32[1,55,1,768]{3,1,2,0:T(8,128)S(1)} %get-tuple-element.44, f32[1,55,1,768]{3,1,2,0:T(8,128)S(1)} %get-tuple-element.42, f32[1,55,1,768]{3,1,2,0:T(8,128)S(1)} %get-tuple-element.43, f32[1,55,1,768]{3,1,2,0:T(8,128)S(1)} %get-tuple-element.41, f32[4,512]{1,0:T(4,128)S(1)} %sub.33, ...), kind=kOutput, calls=%fused_computation.16 | convolution fusion | flops 1073200128 | bytes 1642496 | tf_op jit(solution)/shard_map/xlbj,bji->xlbi/dot_general | solution.py:49
  174.5 0.3 copy.44
  174.9 0.1 copy.27
  175.0 0.6 convolution_bitcast_fusion.1
  175.6 0.5 convolution_bitcast_fusion
  176.2 0.1 collective-permute-start.10
  176.3 6.9 %collective-permute-start.11 = (f32[1,55,128]{2,1,0:T(8,128)S(1)}, f32[1,55,128]{2,1,0:T(8,128)S(1)}, u32[]{:S(2)}, u32[]{:S(2)}) collective-permute-start(f32[1,55,128]{2,1,0:T(8,128)S(1)} %get-tuple-element.40), channel_id=1, source_target_pairs={{1,0},{2,1},{3,2},{4,3},{5,4},{6,5},{7,6},{8,7},{9,8},{10,9},{11,1... | collective-permute-start | bytes 84488 | tf_op jit(solution)/shard_map/ppermute | solution.py:21
  183.1 1.5 collective-permute-done.10
  184.7 10.4 %convolution_bitcast_fusion.5 = f32[1,55,4,512]{3,1,2,0:T(8,128)S(1)} fusion(f32[1,55,1,768]{3,1,2,0:T(8,128)S(1)} %get-tuple-element.38, f32[1,55,1,768]{3,1,2,0:T(8,128)S(1)} %get-tuple-element.36, f32[1,55,1,768]{3,1,2,0:T(8,128)S(1)} %get-tuple-element.37, f32[1,55,1,768]{3,1,2,0:T(8,128)S(1)} %get-tuple-element.35, f32[4,512]{1,0:T(4,128)S(1)} %sub.33, ...), kind=kOutput, calls=%fused_computation.15 | convolution fusion | flops 1073200128 | bytes 1642496 | tf_op jit(solution)/shard_map/xlbj,bji->xlbi/dot_general | solution.py:49
  195.2 0.3 copy.19
  195.5 0.3 reshape.163
  195.9 7.1 %collective-permute-start.13 = (f32[1,55,128]{2,1,0:T(8,128)S(1)}, f32[1,55,128]{2,1,0:T(8,128)S(1)}, u32[]{:S(2)}, u32[]{:S(2)}) collective-permute-start(f32[1,55,128]{2,1,0:T(8,128)S(1)} %get-tuple-element.34), channel_id=1, source_target_pairs={{1,0},{2,1},{3,2},{4,3},{5,4},{6,5},{7,6},{8,7},{9,8},{10,9},{11,1... | collective-permute-start | bytes 84488 | tf_op jit(solution)/shard_map/ppermute | solution.py:21
  203.0 1.3 collective-permute-done.12
  204.3 0.3 collective-permute-done.13
  204.6 10.4 %convolution_bitcast_fusion.4 = f32[1,55,4,512]{3,1,2,0:T(8,128)S(1)} fusion(f32[1,55,1,768]{3,1,2,0:T(8,128)S(1)} %get-tuple-element.32, f32[1,55,1,768]{3,1,2,0:T(8,128)S(1)} %get-tuple-element.30, f32[1,55,1,768]{3,1,2,0:T(8,128)S(1)} %get-tuple-element.31, f32[1,55,1,768]{3,1,2,0:T(8,128)S(1)} %get-tuple-element.29, f32[4,512]{1,0:T(4,128)S(1)} %sub.33, ...), kind=kOutput, calls=%fused_computation.14 | convolution fusion | flops 1073200128 | bytes 1642496 | tf_op jit(solution)/shard_map/xlbj,bji->xlbi/dot_general | solution.py:49
  215.0 0.3 copy.20
  215.3 0.3 reshape.165
  215.7 0.1 collective-permute-start.14
  215.8 6.8 %collective-permute-start.15 = (f32[1,55,128]{2,1,0:T(8,128)S(1)}, f32[1,55,128]{2,1,0:T(8,128)S(1)}, u32[]{:S(2)}, u32[]{:S(2)}) collective-permute-start(f32[1,55,128]{2,1,0:T(8,128)S(1)} %get-tuple-element.28), channel_id=1, source_target_pairs={{1,0},{2,1},{3,2},{4,3},{5,4},{6,5},{7,6},{8,7},{9,8},{10,9},{11,1... | collective-permute-start | bytes 84488 | tf_op jit(solution)/shard_map/ppermute | solution.py:21
  222.5 1.6 collective-permute-done.14
  224.2 10.4 %convolution_bitcast_fusion.3 = f32[1,55,4,512]{3,1,2,0:T(8,128)S(1)} fusion(f32[1,55,1,768]{3,1,2,0:T(8,128)S(1)} %get-tuple-element.26, f32[1,55,1,768]{3,1,2,0:T(8,128)S(1)} %get-tuple-element.24, f32[1,55,1,768]{3,1,2,0:T(8,128)S(1)} %get-tuple-element.25, f32[1,55,1,768]{3,1,2,0:T(8,128)S(1)} %get-tuple-element.23, f32[4,512]{1,0:T(4,128)S(1)} %sub.33, ...), kind=kOutput, calls=%fused_computation.13 | convolution fusion | flops 1073200128 | bytes 1642496 | tf_op jit(solution)/shard_map/xlbj,bji->xlbi/dot_general | solution.py:49
  234.6 0.3 copy.21
  234.9 0.3 reshape.167
  235.3 0.1 collective-permute-start.16
  235.4 6.8 %collective-permute-start.17 = (f32[1,55,128]{2,1,0:T(8,128)S(1)}, f32[1,55,128]{2,1,0:T(8,128)S(1)}, u32[]{:S(2)}, u32[]{:S(2)}) collective-permute-start(f32[1,55,128]{2,1,0:T(8,128)S(1)} %get-tuple-element.22), channel_id=1, source_target_pairs={{1,0},{2,1},{3,2},{4,3},{5,4},{6,5},{7,6},{8,7},{9,8},{10,9},{11,1... | collective-permute-start | bytes 84488 | tf_op jit(solution)/shard_map/ppermute | solution.py:21
  242.1 1.5 collective-permute-done.16
  243.8 10.4 %convolution_bitcast_fusion.2 = f32[1,55,4,512]{3,1,2,0:T(8,128)S(1)} fusion(f32[1,55,1,768]{3,1,2,0:T(8,128)S(1)} %get-tuple-element.20, f32[1,55,1,768]{3,1,2,0:T(8,128)S(1)} %get-tuple-element.18, f32[1,55,1,768]{3,1,2,0:T(8,128)S(1)} %get-tuple-element.19, f32[1,55,1,768]{3,1,2,0:T(8,128)S(1)} %get-tuple-element.17, f32[4,512]{1,0:T(4,128)S(1)} %sub.33, ...), kind=kOutput, calls=%fused_computation.12 | convolution fusion | flops 1073200128 | bytes 1642496 | tf_op jit(solution)/shard_map/xlbj,bji->xlbi/dot_general | solution.py:49
  254.2 0.3 copy.43
  254.6 0.1 copy.28
  254.8 0.9 copy-done.1
  255.7 1.5 multiply_bitcast_fusion
  257.2 78.3 %all-reduce.2.cloned.1.call-done = f32[2,55,2048]{2,0,1:T(2,128)} async-done(((f32[2,55,2048]{2,0,1:T(2,128)}), f32[2,55,2048]{2,0,1:T(2,128)}) %all-reduce.2.cloned.1.call-update) | async-done | bytes 901136 | tf_op jit(solution)/shard_map/psum | solution.py:80
  335.5 2.8 multiply_reduce_fusion
  338.3 83.4 %psum.15 = f32[]{:T(128)} all-reduce(f32[]{:T(128)} %multiply_reduce_fusion), channel_id=1, replica_groups=mesh['mem'=8,'patch'=32] {'patch'}, use_global_device_ids=true, to_apply=%region_3.4 | all-reduce | flops 1 | bytes 8 | tf_op jit(solution)/shard_map/psum | solution.py:81
  422.4 0.9 copy.46
  (62 shorter events, 1.3 us)
Async XLA Ops:
  7.2 167.9 %copy-start = (f32[55,55]{1,0:T(8,128)S(1)}, f32[55,55]{1,0:T(8,128)}, u32[]{:S(2)}) copy-start(f32[55,55]{1,0:T(8,128)} %param.9) | copy-start | bytes 36304
  7.2 2.5 copy-start.2
  7.2 328.3 %all-reduce.2.cloned.1.call-start = ((), (), s32[]{:S(2)}) async-start(), calls=%async_computation | async-start | bytes 1802240 | tf_op jit(solution)/shard_map/psum | solution.py:80
  10.4 7.1 %copy-start.5 = (f32[2048]{0:T(1024)S(1)}, f32[2048]{0:T(1024)}, u32[]{:S(2)}) copy-start(f32[2048]{0:T(1024)} %param.7) | copy-start | bytes 24580
  10.4 13.6 %copy-start.4 = (s32[7,2048]{1,0:T(8,128)S(1)}, s32[7,2048]{1,0:T(8,128)}, u32[]{:S(2)}) copy-start(s32[7,2048]{1,0:T(8,128)} %param.8) | copy-start | bytes 172036
  11.2 93.8 %collective-permute-start.2 = (f32[1,55,128]{2,1,0:T(8,128)S(1)}, f32[1,55,128]{2,1,0:T(8,128)S(1)}, u32[]{:S(2)}, u32[]{:S(2)}) collective-permute-start(f32[1,55,128]{2,1,0:T(8,128)S(1)} %get-tuple-element.63), channel_id=1, source_target_pairs={{0,1},{1,2},{2,3},{3,4},{4,5},{5,6},{6,7},{7,8},{8,9},{9,10},{10,1... | collective-permute-start | bytes 84488 | tf_op jit(solution)/shard_map/ppermute | solution.py:19
  12.7 92.2 %collective-permute-start.3 = (f32[1,55,128]{2,1,0:T(8,128)S(1)}, f32[1,55,128]{2,1,0:T(8,128)S(1)}, u32[]{:S(2)}, u32[]{:S(2)}) collective-permute-start(f32[1,55,128]{2,1,0:T(8,128)S(1)} %get-tuple-element.64), channel_id=1, source_target_pairs={{1,0},{2,1},{3,2},{4,3},{5,4},{6,5},{7,6},{8,7},{9,8},{10,9},{11,1... | collective-permute-start | bytes 84488 | tf_op jit(solution)/shard_map/ppermute | solution.py:21
  17.5 7.8 %collective-permute-start = (f32[128]{0:T(128)S(1)}, f32[128]{0:T(128)S(1)}, u32[]{:S(2)}, u32[]{:S(2)}) collective-permute-start(f32[128]{0:T(128)S(1)} %get-tuple-element.72), channel_id=1, source_target_pairs={{0,1},{1,2},{2,3},{3,4},{4,5},{5,6},{6,7},{7,8},{8,9},{9,10},{10,1... | collective-permute-start | bytes 1544 | tf_op jit(solution)/shard_map/ppermute | solution.py:19
  17.5 7.8 %collective-permute-start.1 = (f32[128]{0:T(128)S(1)}, f32[128]{0:T(128)S(1)}, u32[]{:S(2)}, u32[]{:S(2)}) collective-permute-start(f32[128]{0:T(128)S(1)} %get-tuple-element.73), channel_id=1, source_target_pairs={{1,0},{2,1},{3,2},{4,3},{5,4},{6,5},{7,6},{8,7},{9,8},{10,9},{11,1... | collective-permute-start | bytes 1544 | tf_op jit(solution)/shard_map/ppermute | solution.py:21
  116.1 8.4 %collective-permute-start.4 = (f32[1,55,128]{2,1,0:T(8,128)S(1)}, f32[1,55,128]{2,1,0:T(8,128)S(1)}, u32[]{:S(2)}, u32[]{:S(2)}) collective-permute-start(f32[1,55,128]{2,1,0:T(8,128)S(1)} %get-tuple-element.57), channel_id=1, source_target_pairs={{0,1},{1,2},{2,3},{3,4},{4,5},{5,6},{6,7},{7,8},{8,9},{9,10},{10,1... | collective-permute-start | bytes 84488 | tf_op jit(solution)/shard_map/ppermute | solution.py:19
  116.2 8.6 %collective-permute-start.5 = (f32[1,55,128]{2,1,0:T(8,128)S(1)}, f32[1,55,128]{2,1,0:T(8,128)S(1)}, u32[]{:S(2)}, u32[]{:S(2)}) collective-permute-start(f32[1,55,128]{2,1,0:T(8,128)S(1)} %get-tuple-element.58), channel_id=1, source_target_pairs={{1,0},{2,1},{3,2},{4,3},{5,4},{6,5},{7,6},{8,7},{9,8},{10,9},{11,1... | collective-permute-start | bytes 84488 | tf_op jit(solution)/shard_map/ppermute | solution.py:21
  136.0 8.5 %collective-permute-start.6 = (f32[1,55,128]{2,1,0:T(8,128)S(1)}, f32[1,55,128]{2,1,0:T(8,128)S(1)}, u32[]{:S(2)}, u32[]{:S(2)}) collective-permute-start(f32[1,55,128]{2,1,0:T(8,128)S(1)} %get-tuple-element.51), channel_id=1, source_target_pairs={{0,1},{1,2},{2,3},{3,4},{4,5},{5,6},{6,7},{7,8},{8,9},{9,10},{10,1... | collective-permute-start | bytes 84488 | tf_op jit(solution)/shard_map/ppermute | solution.py:19
  136.0 8.4 %collective-permute-start.7 = (f32[1,55,128]{2,1,0:T(8,128)S(1)}, f32[1,55,128]{2,1,0:T(8,128)S(1)}, u32[]{:S(2)}, u32[]{:S(2)}) collective-permute-start(f32[1,55,128]{2,1,0:T(8,128)S(1)} %get-tuple-element.52), channel_id=1, source_target_pairs={{1,0},{2,1},{3,2},{4,3},{5,4},{6,5},{7,6},{8,7},{9,8},{10,9},{11,1... | collective-permute-start | bytes 84488 | tf_op jit(solution)/shard_map/ppermute | solution.py:21
  155.5 8.4 %collective-permute-start.8 = (f32[1,55,128]{2,1,0:T(8,128)S(1)}, f32[1,55,128]{2,1,0:T(8,128)S(1)}, u32[]{:S(2)}, u32[]{:S(2)}) collective-permute-start(f32[1,55,128]{2,1,0:T(8,128)S(1)} %get-tuple-element.45), channel_id=1, source_target_pairs={{0,1},{1,2},{2,3},{3,4},{4,5},{5,6},{6,7},{7,8},{8,9},{9,10},{10,1... | collective-permute-start | bytes 84488 | tf_op jit(solution)/shard_map/ppermute | solution.py:19
  155.6 8.3 %collective-permute-start.9 = (f32[1,55,128]{2,1,0:T(8,128)S(1)}, f32[1,55,128]{2,1,0:T(8,128)S(1)}, u32[]{:S(2)}, u32[]{:S(2)}) collective-permute-start(f32[1,55,128]{2,1,0:T(8,128)S(1)} %get-tuple-element.46), channel_id=1, source_target_pairs={{1,0},{2,1},{3,2},{4,3},{5,4},{6,5},{7,6},{8,7},{9,8},{10,9},{11,1... | collective-permute-start | bytes 84488 | tf_op jit(solution)/shard_map/ppermute | solution.py:21
  176.2 8.5 %collective-permute-start.10 = (f32[1,55,128]{2,1,0:T(8,128)S(1)}, f32[1,55,128]{2,1,0:T(8,128)S(1)}, u32[]{:S(2)}, u32[]{:S(2)}) collective-permute-start(f32[1,55,128]{2,1,0:T(8,128)S(1)} %get-tuple-element.39), channel_id=1, source_target_pairs={{0,1},{1,2},{2,3},{3,4},{4,5},{5,6},{6,7},{7,8},{8,9},{9,10},{10,1... | collective-permute-start | bytes 84488 | tf_op jit(solution)/shard_map/ppermute | solution.py:19
  176.3 8.4 %collective-permute-start.11 = (f32[1,55,128]{2,1,0:T(8,128)S(1)}, f32[1,55,128]{2,1,0:T(8,128)S(1)}, u32[]{:S(2)}, u32[]{:S(2)}) collective-permute-start(f32[1,55,128]{2,1,0:T(8,128)S(1)} %get-tuple-element.40), channel_id=1, source_target_pairs={{1,0},{2,1},{3,2},{4,3},{5,4},{6,5},{7,6},{8,7},{9,8},{10,9},{11,1... | collective-permute-start | bytes 84488 | tf_op jit(solution)/shard_map/ppermute | solution.py:21
  195.8 8.5 %collective-permute-start.12 = (f32[1,55,128]{2,1,0:T(8,128)S(1)}, f32[1,55,128]{2,1,0:T(8,128)S(1)}, u32[]{:S(2)}, u32[]{:S(2)}) collective-permute-start(f32[1,55,128]{2,1,0:T(8,128)S(1)} %get-tuple-element.33), channel_id=1, source_target_pairs={{0,1},{1,2},{2,3},{3,4},{4,5},{5,6},{6,7},{7,8},{8,9},{9,10},{10,1... | collective-permute-start | bytes 84488 | tf_op jit(solution)/shard_map/ppermute | solution.py:19
  195.9 8.6 %collective-permute-start.13 = (f32[1,55,128]{2,1,0:T(8,128)S(1)}, f32[1,55,128]{2,1,0:T(8,128)S(1)}, u32[]{:S(2)}, u32[]{:S(2)}) collective-permute-start(f32[1,55,128]{2,1,0:T(8,128)S(1)} %get-tuple-element.34), channel_id=1, source_target_pairs={{1,0},{2,1},{3,2},{4,3},{5,4},{6,5},{7,6},{8,7},{9,8},{10,9},{11,1... | collective-permute-start | bytes 84488 | tf_op jit(solution)/shard_map/ppermute | solution.py:21
  215.7 8.5 %collective-permute-start.14 = (f32[1,55,128]{2,1,0:T(8,128)S(1)}, f32[1,55,128]{2,1,0:T(8,128)S(1)}, u32[]{:S(2)}, u32[]{:S(2)}) collective-permute-start(f32[1,55,128]{2,1,0:T(8,128)S(1)} %get-tuple-element.27), channel_id=1, source_target_pairs={{0,1},{1,2},{2,3},{3,4},{4,5},{5,6},{6,7},{7,8},{8,9},{9,10},{10,1... | collective-permute-start | bytes 84488 | tf_op jit(solution)/shard_map/ppermute | solution.py:19
  215.8 8.4 %collective-permute-start.15 = (f32[1,55,128]{2,1,0:T(8,128)S(1)}, f32[1,55,128]{2,1,0:T(8,128)S(1)}, u32[]{:S(2)}, u32[]{:S(2)}) collective-permute-start(f32[1,55,128]{2,1,0:T(8,128)S(1)} %get-tuple-element.28), channel_id=1, source_target_pairs={{1,0},{2,1},{3,2},{4,3},{5,4},{6,5},{7,6},{8,7},{9,8},{10,9},{11,1... | collective-permute-start | bytes 84488 | tf_op jit(solution)/shard_map/ppermute | solution.py:21
  235.3 8.4 %collective-permute-start.16 = (f32[1,55,128]{2,1,0:T(8,128)S(1)}, f32[1,55,128]{2,1,0:T(8,128)S(1)}, u32[]{:S(2)}, u32[]{:S(2)}) collective-permute-start(f32[1,55,128]{2,1,0:T(8,128)S(1)} %get-tuple-element.21), channel_id=1, source_target_pairs={{0,1},{1,2},{2,3},{3,4},{4,5},{5,6},{6,7},{7,8},{8,9},{9,10},{10,1... | collective-permute-start | bytes 84488 | tf_op jit(solution)/shard_map/ppermute | solution.py:19
  235.4 8.3 %collective-permute-start.17 = (f32[1,55,128]{2,1,0:T(8,128)S(1)}, f32[1,55,128]{2,1,0:T(8,128)S(1)}, u32[]{:S(2)}, u32[]{:S(2)}) collective-permute-start(f32[1,55,128]{2,1,0:T(8,128)S(1)} %get-tuple-element.22), channel_id=1, source_target_pairs={{1,0},{2,1},{3,2},{4,3},{5,4},{6,5},{7,6},{8,7},{9,8},{10,9},{11,1... | collective-permute-start | bytes 84488 | tf_op jit(solution)/shard_map/ppermute | solution.py:21
  254.5 1.2 copy-start.1
  335.5 86.8 %copy-start.3 = (f32[2,55,2048]{2,0,1:T(2,128)S(1)}, f32[2,55,2048]{2,0,1:T(2,128)}, u32[]{:S(2)}) copy-start(f32[2,55,2048]{2,0,1:T(2,128)} %all-reduce.2.cloned.1.call-done) | copy-start | bytes 2703364
Sparse Core Ops, SparseCore 0:
  257.4 78.1 all-reduce.1
where the time goes:
time: 436 us; the launch traced here: 431 us
  waiting for transfers between devices  90.1 us (21%)
  local copies, waits for them, and re-layouts  89.3 us (20%)
  matrix products  84.6 us (19%)
  blocking collectives  83.4 us (19%)
  starting transfers between devices  61.6 us (14%)
  between operations  16.6 us (4%)
  other arithmetic  5.89 us (1%)
    dot_general x8, matrix products, apply_tiles(): jnp.einsum('xlbj,bji->xlbi', windows, tiles, precision=lax.Precision.HIGH...  83.5 us
    psum x1, blocking collectives, on_device(): lax.psum(jnp.sum(field * covariance_product), 'patch') / count_all  83.4 us
    gather x2, local copies, waits for them, and re-layouts, on_device(): jnp.take(coeff_wide, position, axis=0)  79.3 us
    psum x1, waiting for transfers between devices, on_device(): covariance_product = lax.psum(summand, 'mem')  78.3 us
    ppermute x9, starting transfers between devices, with_halo(): lax.ppermute(head, axis, [((i + 1) % count, i) for i in range(count)])  59.4 us
    ppermute x9, waiting for transfers between devices, with_halo(): lax.ppermute(tail, axis, [(i, (i + 1) % count) for i in range(count)])  11 us
  transfers between devices with their start and end apart: 19, of which 13 were waited for; matrix products, arithmetic and copies ran while one was open for 19% of the time, Pallas kernels for 0%

commit v1 on v0

v1 whole, which is shorter than its diff:
```python
import functools

import jax
import jax.numpy as jnp
from jax import lax
from jax.experimental import pallas as pl
from jax.experimental.pallas import tpu as pltpu
from jax.sharding import PartitionSpec as P

STEPS = 8
REACH = 128
BLOCK = 256
HALO = STEPS * REACH
LEVELS = 55
LANES = 128


def prepare_kernel(
    all_cells, place, ens, field, diff, neigh, head, tail, ens_in, field_in, diff_in, neigh_in, sems
):
    own = diff.shape[1]
    tiles = own // LANES
    half = own // 2
    start = place[0]
    levels = (0, 16, 32, 48, LEVELS)
    copies = []
    for turn in range(4):
        rows = pl.ds(levels[turn] * 2 * tiles, (levels[turn + 1] - levels[turn]) * 2 * tiles)
        copies.append((
            pltpu.make_async_copy(ens.at[rows], ens_in.at[rows], sems.at[0, turn]),
            pltpu.make_async_copy(field.at[rows], field_in.at[rows], sems.at[1, turn]),
        ))
    others = (
        pltpu.make_async_copy(neigh, neigh_in, sems.at[2, 0]),
        pltpu.make_async_copy(diff, diff_in, sems.at[2, 1]),
    )
    for copy in others + copies[0] + copies[1] + copies[2] + copies[3]:
        copy.start()
    for copy in others:
        copy.wait()
    for part, out in ((0, head), (1, tail)):
        cols = pl.ds(part * half, half)
        out[55:56, :] = jnp.ones((1, half), jnp.float32)
        cell = lax.broadcasted_iota(jnp.int32, (7, half), 1) + (start + part * half)
        shift = neigh_in[:, cols] - cell
        shift = jnp.where(shift > all_cells // 2, shift - all_cells, shift)
        shift = jnp.where(shift < -(all_cells // 2), shift + all_cells, shift)
        out[56:63, :] = shift.astype(jnp.float32)
        out[63:64, :] = diff_in[:, cols]
    for turn in range(4):
        for copy in copies[turn]:
            copy.wait()
        low, high = levels[turn], levels[turn + 1]
        rows = pl.ds(low * 2 * tiles, (high - low) * 2 * tiles)
        ens_in[rows, :] = ens_in[rows, :] * field_in[rows, :]
        for part, out in ((0, head), (1, tail)):
            for tile in range(tiles // 2):
                at = low * 2 * tiles + 2 * (part * (tiles // 2) + tile)
                out[low:high, tile * LANES : (tile + 1) * LANES] = (
                    ens_in[pl.ds(at, high - low, stride=2 * tiles), :]
                    + ens_in[pl.ds(at + 1, high - low, stride=2 * tiles), :]
                )


def build_block(shift, store):
    row = lax.broadcasted_iota(jnp.int32, (LANES, LANES), 0).astype(jnp.float32).astype(jnp.bfloat16)
    lane = lax.broadcasted_iota(jnp.int32, (1, LANES), 1).astype(jnp.float32)
    one = jnp.ones((LANES, LANES), jnp.bfloat16)
    zero = jnp.zeros((LANES, LANES), jnp.bfloat16)
    for chunk in range(BLOCK // LANES):
        part = shift[:, chunk * LANES : (chunk + 1) * LANES]
        for side in range(3):
            local = part + (lane + (1.0 - side) * LANES)
            inside = jnp.logical_and(jnp.logical_and(local >= 0.0, local < LANES), part != 0.0)
            local = jnp.where(inside, local, -1.0).astype(jnp.bfloat16)
            hit = zero
            for slot in range(7):
                hit = jnp.where(row == local[slot : slot + 1, :], one, hit)
            store(chunk + side, chunk, hit)
        store((chunk + 3) % 4, chunk, zero)


def split(value, coeff):
    both = jnp.concatenate([value, coeff * value], axis=0)
    high = both.astype(jnp.bfloat16)
    low = (both - high.astype(jnp.float32)).astype(jnp.bfloat16)
    return high, low


def store_parts(buf, at, parts):
    width = parts[0].shape[1]
    buf[0:112, at : at + width] = parts[0]
    buf[112:224, at : at + width] = parts[1]


def sweep(state, now, later, margin, places):
    def matmul(at, width, matrix):
        window = now[:, at + margin - REACH : at + margin + width + REACH]
        return jnp.dot(window, matrix, preferred_element_type=jnp.float32)

    def finish(at, width, kept, total):
        coeff = state[56:57, at : at + width]
        value = state[0:56, at : at + width]
        change = coeff * (total[0:56] + total[112:168]) + (total[56:112] + total[168:224])
        value = value * (1.0 - change[55:56]) + change
        if kept:
            state[0:56, at : at + width] = value
        if later is not None:
            store_parts(later, at + margin, split(value, coeff))

    waiting = None
    for at, width, matrix, kept in places:
        total = matmul(at, width, matrix())
        if waiting is not None:
            finish(*waiting)
        waiting = (at, width, kept, total)
    finish(*waiting)


def interior_blocks(step, count):
    skip = (step + 1) // 2
    return range(skip, count - skip)


def interior_kernel(head, tail, adj, state, buf0, buf1, buf2, buf3):
    bufs = (buf0, buf1, buf2, buf3)
    blocks = adj.shape[0]
    half = blocks // 2
    for block in range(blocks):
        source, at = (head, block * BLOCK) if block < half else (tail, (block - half) * BLOCK)

        def store(down, across, value):
            adj[block, down * LANES : (down + 1) * LANES, across * LANES : (across + 1) * LANES] = value

        value = source[:, at : at + BLOCK]
        build_block(value[56:63], store)
        coeff = 0.5 * value[63:64]
        here = block * BLOCK
        state[0:56, here : here + BLOCK] = value[0:56]
        state[56:64, here : here + BLOCK] = jnp.broadcast_to(coeff, (8, BLOCK))
        store_parts(buf0, here, split(value[0:56], coeff))
    for step in range(1, STEPS - 1):
        whole = interior_blocks(step, blocks)
        places = [(block * BLOCK, BLOCK, functools.partial(lambda b: adj[b], block), True) for block in whole]
        if step % 2:
            low, high = whole[0] - 1, whole[-1] + 1
            places.append((low * BLOCK + REACH, REACH, lambda: adj[low, REACH:, REACH:], False))
            places.append((high * BLOCK, REACH, lambda: adj[high, : BLOCK + REACH, :REACH], False))
        sweep(state, bufs[(step - 1) % 4], bufs[step % 4], 0, places)


def smooth_kernel(
    ids, left, head, tail, right, root, ens, inner, done, own0, own1, own2, own3,
    keep, send, state, outer, buf0, buf1, buf2, buf3, square, rowed,
):
    wide = state.shape[1]
    own = wide - 2 * HALO
    tiles = own // LANES
    blocks = wide // BLOCK
    fringe = HALO // BLOCK
    bufs = (buf0, buf1, buf2, buf3)

    state[:, HALO : HALO + own] = done[...]
    edge = jnp.zeros((224, REACH), jnp.bfloat16)
    buf0[:, 0:REACH] = edge
    buf0[:, REACH + wide : REACH + wide + REACH] = edge
    buf2[:, 2 * REACH : 3 * REACH] = edge
    buf2[:, wide - REACH : wide] = edge

    def carry_over(step, first, last):
        source, target = (own0, own1, own2, own3)[step % 4], bufs[step % 4]
        for low, high in ((first, last), (own - last, own - first)):
            target[:, REACH + HALO + low : REACH + HALO + high] = source[:, low:high]

    for step in range(STEPS - 1):
        inside = interior_blocks(step, own // BLOCK)
        if step % 2 == 0:
            carry_over(step, inside[0] * BLOCK, min(inside[0] * BLOCK + BLOCK + REACH, own // 2))
        else:
            carry_over(step, inside[0] * BLOCK, inside[0] * BLOCK + REACH)

    for which, part in ((0, left), (1, right)):
        for index in range(fringe):
            block = which * fringe + index
            value = part[:, index * BLOCK : (index + 1) * BLOCK]
            coeff = 0.5 * value[63:64]
            here = which * (HALO + own) + index * BLOCK
            state[0:56, here : here + BLOCK] = value[0:56]
            state[56:64, here : here + BLOCK] = jnp.broadcast_to(coeff, (8, BLOCK))
            store_parts(buf0, here + REACH, split(value[0:56], coeff))

            def store(down, across, piece):
                outer[block, down * LANES : (down + 1) * LANES, across * LANES : (across + 1) * LANES] = piece

            build_block(value[56:63], store)

    def adjacency(block):
        if block < fringe:
            return outer[block]
        if block < blocks - fringe:
            return inner[block - fringe]
        return outer[block - (blocks - 2 * fringe)]

    for step in range(1, STEPS + 1):
        inside = [fringe + block for block in interior_blocks(step, own // BLOCK)]
        places = [
            (block * BLOCK, BLOCK, functools.partial(adjacency, block), True)
            for block in range(step // 2, blocks - step // 2)
            if block not in inside
        ]
        sweep(state, bufs[(step - 1) % 4], bufs[step % 4] if step < STEPS else None, REACH, places)

    square[...] = jnp.zeros(square.shape, jnp.float32)
    square[0:LEVELS, 0:LEVELS] = root[...]
    matrix = lax.dot_general(
        square[...], square[...], (((1,), (1,)), ((), ())),
        precision=lax.Precision.HIGHEST, preferred_element_type=jnp.float32,
    )
    matrix_high = matrix.astype(jnp.bfloat16)
    matrix_low = (matrix - matrix_high.astype(jnp.float32)).astype(jnp.bfloat16)
    stacked = jnp.concatenate([matrix_high, matrix_low], axis=0)
    total = jnp.zeros((1, BLOCK), jnp.float32)
    for block in range(own // BLOCK):
        value = state[:, HALO + block * BLOCK : HALO + (block + 1) * BLOCK]
        high = value.astype(jnp.bfloat16)
        low = (value - high.astype(jnp.float32)).astype(jnp.bfloat16)
        first = jnp.dot(stacked, high, preferred_element_type=jnp.float32)
        second = jnp.dot(matrix_high, low, preferred_element_type=jnp.float32)
        smoothed = first[0:LEVELS] + (first[64 : 64 + LEVELS] + second[0:LEVELS])
        source = head if block < own // BLOCK // 2 else tail
        at = (block * BLOCK) % head.shape[1]
        total = total + jnp.sum(source[0:LEVELS, at : at + BLOCK] * smoothed, axis=0, keepdims=True)
        for tile in range(BLOCK // LANES):
            spot = block * (BLOCK // LANES) + tile
            rowed[pl.ds(spot, LEVELS, stride=tiles), :] = smoothed[:, tile * LANES : (tile + 1) * LANES]
    slots = 4
    chunk = rowed.shape[0] // slots
    spot = pl.ds(slots * chunk, 8)
    keep[spot, :] = send[spot, :] = jnp.broadcast_to(jnp.sum(total, axis=1, keepdims=True), (8, LANES))

    mine, chip = ids[0], ids[1]
    spare = slots * chunk - LEVELS * tiles

    def products(slot, start, first, count):
        rows = rowed[pl.ds(pl.multiple_of(start + first, 8), count), :]
        at = 2 * (start + first)
        here = pl.ds(slot * chunk + first, count)
        keep[here, :] = ens[pl.ds(at + mine, count, stride=2), :] * rows
        send[here, :] = ens[pl.ds(at + 1 - mine, count, stride=2), :] * rows

    for slot in range(slots):
        target = lax.rem(chip + slot, slots)
        start = target * chunk
        products(slot, start, 0, chunk - spare)

        @pl.when(target < slots - 1)
        def _():
            products(slot, start, chunk - spare, spare)

        @pl.when(target == slots - 1)
        def _():
            nothing = jnp.zeros((spare, LANES), jnp.float32)
            keep[pl.ds((slot + 1) * chunk - spare, spare), :] = nothing
            send[pl.ds((slot + 1) * chunk - spare, spare), :] = nothing


def place_kernel(scale, ids, same, other, out, quadratic, lines, sems):
    mine, chip = ids[0], ids[1]
    slots = same.shape[0]
    chunk = lines.shape[0] // slots // 2
    short = 2 * chunk - (lines.shape[0] - out.shape[0])

    def copies(slot):
        source = lax.rem(chip + slots - slot, slots)
        start = pl.multiple_of(source * 2 * chunk, 8)
        rows = pl.ds(start, short)
        rest = pl.ds(pl.multiple_of(start + short, 8), 2 * chunk - short)
        return source, start, (
            pltpu.make_async_copy(lines.at[rows], out.at[rows], sems.at[0, slot]),
            pltpu.make_async_copy(lines.at[rest], out.at[rest], sems.at[1, slot]),
        )

    for slot in range(slots):
        source, start, (main, extra) = copies(slot)
        lines[pl.ds(start + mine, chunk, stride=2), :] = same[slot, 0:chunk, :]
        lines[pl.ds(start + 1 - mine, chunk, stride=2), :] = other[slot, 0:chunk, :]
        main.start()
        pl.when(source < slots - 1)(extra.start)
    terms = [same[slot, chunk : chunk + 8, :] for slot in range(slots)]
    quadratic[0, 0] = jnp.max((terms[0] + terms[2]) + (terms[1] + terms[3])) * scale
    for slot in range(slots):
        source, start, (main, extra) = copies(slot)
        main.wait()
        pl.when(source < slots - 1)(extra.wait)


def interleave(array):
    cells = array.shape[2]
    array = array.reshape(2, LEVELS, cells // LANES, LANES)
    return array.transpose(1, 2, 0, 3).reshape(-1, LANES)


def on_device(ensemble, field, diffusivity, neighbours, vertical_root):
    own = diffusivity.shape[0]
    patches = lax.axis_size("patch")
    members = lax.axis_size("mem")
    chips = members // 2
    all_cells = own * patches
    half = own // 2
    tiles = own // LANES
    vmem = pl.BlockSpec(memory_space=pltpu.VMEM)
    smem = pl.BlockSpec(memory_space=pltpu.SMEM)
    hbm = pl.BlockSpec(memory_space=pltpu.HBM)
    params = pltpu.CompilerParams(vmem_limit_bytes=32 * 1024 * 1024)
    place = (lax.axis_index("patch") * own).astype(jnp.int32).reshape(1)
    member = lax.axis_index("mem")
    ids = jnp.stack([lax.rem(member, 2), member // 2]).astype(jnp.int32)
    ens_rows = interleave(ensemble[0])
    field_rows = interleave(field)

    in_hbm = [
        pltpu.with_memory_space_constraint(array, pltpu.HBM)
        for array in (ens_rows, field_rows, diffusivity.reshape(1, own), neighbours)
    ]
    side = jax.ShapeDtypeStruct((64, half), jnp.float32)
    head, tail = pl.pallas_call(
        functools.partial(prepare_kernel, all_cells),
        out_shape=(side, side),
        in_specs=[smem, hbm, hbm, hbm, hbm],
        out_specs=(vmem, vmem),
        scratch_shapes=[
            pltpu.VMEM(ens_rows.shape, jnp.float32),
            pltpu.VMEM(ens_rows.shape, jnp.float32),
            pltpu.VMEM((1, own), jnp.float32),
            pltpu.VMEM((7, own), jnp.int32),
            pltpu.SemaphoreType.DMA((3, 4)),
        ],
        compiler_params=params,
        name="prepare",
    )(place, *in_hbm)

    left = lax.ppermute(tail, "patch", [(i, (i + 1) % patches) for i in range(patches)])
    right = lax.ppermute(head, "patch", [((i + 1) % patches, i) for i in range(patches)])

    parts = jax.ShapeDtypeStruct((224, own), jnp.bfloat16)
    inside = pl.pallas_call(
        interior_kernel,
        out_shape=(
            jax.ShapeDtypeStruct((own // BLOCK, 2 * BLOCK, BLOCK), jnp.bfloat16),
            jax.ShapeDtypeStruct((64, own), jnp.float32),
            parts, parts, parts, parts,
        ),
        in_specs=[vmem] * 2,
        out_specs=(vmem,) * 6,
        compiler_params=params,
        cost_estimate=pl.CostEstimate(flops=4_000_000_000, bytes_accessed=4_000_000, transcendentals=0),
        name="interior",
    )(head, tail)

    wide = own + 2 * HALO
    chunk = 56 * tiles // chips
    terms = jax.ShapeDtypeStruct((chips * chunk + 8, LANES), jnp.float32)
    wide_parts = pltpu.VMEM((224, wide + 2 * REACH), jnp.bfloat16)
    keep, send = pl.pallas_call(
        smooth_kernel,
        out_shape=(terms, terms),
        in_specs=[smem] + [vmem] * 12,
        out_specs=(vmem, vmem),
        scratch_shapes=[
            pltpu.VMEM((64, wide), jnp.float32),
            pltpu.VMEM((2 * HALO // BLOCK, 2 * BLOCK, BLOCK), jnp.bfloat16),
            wide_parts, wide_parts, wide_parts, wide_parts,
            pltpu.VMEM((64, 64), jnp.float32),
            pltpu.VMEM((56 * tiles, LANES), jnp.float32),
        ],
        compiler_params=params,
        name="smooth",
    )(ids, left, head, tail, right, vertical_root, ens_rows, *inside)

    def shift_chips(array, by):
        pairs = [(2 * z + c, 2 * ((z + by) % chips) + c) for z in range(chips) for c in range(2)]
        return lax.ppermute(array, "mem", pairs)

    twin = [(i, i ^ 1) for i in range(members)]
    order = [2, 1, 3]
    pair_sum = keep + lax.ppermute(send, "mem", twin)
    pieces = [pair_sum[chunk * slot : chunk * (slot + 1)] for slot in range(chips)]
    terms = {by: shift_chips(pieces[by], by) for by in order}
    spread = jnp.broadcast_to(pair_sum[chips * chunk : chips * chunk + 1][None], (patches, 1, LANES))
    spread = lax.all_to_all(spread, "patch", 0, 0)
    terms, spread = lax.optimization_barrier((terms, spread))
    total = (pieces[0] + terms[1] + terms[2] + terms[3]) / (members - 1.0)
    total = jnp.concatenate([total, jnp.broadcast_to(jnp.sum(spread, axis=0), (8, LANES))], axis=0)
    copies = {by: shift_chips(total, by) for by in order}
    same = jnp.stack([total, copies[1], copies[2], copies[3]])
    other = lax.ppermute(same, "mem", twin)
    scale = 1.0 / ((members - 1.0) * field.shape[0] * field.shape[1] * all_cells)
    rows, quadratic = pl.pallas_call(
        functools.partial(place_kernel, scale),
        out_shape=(
            jax.ShapeDtypeStruct(field_rows.shape, jnp.float32),
            jax.ShapeDtypeStruct((1, 1), jnp.float32),
        ),
        in_specs=[smem, vmem, vmem],
        out_specs=(hbm, smem),
        scratch_shapes=[
            pltpu.VMEM((chips * chunk * 2, LANES), jnp.float32),
            pltpu.SemaphoreType.DMA((2, chips)),
        ],
        compiler_params=params,
        name="place",
    )(ids, same, other)
    product = rows.reshape(LEVELS, tiles, 2, LANES).transpose(2, 0, 1, 3).reshape(field.shape)
    return (product, quadratic.reshape(()))


def solution(mesh):
    return jax.shard_map(
        on_device,
        mesh=mesh,
        in_specs=(
            P("mem", None, None, "patch"),
            P(None, None, "patch"),
            P("patch"),
            P(None, "patch"),
            P(),
        ),
        out_specs=(P(None, None, "patch"), P()),
        check_vma=False,
    )
```

time: 436 us -> 70.3 us (0.16)
  the two profiles are of different devices: /device:TPU:32 before, /device:TPU:1 now
where the time goes in v1:
time: 70.3 us; the launch traced here: 70.2 us
  starting transfers between devices  26.5 us (38%)
  Pallas kernels  14.7 us (21%)
  blocking collectives  14.3 us (20%)
  waiting for transfers between devices  13.5 us (19%)
  between operations  0.87 us (1%)
    ppermute x6, starting transfers between devices, shift_chips(): return lax.ppermute(array, 'mem', pairs)  14.7 us
    all_to_all x1, blocking collectives, on_device(): spread = lax.all_to_all(spread, 'patch', 0, 0)  14.3 us
    ppermute x6, waiting for transfers between devices, shift_chips(): return lax.ppermute(array, 'mem', pairs)  9.99 us
    pallas_call x1, Pallas kernels, on_device(): pl.pallas_call(smooth_kernel, out_shape=(terms, terms), in_specs=[smem] +...  7.13 us
    ppermute x1, starting transfers between devices, on_device(): lax.ppermute(head, 'patch', [((i + 1) % patches, i) for i in range(patche...  5.16 us
    pallas_call x1, Pallas kernels, on_device(): pl.pallas_call(interior_kernel, out_shape=(jax.ShapeDtypeStruct((own // B...  3.75 us
    ppermute x1, starting transfers between devices, on_device(): pair_sum = keep + lax.ppermute(send, 'mem', twin)  2.81 us
    ppermute x1, starting transfers between devices, on_device(): lax.ppermute(tail, 'patch', [(i, (i + 1) % patches) for i in range(patche...  2.12 us
  transfers between devices with their start and end apart: 10, of which 6 were waited for; matrix products, arithmetic and copies ran while one was open for 0% of the time, Pallas kernels for 5%

profile of v1, /device:TPU:1, one launch (start us, length us, event | category | flops | bytes accessed | tf_op | source)
XLA Modules:
  0.0 70.2 jit_solution(8796505272402833187)
XLA Ops:
  0.6 1.8 %prepare.1 = (f32[64,1024]{1,0:T(8,128)S(1)}, f32[64,1024]{1,0:T(8,128)S(1)}) custom-call(s32[1]{0:T(128)} %bitcast.2.place, f32[1760,128]{1,0:T(8,128)} %bitcast.27, f32[1760,128]{1,0:T(8,128)} %bitcast.29, f32[1,2048]{1,0:T(1,128)} %bitcast.33, s32[7,2048]{1,0:T(8,128)} %neigh.1), custom_call_target="tpu_custom_call" | custom-call | tf_op jit(solution)/shard_map/prepare/pallas_call | solution.py:326
  2.4 2.1 %collective-permute-start = (f32[64,1024]{1,0:T(8,128)S(1)}, f32[64,1024]{1,0:T(8,128)S(1)}, u32[]{:S(2)}, u32[]{:S(2)}) collective-permute-start(f32[64,1024]{1,0:T(8,128)S(1)} %get-tuple-element.18.tail), channel_id=1, source_target_pairs={{0,1},{1,2},{2,3},{3,4},{4,5},{5,6},{6,7},{7,8},{8,9},{9,10},{10,1... | collective-permute-start | bytes 786440 | tf_op jit(solution)/shard_map/ppermute | solution.py:342
  4.6 5.2 %collective-permute-start.1 = (f32[64,1024]{1,0:T(8,128)S(1)}, f32[64,1024]{1,0:T(8,128)S(1)}, u32[]{:S(2)}, u32[]{:S(2)}) collective-permute-start(f32[64,1024]{1,0:T(8,128)S(1)} %get-tuple-element.19.head), channel_id=1, source_target_pairs={{1,0},{2,1},{3,2},{4,3},{5,4},{6,5},{7,6},{8,7},{9,8},{10,9},{11,1... | collective-permute-start | bytes 786440 | tf_op jit(solution)/shard_map/ppermute | solution.py:343
  9.7 0.1 pad_add_fusion.ids
  9.8 0.0 copy-start
  9.8 0.0 copy-start.1
  9.8 3.7 %interior.1 = (bf16[8,512,256]{2,1,0:T(8,128)(2,1)S(1)}, f32[64,2048]{1,0:T(8,128)S(1)}, bf16[224,2048]{1,0:T(8,128)(2,1)S(1)}, bf16[224,2048]{1,0:T(8,128)(2,1)...) custom-call(f32[64,1024]{1,0:T(8,128)S(1)} %get-tuple-element.19.head, ...), custom_call_target="tpu_custom_call" | custom-call | flops 4000000000 | bytes 4000000 | tf_op jit(solution)/shard_map/interior/pallas_call | solution.py:346
  13.6 0.6 collective-permute-done.left
  14.2 0.0 collective-permute-done.1.right
  14.2 0.0 copy-done
  14.2 0.0 copy-done.1
  14.2 7.1 %smooth.1 = (f32[904,128]{1,0:T(8,128)S(1)}, f32[904,128]{1,0:T(8,128)S(1)}) custom-call(s32[2]{0:T(128)S(1)} %pad_add_fusion.ids, f32[64,1024]{1,0:T(8,128)S(1)} %collective-permute-done.left, f32[64,1024]{1,0:T(8,128)S(1)} %get-tuple-element.19.head, f32[64,1024]{1,0:T(8,128)S(1)} %get-tuple-element.18.tail, f32[64,1024]{1,0:T(8,128)S(1)} %collective-permute-done.1.right, ...), custom_call_target="tpu_custom_call" | custom-call | tf_op jit(solution)/shard_map/smooth/pallas_call | solution.py:364
  21.3 2.8 %collective-permute-start.2 = (f32[904,128]{1,0:T(8,128)S(1)}, f32[904,128]{1,0:T(8,128)S(1)}, u32[]{:S(2)}, u32[]{:S(2)}) collective-permute-start(f32[904,128]{1,0:T(8,128)S(1)} %get-tuple-element.27), channel_id=1, source_target_pairs={{0,32},{32,0},{64,96},{96,64},{128,160},{160,128},{192,224},{224,1... | collective-permute-start | bytes 1388552 | tf_op jit(solution)/shard_map/ppermute | solution.py:386
  24.1 1.4 %collective-permute-done.2 = f32[904,128]{1,0:T(8,128)S(1)} collective-permute-done((f32[904,128]{1,0:T(8,128)S(1)}, f32[904,128]{1,0:T(8,128)S(1)}, u32[]{:S(2)}, u32[]{:S(2)}) %collective-permute-start.2) | collective-permute-done | bytes 462880 | tf_op jit(solution)/shard_map/ppermute | solution.py:386
  25.6 0.1 add.13
  25.7 5.7 %collective-permute-start.5 = (f32[224,128]{1,0:T(8,128)S(1)}, f32[224,128]{1,0:T(8,128)S(1)}, u32[]{:S(2)}, u32[]{:S(2)}) collective-permute-start(f32[224,128]{1,0:T(8,128)S(1)} %get-tuple-element.34), channel_id=1, source_target_pairs={{0,192},{32,224},{64,0},{96,32},{128,64},{160,96},{192,128},{224,1... | collective-permute-start | bytes 344072 | tf_op jit(solution)/shard_map/ppermute | solution.py:382
  31.4 1.0 %collective-permute-start.4 = (f32[224,128]{1,0:T(8,128)S(1)}, f32[224,128]{1,0:T(8,128)S(1)}, u32[]{:S(2)}, u32[]{:S(2)}) collective-permute-start(f32[224,128]{1,0:T(8,128)S(1)} %get-tuple-element.35), channel_id=1, source_target_pairs={{0,128},{32,160},{64,192},{96,224},{128,0},{160,32},{192,64},{224,... | collective-permute-start | bytes 344072 | tf_op jit(solution)/shard_map/ppermute | solution.py:382
  32.3 2.3 %collective-permute-start.3 = (f32[224,128]{1,0:T(8,128)S(1)}, f32[224,128]{1,0:T(8,128)S(1)}, u32[]{:S(2)}, u32[]{:S(2)}) collective-permute-start(f32[224,128]{1,0:T(8,128)S(1)} %get-tuple-element.36), channel_id=1, source_target_pairs={{0,64},{32,96},{64,128},{96,160},{128,192},{160,224},{192,0},{224,... | collective-permute-start | bytes 344072 | tf_op jit(solution)/shard_map/ppermute | solution.py:382
  34.6 14.3 %all_to_all.5 = f32[32,1,128]{2,1,0:T(1,128)S(1)} all-to-all(f32[32,1,128]{2,1,0:T(1,128)S(1)} %broadcast_in_dim.14), channel_id=1, replica_groups=mesh['mem'=8,'patch'=32] {'patch'}, dimensions={0} | all-to-all | bytes 32768 | tf_op jit(solution)/shard_map/all_to_all | solution.py:390
  48.9 0.0 collective-permute-done.5
  48.9 0.0 collective-permute-done.4
  48.9 0.0 collective-permute-done.3
  48.9 0.1 reduce_sum.9
  49.0 2.2 %collective-permute-start.7 = (f32[232,128]{1,0:T(8,128)S(1)}, f32[232,128]{1,0:T(8,128)S(1)}, u32[]{:S(2)}, u32[]{:S(2)}) collective-permute-start(f32[232,128]{1,0:T(8,128)S(1)} %get-tuple-element.38), channel_id=1, source_target_pairs={{0,128},{32,160},{64,192},{96,224},{128,0},{160,32},{192,64},{224,... | collective-permute-start | bytes 356360 | tf_op jit(solution)/shard_map/ppermute | solution.py:382
  51.2 1.3 %collective-permute-start.6 = (f32[232,128]{1,0:T(8,128)S(1)}, f32[232,128]{1,0:T(8,128)S(1)}, u32[]{:S(2)}, u32[]{:S(2)}) collective-permute-start(f32[232,128]{1,0:T(8,128)S(1)} %get-tuple-element.38), channel_id=1, source_target_pairs={{0,64},{32,96},{64,128},{96,160},{128,192},{160,224},{192,0},{224,... | collective-permute-start | bytes 356360 | tf_op jit(solution)/shard_map/ppermute | solution.py:382
  52.5 2.3 %collective-permute-start.8 = (f32[232,128]{1,0:T(8,128)S(1)}, f32[232,128]{1,0:T(8,128)S(1)}, u32[]{:S(2)}, u32[]{:S(2)}) collective-permute-start(f32[232,128]{1,0:T(8,128)S(1)} %get-tuple-element.38), channel_id=1, source_target_pairs={{0,192},{32,224},{64,0},{96,32},{128,64},{160,96},{192,128},{224,1... | collective-permute-start | bytes 356360 | tf_op jit(solution)/shard_map/ppermute | solution.py:382
  54.8 2.9 %collective-permute-done.7 = f32[232,128]{1,0:T(8,128)S(1)} collective-permute-done((f32[232,128]{1,0:T(8,128)S(1)}, f32[232,128]{1,0:T(8,128)S(1)}, u32[]{:S(2)}, u32[]{:S(2)}) %collective-permute-start.7) | collective-permute-done | bytes 118816 | tf_op jit(solution)/shard_map/ppermute | solution.py:382
  57.7 4.4 %collective-permute-done.6 = f32[232,128]{1,0:T(8,128)S(1)} collective-permute-done((f32[232,128]{1,0:T(8,128)S(1)}, f32[232,128]{1,0:T(8,128)S(1)}, u32[]{:S(2)}, u32[]{:S(2)}) %collective-permute-start.6) | collective-permute-done | bytes 118816 | tf_op jit(solution)/shard_map/ppermute | solution.py:382
  62.1 2.7 %collective-permute-done.8 = f32[232,128]{1,0:T(8,128)S(1)} collective-permute-done((f32[232,128]{1,0:T(8,128)S(1)}, f32[232,128]{1,0:T(8,128)S(1)}, u32[]{:S(2)}, u32[]{:S(2)}) %collective-permute-start.8) | collective-permute-done | bytes 118816 | tf_op jit(solution)/shard_map/ppermute | solution.py:382
  64.8 1.7 %collective-permute-start.9 = (f32[4,232,128]{2,1,0:T(8,128)S(1)}, f32[4,232,128]{2,1,0:T(8,128)S(1)}, u32[]{:S(2)}, u32[]{:S(2)}) collective-permute-start(f32[4,232,128]{2,1,0:T(8,128)S(1)} %pad_maximum_fusion.same), channel_id=1, source_target_pairs={{0,32},{32,0},{64,96},{96,64},{128,160},{160,128},{192,224},{224,1... | collective-permute-start | bytes 1425416 | tf_op jit(solution)/shard_map/ppermute | solution.py:396
  66.5 1.5 %collective-permute-done.9.other = f32[4,232,128]{2,1,0:T(8,128)S(1)} collective-permute-done((f32[4,232,128]{2,1,0:T(8,128)S(1)}, f32[4,232,128]{2,1,0:T(8,128)S(1)}, u32[]{:S(2)}, u32[]{:S(2)}) %collective-permute-start.9) | collective-permute-done | bytes 475168 | tf_op jit(solution)/shard_map/ppermute | solution.py:396
  68.0 2.1 %place.1 = (f32[1760,128]{1,0:T(8,128)}, f32[1,1]{1,0:T(1,128)}) custom-call(s32[2]{0:T(128)S(1)} %pad_add_fusion.ids, f32[4,232,128]{2,1,0:T(8,128)S(1)} %pad_maximum_fusion.same, f32[4,232,128]{2,1,0:T(8,128)S(1)} %collective-permute-done.9.other), custom_call_target="tpu_custom_call" | custom-call | tf_op jit(solution)/shard_map/place/pallas_call | solution.py:398
  (7 shorter events, 0.1 us)
Async XLA Ops:
  2.4 11.7 %collective-permute-start = (f32[64,1024]{1,0:T(8,128)S(1)}, f32[64,1024]{1,0:T(8,128)S(1)}, u32[]{:S(2)}, u32[]{:S(2)}) collective-permute-start(f32[64,1024]{1,0:T(8,128)S(1)} %get-tuple-element.18.tail), channel_id=1, source_target_pairs={{0,1},{1,2},{2,3},{3,4},{4,5},{5,6},{6,7},{7,8},{8,9},{9,10},{10,1... | collective-permute-start | bytes 786440 | tf_op jit(solution)/shard_map/ppermute | solution.py:342
  4.6 9.6 %collective-permute-start.1 = (f32[64,1024]{1,0:T(8,128)S(1)}, f32[64,1024]{1,0:T(8,128)S(1)}, u32[]{:S(2)}, u32[]{:S(2)}) collective-permute-start(f32[64,1024]{1,0:T(8,128)S(1)} %get-tuple-element.19.head), channel_id=1, source_target_pairs={{1,0},{2,1},{3,2},{4,3},{5,4},{6,5},{7,6},{8,7},{9,8},{10,9},{11,1... | collective-permute-start | bytes 786440 | tf_op jit(solution)/shard_map/ppermute | solution.py:343
  9.8 4.4 %copy-start = (f32[1,2,55,2048]{3,1,2,0:T(2,128)S(1)}, f32[1,2,55,2048]{3,1,2,0:T(2,128)}, u32[]{:S(2)}) copy-start(f32[1,2,55,2048]{3,1,2,0:T(2,128)} %param.5) | copy-start | bytes 2703364
  9.8 4.4 %copy-start.1 = (f32[55,55]{1,0:T(8,128)S(1)}, f32[55,55]{1,0:T(8,128)}, u32[]{:S(2)}) copy-start(f32[55,55]{1,0:T(8,128)} %root.1) | copy-start | bytes 36304
  21.3 4.3 %collective-permute-start.2 = (f32[904,128]{1,0:T(8,128)S(1)}, f32[904,128]{1,0:T(8,128)S(1)}, u32[]{:S(2)}, u32[]{:S(2)}) collective-permute-start(f32[904,128]{1,0:T(8,128)S(1)} %get-tuple-element.27), channel_id=1, source_target_pairs={{0,32},{32,0},{64,96},{96,64},{128,160},{160,128},{192,224},{224,1... | collective-permute-start | bytes 1388552 | tf_op jit(solution)/shard_map/ppermute | solution.py:386
  25.7 23.2 %collective-permute-start.5 = (f32[224,128]{1,0:T(8,128)S(1)}, f32[224,128]{1,0:T(8,128)S(1)}, u32[]{:S(2)}, u32[]{:S(2)}) collective-permute-start(f32[224,128]{1,0:T(8,128)S(1)} %get-tuple-element.34), channel_id=1, source_target_pairs={{0,192},{32,224},{64,0},{96,32},{128,64},{160,96},{192,128},{224,1... | collective-permute-start | bytes 344072 | tf_op jit(solution)/shard_map/ppermute | solution.py:382
  31.4 17.5 %collective-permute-start.4 = (f32[224,128]{1,0:T(8,128)S(1)}, f32[224,128]{1,0:T(8,128)S(1)}, u32[]{:S(2)}, u32[]{:S(2)}) collective-permute-start(f32[224,128]{1,0:T(8,128)S(1)} %get-tuple-element.35), channel_id=1, source_target_pairs={{0,128},{32,160},{64,192},{96,224},{128,0},{160,32},{192,64},{224,... | collective-permute-start | bytes 344072 | tf_op jit(solution)/shard_map/ppermute | solution.py:382
  32.3 16.6 %collective-permute-start.3 = (f32[224,128]{1,0:T(8,128)S(1)}, f32[224,128]{1,0:T(8,128)S(1)}, u32[]{:S(2)}, u32[]{:S(2)}) collective-permute-start(f32[224,128]{1,0:T(8,128)S(1)} %get-tuple-element.36), channel_id=1, source_target_pairs={{0,64},{32,96},{64,128},{96,160},{128,192},{160,224},{192,0},{224,... | collective-permute-start | bytes 344072 | tf_op jit(solution)/shard_map/ppermute | solution.py:382
  49.0 8.7 %collective-permute-start.7 = (f32[232,128]{1,0:T(8,128)S(1)}, f32[232,128]{1,0:T(8,128)S(1)}, u32[]{:S(2)}, u32[]{:S(2)}) collective-permute-start(f32[232,128]{1,0:T(8,128)S(1)} %get-tuple-element.38), channel_id=1, source_target_pairs={{0,128},{32,160},{64,192},{96,224},{128,0},{160,32},{192,64},{224,... | collective-permute-start | bytes 356360 | tf_op jit(solution)/shard_map/ppermute | solution.py:382
  51.2 10.8 %collective-permute-start.6 = (f32[232,128]{1,0:T(8,128)S(1)}, f32[232,128]{1,0:T(8,128)S(1)}, u32[]{:S(2)}, u32[]{:S(2)}) collective-permute-start(f32[232,128]{1,0:T(8,128)S(1)} %get-tuple-element.38), channel_id=1, source_target_pairs={{0,64},{32,96},{64,128},{96,160},{128,192},{160,224},{192,0},{224,... | collective-permute-start | bytes 356360 | tf_op jit(solution)/shard_map/ppermute | solution.py:382
  52.5 12.3 %collective-permute-start.8 = (f32[232,128]{1,0:T(8,128)S(1)}, f32[232,128]{1,0:T(8,128)S(1)}, u32[]{:S(2)}, u32[]{:S(2)}) collective-permute-start(f32[232,128]{1,0:T(8,128)S(1)} %get-tuple-element.38), channel_id=1, source_target_pairs={{0,192},{32,224},{64,0},{96,32},{128,64},{160,96},{192,128},{224,1... | collective-permute-start | bytes 356360 | tf_op jit(solution)/shard_map/ppermute | solution.py:382
  64.8 3.1 %collective-permute-start.9 = (f32[4,232,128]{2,1,0:T(8,128)S(1)}, f32[4,232,128]{2,1,0:T(8,128)S(1)}, u32[]{:S(2)}, u32[]{:S(2)}) collective-permute-start(f32[4,232,128]{2,1,0:T(8,128)S(1)} %pad_maximum_fusion.same), channel_id=1, source_target_pairs={{0,32},{32,0},{64,96},{96,64},{128,160},{160,128},{192,224},{224,1... | collective-permute-start | bytes 1425416 | tf_op jit(solution)/shard_map/ppermute | solution.py:396

commit v2 on v1

--- a/solution.py
+++ b/solution.py
@@ -235,22 +235,23 @@
             rowed[pl.ds(spot, LEVELS, stride=tiles), :] = smoothed[:, tile * LANES : (tile + 1) * LANES]
     slots = 4
     chunk = rowed.shape[0] // slots
-    spot = pl.ds(slots * chunk, 8)
-    keep[spot, :] = send[spot, :] = jnp.broadcast_to(jnp.sum(total, axis=1, keepdims=True), (8, LANES))
-
+    pitch = chunk + 8
+    spare_rows = jnp.broadcast_to(jnp.sum(total, axis=1, keepdims=True), (8, LANES))
     mine, chip = ids[0], ids[1]
     spare = slots * chunk - LEVELS * tiles
 
     def products(slot, start, first, count):
         rows = rowed[pl.ds(pl.multiple_of(start + first, 8), count), :]
         at = 2 * (start + first)
-        here = pl.ds(slot * chunk + first, count)
+        here = pl.ds(slot * pitch + first, count)
         keep[here, :] = ens[pl.ds(at + mine, count, stride=2), :] * rows
         send[here, :] = ens[pl.ds(at + 1 - mine, count, stride=2), :] * rows
 
     for slot in range(slots):
         target = lax.rem(chip + slot, slots)
         start = target * chunk
+        keep[pl.ds(slot * pitch + chunk, 8), :] = spare_rows
+        send[pl.ds(slot * pitch + chunk, 8), :] = spare_rows
         products(slot, start, 0, chunk - spare)
 
         @pl.when(target < slots - 1)
@@ -260,11 +261,11 @@
         @pl.when(target == slots - 1)
         def _():
             nothing = jnp.zeros((spare, LANES), jnp.float32)
-            keep[pl.ds((slot + 1) * chunk - spare, spare), :] = nothing
-            send[pl.ds((slot + 1) * chunk - spare, spare), :] = nothing
-
-
-def place_kernel(scale, ids, same, other, out, quadratic, lines, sems):
+            keep[pl.ds(slot * pitch + chunk - spare, spare), :] = nothing
+            send[pl.ds(slot * pitch + chunk - spare, spare), :] = nothing
+
+
+def place_kernel(scale, ids, same, other, spread, out, quadratic, lines, sems):
     mine, chip = ids[0], ids[1]
     slots = same.shape[0]
     chunk = lines.shape[0] // slots // 2
@@ -286,8 +287,7 @@
         lines[pl.ds(start + 1 - mine, chunk, stride=2), :] = other[slot, 0:chunk, :]
         main.start()
         pl.when(source < slots - 1)(extra.start)
-    terms = [same[slot, chunk : chunk + 8, :] for slot in range(slots)]
-    quadratic[0, 0] = jnp.max((terms[0] + terms[2]) + (terms[1] + terms[3])) * scale
+    quadratic[0, 0] = jnp.max(jnp.sum(spread[...], axis=0, keepdims=True)) * scale
     for slot in range(slots):
         source, start, (main, extra) = copies(slot)
         main.wait()
@@ -339,8 +339,17 @@
         name="prepare",
     )(place, *in_hbm)
 
-    left = lax.ppermute(tail, "patch", [(i, (i + 1) % patches) for i in range(patches)])
-    right = lax.ppermute(head, "patch", [((i + 1) % patches, i) for i in range(patches)])
+    odd = lax.rem(lax.axis_index("patch"), 2) == 1
+    first = jnp.where(odd, tail, head)
+    second = jnp.where(odd, head, tail)
+    swaps = [[], []]
+    for low in range(patches):
+        high = (low + 1) % patches
+        swaps[low % 2] += [(low, high), (high, low)]
+    first = lax.ppermute(first, "patch", swaps[1])
+    second = lax.ppermute(second, "patch", swaps[0])
+    left = jnp.where(odd, second, first)
+    right = jnp.where(odd, first, second)
 
     parts = jax.ShapeDtypeStruct((224, own), jnp.bfloat16)
     inside = pl.pallas_call(
@@ -359,7 +368,7 @@
 
     wide = own + 2 * HALO
     chunk = 56 * tiles // chips
-    terms = jax.ShapeDtypeStruct((chips * chunk + 8, LANES), jnp.float32)
+    terms = jax.ShapeDtypeStruct((chips * (chunk + 8), LANES), jnp.float32)
     wide_parts = pltpu.VMEM((224, wide + 2 * REACH), jnp.bfloat16)
     keep, send = pl.pallas_call(
         smooth_kernel,
@@ -384,24 +393,25 @@
     twin = [(i, i ^ 1) for i in range(members)]
     order = [2, 1, 3]
     pair_sum = keep + lax.ppermute(send, "mem", twin)
-    pieces = [pair_sum[chunk * slot : chunk * (slot + 1)] for slot in range(chips)]
+    pitch = chunk + 8
+    pieces = [pair_sum[pitch * slot : pitch * (slot + 1)] for slot in range(chips)]
     terms = {by: shift_chips(pieces[by], by) for by in order}
-    spread = jnp.broadcast_to(pair_sum[chips * chunk : chips * chunk + 1][None], (patches, 1, LANES))
+    total = ((terms[3] + terms[1]) + (terms[2] + pieces[0])) / (members - 1.0)
+    mine = total[0:chunk]
+    copies = {by: shift_chips(mine, by) for by in order}
+    spread = jnp.broadcast_to(total[chunk : chunk + 1][None], (patches, 1, LANES))
     spread = lax.all_to_all(spread, "patch", 0, 0)
-    terms, spread = lax.optimization_barrier((terms, spread))
-    total = (pieces[0] + terms[1] + terms[2] + terms[3]) / (members - 1.0)
-    total = jnp.concatenate([total, jnp.broadcast_to(jnp.sum(spread, axis=0), (8, LANES))], axis=0)
-    copies = {by: shift_chips(total, by) for by in order}
-    same = jnp.stack([total, copies[1], copies[2], copies[3]])
+    copies, spread = lax.optimization_barrier((copies, spread))
+    same = jnp.stack([mine, copies[1], copies[2], copies[3]])
     other = lax.ppermute(same, "mem", twin)
-    scale = 1.0 / ((members - 1.0) * field.shape[0] * field.shape[1] * all_cells)
+    scale = 1.0 / (field.shape[0] * field.shape[1] * all_cells)
     rows, quadratic = pl.pallas_call(
         functools.partial(place_kernel, scale),
         out_shape=(
             jax.ShapeDtypeStruct(field_rows.shape, jnp.float32),
             jax.ShapeDtypeStruct((1, 1), jnp.float32),
         ),
-        in_specs=[smem, vmem, vmem],
+        in_specs=[smem, vmem, vmem, vmem],
         out_specs=(hbm, smem),
         scratch_shapes=[
             pltpu.VMEM((chips * chunk * 2, LANES), jnp.float32),
@@ -409,7 +419,7 @@
         ],
         compiler_params=params,
         name="place",
-    )(ids, same, other)
+    )(ids, same, other, spread.reshape(patches, LANES))
     product = rows.reshape(LEVELS, tiles, 2, LANES).transpose(2, 0, 1, 3).reshape(field.shape)
     return (product, quadratic.reshape(()))
 

time: 70.3 us -> 73.1 us (1.040)
  starting transfers between devices: 26.5 us -> 30.1 us
  blocking collectives: 14.3 us -> 12.7 us
  waiting for transfers between devices: 13.5 us -> 14.6 us
    ppermute x6, starting transfers between devices: 14.7 us -> 17.7 us  [shift_chips(): return lax.ppermute(array, 'mem', pairs)]
    ppermute x2, waiting for transfers between devices: 0.61 us -> 3.15 us  [the longest x1 1.88 us: on_device(): second = lax.ppermute(second, 'patch', swaps[0])]
    ppermute x1, starting transfers between devices: 1.65 us -> 3.3 us  [on_device(): other = lax.ppermute(same, 'mem', twin)]
    all_to_all x1, blocking collectives: 14.3 us -> 12.7 us  [on_device(): spread = lax.all_to_all(spread, 'patch', 0, 0)]
    ppermute x6, waiting for transfers between devices: 9.99 us -> 8.54 us  [shift_chips(): return lax.ppermute(array, 'mem', pairs)]
    ppermute x1, starting transfers between devices: 2.81 us -> 1.95 us  [on_device(): pair_sum = keep + lax.ppermute(send, 'mem', twin)]
where the time goes in v2:
time: 73.1 us; the launch traced here: 73 us
  starting transfers between devices  30.1 us (41%)
  waiting for transfers between devices  14.6 us (20%)
  Pallas kernels  14.3 us (20%)
  blocking collectives  12.7 us (17%)
  between operations  0.9 us (1%)
    ppermute x6, starting transfers between devices, shift_chips(): return lax.ppermute(array, 'mem', pairs)  17.7 us
    all_to_all x1, blocking collectives, on_device(): spread = lax.all_to_all(spread, 'patch', 0, 0)  12.7 us
    ppermute x6, waiting for transfers between devices, shift_chips(): return lax.ppermute(array, 'mem', pairs)  8.54 us
    ppermute x1, starting transfers between devices, on_device(): first = lax.ppermute(first, 'patch', swaps[1])  7.2 us
    pallas_call x1, Pallas kernels, on_device(): pl.pallas_call(smooth_kernel, out_shape=(terms, terms), in_specs=[smem] +...  6.85 us
    pallas_call x1, Pallas kernels, on_device(): pl.pallas_call(interior_kernel, out_shape=(jax.ShapeDtypeStruct((own // B...  3.62 us
    ppermute x1, starting transfers between devices, on_device(): other = lax.ppermute(same, 'mem', twin)  3.3 us
    pallas_call x1, Pallas kernels, on_device(): pl.pallas_call(functools.partial(place_kernel, scale), out_shape=(jax.Sha...  2.05 us
  transfers between devices with their start and end apart: 10, of which 6 were waited for; matrix products, arithmetic and copies ran while one was open for 0% of the time, Pallas kernels for 5%

profile of v2, /device:TPU:1, one launch (start us, length us, event | category | flops | bytes accessed | tf_op | source)
XLA Modules:
  0.0 73.0 jit_solution(6713386268546753475)
XLA Ops:
  0.6 1.8 %prepare.1 = (f32[64,1024]{1,0:T(8,128)S(1)}, f32[64,1024]{1,0:T(8,128)S(1)}) custom-call(s32[1]{0:T(128)} %bitcast.2.place, f32[1760,128]{1,0:T(8,128)} %bitcast.28, f32[1760,128]{1,0:T(8,128)} %bitcast.31, f32[1,2048]{1,0:T(1,128)} %bitcast.35, s32[7,2048]{1,0:T(8,128)} %neigh.1), custom_call_target="tpu_custom_call" | custom-call | tf_op jit(solution)/shard_map/prepare/pallas_call | solution.py:326
  2.5 7.2 %collective-permute-start.1 = (f32[64,1024]{1,0:T(8,128)S(1)}, f32[64,1024]{1,0:T(8,128)S(1)}, u32[]{:S(2)}, u32[]{:S(2)}) collective-permute-start(f32[64,1024]{1,0:T(8,128)S(1)} %get-tuple-element.36), channel_id=1, source_target_pairs={{1,2},{2,1},{3,4},{4,3},{5,6},{6,5},{7,8},{8,7},{9,10},{10,9},{11,... | collective-permute-start | bytes 786440 | tf_op jit(solution)/shard_map/ppermute | solution.py:349
  9.7 0.0 collective-permute-start
  9.7 0.1 pad_add_fusion.ids
  9.8 0.0 copy-start
  9.8 0.0 copy-start.1
  9.8 3.6 %interior.1 = (bf16[8,512,256]{2,1,0:T(8,128)(2,1)S(1)}, f32[64,2048]{1,0:T(8,128)S(1)}, bf16[224,2048]{1,0:T(8,128)(2,1)S(1)}, bf16[224,2048]{1,0:T(8,128)(2,1)...) custom-call(f32[64,1024]{1,0:T(8,128)S(1)} %get-tuple-element.18.head, ...), custom_call_target="tpu_custom_call" | custom-call | flops 4000000000 | bytes 4000000 | tf_op jit(solution)/shard_map/interior/pallas_call | solution.py:355
  13.4 1.3 %collective-permute-done.1 = f32[64,1024]{1,0:T(8,128)S(1)} collective-permute-done((f32[64,1024]{1,0:T(8,128)S(1)}, f32[64,1024]{1,0:T(8,128)S(1)}, u32[]{:S(2)}, u32[]{:S(2)}) %collective-permute-start.1) | collective-permute-done | bytes 262176 | tf_op jit(solution)/shard_map/ppermute | solution.py:349
  14.7 1.9 %collective-permute-done = f32[64,1024]{1,0:T(8,128)S(1)} collective-permute-done((f32[64,1024]{1,0:T(8,128)S(1)}, f32[64,1024]{1,0:T(8,128)S(1)}, u32[]{:S(2)}, u32[]{:S(2)}) %collective-permute-start) | collective-permute-done | bytes 262176 | tf_op jit(solution)/shard_map/ppermute | solution.py:350
  16.6 0.0 copy-done
  16.6 0.0 copy-done.1
  16.6 6.9 %smooth.1 = (f32[928,128]{1,0:T(8,128)S(1)}, f32[928,128]{1,0:T(8,128)S(1)}) custom-call(s32[2]{0:T(128)S(1)} %pad_add_fusion.ids, f32[64,1024]{1,0:T(8,128)S(1)} %get-tuple-element.35.left, f32[64,1024]{1,0:T(8,128)S(1)} %get-tuple-element.18.head, f32[64,1024]{1,0:T(8,128)S(1)} %get-tuple-element.19.tail, f32[64,1024]{1,0:T(8,128)S(1)} %get-tuple-element.34.right, ...), custom_call_target="tpu_custom_call" | custom-call | tf_op jit(solution)/shard_map/smooth/pallas_call | solution.py:373
  23.5 1.9 %collective-permute-start.2 = (f32[928,128]{1,0:T(8,128)S(1)}, f32[928,128]{1,0:T(8,128)S(1)}, u32[]{:S(2)}, u32[]{:S(2)}) collective-permute-start(f32[928,128]{1,0:T(8,128)S(1)} %get-tuple-element.27), channel_id=1, source_target_pairs={{0,32},{32,0},{64,96},{96,64},{128,160},{160,128},{192,224},{224,1... | collective-permute-start | bytes 1425416 | tf_op jit(solution)/shard_map/ppermute | solution.py:395
  25.4 1.5 %collective-permute-done.2 = f32[928,128]{1,0:T(8,128)S(1)} collective-permute-done((f32[928,128]{1,0:T(8,128)S(1)}, f32[928,128]{1,0:T(8,128)S(1)}, u32[]{:S(2)}, u32[]{:S(2)}) %collective-permute-start.2) | collective-permute-done | bytes 475168 | tf_op jit(solution)/shard_map/ppermute | solution.py:395
  26.9 0.1 add.13
  27.0 3.2 %collective-permute-start.4 = (f32[232,128]{1,0:T(8,128)S(1)}, f32[232,128]{1,0:T(8,128)S(1)}, u32[]{:S(2)}, u32[]{:S(2)}) collective-permute-start(f32[232,128]{1,0:T(8,128)S(1)} %get-tuple-element.38), channel_id=1, source_target_pairs={{0,64},{32,96},{64,128},{96,160},{128,192},{160,224},{192,0},{224,... | collective-permute-start | bytes 356360 | tf_op jit(solution)/shard_map/ppermute | solution.py:391
  30.3 4.2 %collective-permute-start.5 = (f32[232,128]{1,0:T(8,128)S(1)}, f32[232,128]{1,0:T(8,128)S(1)}, u32[]{:S(2)}, u32[]{:S(2)}) collective-permute-start(f32[232,128]{1,0:T(8,128)S(1)} %get-tuple-element.39), channel_id=1, source_target_pairs={{0,128},{32,160},{64,192},{96,224},{128,0},{160,32},{192,64},{224,... | collective-permute-start | bytes 356360 | tf_op jit(solution)/shard_map/ppermute | solution.py:391
  34.5 2.4 %collective-permute-start.3 = (f32[232,128]{1,0:T(8,128)S(1)}, f32[232,128]{1,0:T(8,128)S(1)}, u32[]{:S(2)}, u32[]{:S(2)}) collective-permute-start(f32[232,128]{1,0:T(8,128)S(1)} %get-tuple-element.40), channel_id=1, source_target_pairs={{0,192},{32,224},{64,0},{96,32},{128,64},{160,96},{192,128},{224,1... | collective-permute-start | bytes 356360 | tf_op jit(solution)/shard_map/ppermute | solution.py:391
  36.9 0.0 collective-permute-done.4
  36.9 4.8 %collective-permute-done.5 = f32[232,128]{1,0:T(8,128)S(1)} collective-permute-done((f32[232,128]{1,0:T(8,128)S(1)}, f32[232,128]{1,0:T(8,128)S(1)}, u32[]{:S(2)}, u32[]{:S(2)}) %collective-permute-start.5) | collective-permute-done | bytes 118816 | tf_op jit(solution)/shard_map/ppermute | solution.py:391
  41.6 3.7 %collective-permute-done.3 = f32[232,128]{1,0:T(8,128)S(1)} collective-permute-done((f32[232,128]{1,0:T(8,128)S(1)}, f32[232,128]{1,0:T(8,128)S(1)}, u32[]{:S(2)}, u32[]{:S(2)}) %collective-permute-start.3) | collective-permute-done | bytes 118816 | tf_op jit(solution)/shard_map/ppermute | solution.py:391
  45.4 4.3 %collective-permute-start.7 = (f32[224,128]{1,0:T(8,128)S(1)}, f32[224,128]{1,0:T(8,128)S(1)}, u32[]{:S(2)}, u32[]{:S(2)}) collective-permute-start(f32[224,128]{1,0:T(8,128)S(1)} %get-tuple-element.42), channel_id=1, source_target_pairs={{0,128},{32,160},{64,192},{96,224},{128,0},{160,32},{192,64},{224,... | collective-permute-start | bytes 344072 | tf_op jit(solution)/shard_map/ppermute | solution.py:391
  49.7 1.1 %collective-permute-start.6 = (f32[224,128]{1,0:T(8,128)S(1)}, f32[224,128]{1,0:T(8,128)S(1)}, u32[]{:S(2)}, u32[]{:S(2)}) collective-permute-start(f32[224,128]{1,0:T(8,128)S(1)} %get-tuple-element.42), channel_id=1, source_target_pairs={{0,64},{32,96},{64,128},{96,160},{128,192},{160,224},{192,0},{224,... | collective-permute-start | bytes 344072 | tf_op jit(solution)/shard_map/ppermute | solution.py:391
  50.8 2.5 %collective-permute-start.8 = (f32[224,128]{1,0:T(8,128)S(1)}, f32[224,128]{1,0:T(8,128)S(1)}, u32[]{:S(2)}, u32[]{:S(2)}) collective-permute-start(f32[224,128]{1,0:T(8,128)S(1)} %get-tuple-element.42), channel_id=1, source_target_pairs={{0,192},{32,224},{64,0},{96,32},{128,64},{160,96},{192,128},{224,1... | collective-permute-start | bytes 344072 | tf_op jit(solution)/shard_map/ppermute | solution.py:391
  53.3 12.7 %all_to_all.5 = f32[32,1,128]{2,1,0:T(1,128)S(1)} all-to-all(f32[32,1,128]{2,1,0:T(1,128)S(1)} %broadcast_in_dim.9), channel_id=1, replica_groups=mesh['mem'=8,'patch'=32] {'patch'}, dimensions={0} | all-to-all | bytes 32768 | tf_op jit(solution)/shard_map/all_to_all | solution.py:403
  66.0 0.0 collective-permute-done.7
  66.0 0.0 collective-permute-done.6
  66.0 0.0 collective-permute-done.8
  66.0 3.3 %collective-permute-start.9 = (f32[4,224,128]{2,1,0:T(8,128)S(1)}, f32[4,224,128]{2,1,0:T(8,128)S(1)}, u32[]{:S(2)}, u32[]{:S(2)}) collective-permute-start(f32[4,224,128]{2,1,0:T(8,128)S(1)} %pad_maximum_fusion.same), channel_id=1, source_target_pairs={{0,32},{32,0},{64,96},{96,64},{128,160},{160,128},{192,224},{224,1... | collective-permute-start | bytes 1376264 | tf_op jit(solution)/shard_map/ppermute | solution.py:406
  69.3 1.4 %collective-permute-done.9.other = f32[4,224,128]{2,1,0:T(8,128)S(1)} collective-permute-done((f32[4,224,128]{2,1,0:T(8,128)S(1)}, f32[4,224,128]{2,1,0:T(8,128)S(1)}, u32[]{:S(2)}, u32[]{:S(2)}) %collective-permute-start.9) | collective-permute-done | bytes 458784 | tf_op jit(solution)/shard_map/ppermute | solution.py:406
  70.8 2.1 %place.1 = (f32[1760,128]{1,0:T(8,128)}, f32[1,1]{1,0:T(1,128)}) custom-call(s32[2]{0:T(128)S(1)} %pad_add_fusion.ids, f32[4,224,128]{2,1,0:T(8,128)S(1)} %pad_maximum_fusion.same, f32[4,224,128]{2,1,0:T(8,128)S(1)} %collective-permute-done.9.other, f32[32,128]{1,0:T(8,128)S(1)} %bitcast.30), custom_call_target="tpu_custom_call" | custom-call | tf_op jit(solution)/shard_map/place/pallas_call | solution.py:408
  (8 shorter events, 0.2 us)
Async XLA Ops:
  2.5 12.2 %collective-permute-start.1 = (f32[64,1024]{1,0:T(8,128)S(1)}, f32[64,1024]{1,0:T(8,128)S(1)}, u32[]{:S(2)}, u32[]{:S(2)}) collective-permute-start(f32[64,1024]{1,0:T(8,128)S(1)} %get-tuple-element.36), channel_id=1, source_target_pairs={{1,2},{2,1},{3,4},{4,3},{5,6},{6,5},{7,8},{8,7},{9,10},{10,9},{11,... | collective-permute-start | bytes 786440 | tf_op jit(solution)/shard_map/ppermute | solution.py:349
  9.7 6.9 %collective-permute-start = (f32[64,1024]{1,0:T(8,128)S(1)}, f32[64,1024]{1,0:T(8,128)S(1)}, u32[]{:S(2)}, u32[]{:S(2)}) collective-permute-start(f32[64,1024]{1,0:T(8,128)S(1)} %get-tuple-element.37), channel_id=1, source_target_pairs={{0,1},{1,0},{2,3},{3,2},{4,5},{5,4},{6,7},{7,6},{8,9},{9,8},{10,11... | collective-permute-start | bytes 786440 | tf_op jit(solution)/shard_map/ppermute | solution.py:350
  9.8 6.8 %copy-start = (f32[1,2,55,2048]{3,1,2,0:T(2,128)S(1)}, f32[1,2,55,2048]{3,1,2,0:T(2,128)}, u32[]{:S(2)}) copy-start(f32[1,2,55,2048]{3,1,2,0:T(2,128)} %param.5) | copy-start | bytes 2703364
  9.8 6.8 %copy-start.1 = (f32[55,55]{1,0:T(8,128)S(1)}, f32[55,55]{1,0:T(8,128)}, u32[]{:S(2)}) copy-start(f32[55,55]{1,0:T(8,128)} %root.1) | copy-start | bytes 36304
  23.5 3.4 %collective-permute-start.2 = (f32[928,128]{1,0:T(8,128)S(1)}, f32[928,128]{1,0:T(8,128)S(1)}, u32[]{:S(2)}, u32[]{:S(2)}) collective-permute-start(f32[928,128]{1,0:T(8,128)S(1)} %get-tuple-element.27), channel_id=1, source_target_pairs={{0,32},{32,0},{64,96},{96,64},{128,160},{160,128},{192,224},{224,1... | collective-permute-start | bytes 1425416 | tf_op jit(solution)/shard_map/ppermute | solution.py:395
  27.0 9.8 %collective-permute-start.4 = (f32[232,128]{1,0:T(8,128)S(1)}, f32[232,128]{1,0:T(8,128)S(1)}, u32[]{:S(2)}, u32[]{:S(2)}) collective-permute-start(f32[232,128]{1,0:T(8,128)S(1)} %get-tuple-element.38), channel_id=1, source_target_pairs={{0,64},{32,96},{64,128},{96,160},{128,192},{160,224},{192,0},{224,... | collective-permute-start | bytes 356360 | tf_op jit(solution)/shard_map/ppermute | solution.py:391
  30.3 11.4 %collective-permute-start.5 = (f32[232,128]{1,0:T(8,128)S(1)}, f32[232,128]{1,0:T(8,128)S(1)}, u32[]{:S(2)}, u32[]{:S(2)}) collective-permute-start(f32[232,128]{1,0:T(8,128)S(1)} %get-tuple-element.39), channel_id=1, source_target_pairs={{0,128},{32,160},{64,192},{96,224},{128,0},{160,32},{192,64},{224,... | collective-permute-start | bytes 356360 | tf_op jit(solution)/shard_map/ppermute | solution.py:391
  34.5 10.9 %collective-permute-start.3 = (f32[232,128]{1,0:T(8,128)S(1)}, f32[232,128]{1,0:T(8,128)S(1)}, u32[]{:S(2)}, u32[]{:S(2)}) collective-permute-start(f32[232,128]{1,0:T(8,128)S(1)} %get-tuple-element.40), channel_id=1, source_target_pairs={{0,192},{32,224},{64,0},{96,32},{128,64},{160,96},{192,128},{224,1... | collective-permute-start | bytes 356360 | tf_op jit(solution)/shard_map/ppermute | solution.py:391
  45.4 20.5 %collective-permute-start.7 = (f32[224,128]{1,0:T(8,128)S(1)}, f32[224,128]{1,0:T(8,128)S(1)}, u32[]{:S(2)}, u32[]{:S(2)}) collective-permute-start(f32[224,128]{1,0:T(8,128)S(1)} %get-tuple-element.42), channel_id=1, source_target_pairs={{0,128},{32,160},{64,192},{96,224},{128,0},{160,32},{192,64},{224,... | collective-permute-start | bytes 344072 | tf_op jit(solution)/shard_map/ppermute | solution.py:391
  49.7 16.3 %collective-permute-start.6 = (f32[224,128]{1,0:T(8,128)S(1)}, f32[224,128]{1,0:T(8,128)S(1)}, u32[]{:S(2)}, u32[]{:S(2)}) collective-permute-start(f32[224,128]{1,0:T(8,128)S(1)} %get-tuple-element.42), channel_id=1, source_target_pairs={{0,64},{32,96},{64,128},{96,160},{128,192},{160,224},{192,0},{224,... | collective-permute-start | bytes 344072 | tf_op jit(solution)/shard_map/ppermute | solution.py:391
  50.8 15.1 %collective-permute-start.8 = (f32[224,128]{1,0:T(8,128)S(1)}, f32[224,128]{1,0:T(8,128)S(1)}, u32[]{:S(2)}, u32[]{:S(2)}) collective-permute-start(f32[224,128]{1,0:T(8,128)S(1)} %get-tuple-element.42), channel_id=1, source_target_pairs={{0,192},{32,224},{64,0},{96,32},{128,64},{160,96},{192,128},{224,1... | collective-permute-start | bytes 344072 | tf_op jit(solution)/shard_map/ppermute | solution.py:391
  66.0 4.7 %collective-permute-start.9 = (f32[4,224,128]{2,1,0:T(8,128)S(1)}, f32[4,224,128]{2,1,0:T(8,128)S(1)}, u32[]{:S(2)}, u32[]{:S(2)}) collective-permute-start(f32[4,224,128]{2,1,0:T(8,128)S(1)} %pad_maximum_fusion.same), channel_id=1, source_target_pairs={{0,32},{32,0},{64,96},{96,64},{128,160},{160,128},{192,224},{224,1... | collective-permute-start | bytes 1376264 | tf_op jit(solution)/shard_map/ppermute | solution.py:406

commit v3 on v1

--- a/solution.py
+++ b/solution.py
@@ -13,6 +13,7 @@
 HALO = STEPS * REACH
 LEVELS = 55
 LANES = 128
+EARLY, LATE = (0, 2), (1, 3)
 
 
 def prepare_kernel(
@@ -93,20 +94,23 @@
     buf[112:224, at : at + width] = parts[1]
 
 
-def sweep(state, now, later, margin, places):
+def sweep(state, now, later, bases, places):
+    first, origin = bases
+
     def matmul(at, width, matrix):
-        window = now[:, at + margin - REACH : at + margin + width + REACH]
-        return jnp.dot(window, matrix, preferred_element_type=jnp.float32)
+        low = at - origin - REACH
+        return jnp.dot(now[:, low : low + width + 2 * REACH], matrix, preferred_element_type=jnp.float32)
 
     def finish(at, width, kept, total):
-        coeff = state[56:57, at : at + width]
-        value = state[0:56, at : at + width]
+        here = slice(at - first, at - first + width)
+        coeff = state[56:57, here]
+        value = state[0:56, here]
         change = coeff * (total[0:56] + total[112:168]) + (total[56:112] + total[168:224])
         value = value * (1.0 - change[55:56]) + change
         if kept:
-            state[0:56, at : at + width] = value
+            state[0:56, here] = value
         if later is not None:
-            store_parts(later, at + margin, split(value, coeff))
+            store_parts(later, at - origin, split(value, coeff))
 
     waiting = None
     for at, width, matrix, kept in places:
@@ -146,69 +150,101 @@
             low, high = whole[0] - 1, whole[-1] + 1
             places.append((low * BLOCK + REACH, REACH, lambda: adj[low, REACH:, REACH:], False))
             places.append((high * BLOCK, REACH, lambda: adj[high, : BLOCK + REACH, :REACH], False))
-        sweep(state, bufs[(step - 1) % 4], bufs[step % 4], 0, places)
-
-
-def smooth_kernel(
-    ids, left, head, tail, right, root, ens, inner, done, own0, own1, own2, own3,
+        sweep(state, bufs[(step - 1) % 4], bufs[step % 4], (0, 0), places)
+
+
+def load_halo(part, at, state, outer, buf, bases):
+    for index in range(HALO // BLOCK):
+        value = part[:, index * BLOCK : (index + 1) * BLOCK]
+        coeff = 0.5 * value[63:64]
+        here = at + index * BLOCK
+        spot = slice(here - bases[0], here - bases[0] + BLOCK)
+        state[0:56, spot] = value[0:56]
+        state[56:64, spot] = jnp.broadcast_to(coeff, (8, BLOCK))
+        store_parts(buf, here - bases[1], split(value[0:56], coeff))
+
+        def store(down, across, piece):
+            outer[index, down * LANES : (down + 1) * LANES, across * LANES : (across + 1) * LANES] = piece
+
+        build_block(value[56:63], store)
+
+
+def carry_over(owns, bufs, side, bases):
+    own = owns[0].shape[1]
+    for step in range(STEPS - 1):
+        low = interior_blocks(step, own // BLOCK)[0] * BLOCK
+        if step % 2 == 0:
+            high = low + BLOCK + REACH
+        else:
+            high = low + REACH
+        if side:
+            low, high = own - high, own - low
+        at = HALO - bases[1]
+        bufs[step % 4][:, at + low : at + high] = owns[step % 4][:, low:high]
+
+
+def left_kernel(left, inner, done, own0, own1, own2, own3, state, seam, outer, buf0, buf1, buf2, buf3):
+    own = done.shape[1]
+    bases = (0, -REACH)
+    bufs = (buf0, buf1, buf2, buf3)
+    fringe = HALO // BLOCK
+    middle = fringe + own // BLOCK // 2
+    state[:, HALO:] = done[:, 0 : own // 2]
+    edge = jnp.zeros((224, REACH), jnp.bfloat16)
+    buf0[:, 0:REACH] = edge
+    buf2[:, 2 * REACH : 3 * REACH] = edge
+    carry_over((own0, own1, own2, own3), bufs, 0, bases)
+    load_halo(left, 0, state, outer, buf0, bases)
+    for step in range(1, STEPS + 1):
+        inside = interior_blocks(step, own // BLOCK)
+        stop = fringe + inside[0] if len(inside) else middle - (step == STEPS)
+        places = [
+            (
+                block * BLOCK, BLOCK,
+                functools.partial(lambda b: outer[b] if b < fringe else inner[b - fringe], block), True,
+            )
+            for block in range(step // 2, stop)
+        ]
+        sweep(state, bufs[(step - 1) % 4], bufs[step % 4] if step < STEPS else None, bases, places)
+    low = (middle - 1) * BLOCK - REACH - bases[1]
+    seam[...] = bufs[(STEPS - 1) % 4][:, low : low + BLOCK + REACH]
+
+
+def right_kernel(
+    ids, right, head, tail, root, ens, west, seam, inner, done, own0, own1, own2, own3,
     keep, send, state, outer, buf0, buf1, buf2, buf3, square, rowed,
 ):
-    wide = state.shape[1]
-    own = wide - 2 * HALO
+    own = done.shape[1]
+    wide = own + 2 * HALO
     tiles = own // LANES
     blocks = wide // BLOCK
     fringe = HALO // BLOCK
+    middle = blocks // 2
+    bases = ((middle - 1) * BLOCK, (middle - 2) * BLOCK)
     bufs = (buf0, buf1, buf2, buf3)
-
-    state[:, HALO : HALO + own] = done[...]
+    state[:, 0:BLOCK] = west[:, (middle - 1) * BLOCK :]
+    state[:, BLOCK : BLOCK + own // 2] = done[:, own // 2 :]
     edge = jnp.zeros((224, REACH), jnp.bfloat16)
-    buf0[:, 0:REACH] = edge
-    buf0[:, REACH + wide : REACH + wide + REACH] = edge
-    buf2[:, 2 * REACH : 3 * REACH] = edge
-    buf2[:, wide - REACH : wide] = edge
-
-    def carry_over(step, first, last):
-        source, target = (own0, own1, own2, own3)[step % 4], bufs[step % 4]
-        for low, high in ((first, last), (own - last, own - first)):
-            target[:, REACH + HALO + low : REACH + HALO + high] = source[:, low:high]
-
-    for step in range(STEPS - 1):
+    buf0[:, wide - bases[1] :] = edge
+    buf2[:, wide - 2 * REACH - bases[1] : wide - REACH - bases[1]] = edge
+    carry_over((own0, own1, own2, own3), bufs, 1, bases)
+    load_halo(right, HALO + own, state, outer, buf0, bases)
+    for step in range(1, STEPS + 1):
         inside = interior_blocks(step, own // BLOCK)
-        if step % 2 == 0:
-            carry_over(step, inside[0] * BLOCK, min(inside[0] * BLOCK + BLOCK + REACH, own // 2))
-        else:
-            carry_over(step, inside[0] * BLOCK, inside[0] * BLOCK + REACH)
-
-    for which, part in ((0, left), (1, right)):
-        for index in range(fringe):
-            block = which * fringe + index
-            value = part[:, index * BLOCK : (index + 1) * BLOCK]
-            coeff = 0.5 * value[63:64]
-            here = which * (HALO + own) + index * BLOCK
-            state[0:56, here : here + BLOCK] = value[0:56]
-            state[56:64, here : here + BLOCK] = jnp.broadcast_to(coeff, (8, BLOCK))
-            store_parts(buf0, here + REACH, split(value[0:56], coeff))
-
-            def store(down, across, piece):
-                outer[block, down * LANES : (down + 1) * LANES, across * LANES : (across + 1) * LANES] = piece
-
-            build_block(value[56:63], store)
-
-    def adjacency(block):
-        if block < fringe:
-            return outer[block]
-        if block < blocks - fringe:
-            return inner[block - fringe]
-        return outer[block - (blocks - 2 * fringe)]
-
-    for step in range(1, STEPS + 1):
-        inside = [fringe + block for block in interior_blocks(step, own // BLOCK)]
+        start = fringe + inside[-1] + 1 if len(inside) else middle - (step == STEPS)
         places = [
-            (block * BLOCK, BLOCK, functools.partial(adjacency, block), True)
-            for block in range(step // 2, blocks - step // 2)
-            if block not in inside
+            (
+                block * BLOCK, BLOCK,
+                functools.partial(
+                    lambda b: inner[b - fringe] if b < blocks - fringe else outer[b - (blocks - fringe)], block
+                ), True,
+            )
+            for block in range(start, blocks - step // 2)
         ]
-        sweep(state, bufs[(step - 1) % 4], bufs[step % 4] if step < STEPS else None, REACH, places)
+        if step == STEPS:
+            low = (middle - 1) * BLOCK - REACH - bases[1]
+            bufs[(step - 1) % 4][:, low : low + BLOCK + REACH] = seam[...]
+        sweep(state, bufs[(step - 1) % 4], bufs[step % 4] if step < STEPS else None, bases, places)
 
     square[...] = jnp.zeros(square.shape, jnp.float32)
     square[0:LEVELS, 0:LEVELS] = root[...]
@@ -221,7 +257,8 @@
     stacked = jnp.concatenate([matrix_high, matrix_low], axis=0)
     total = jnp.zeros((1, BLOCK), jnp.float32)
     for block in range(own // BLOCK):
-        value = state[:, HALO + block * BLOCK : HALO + (block + 1) * BLOCK]
+        at = (fringe + block) * BLOCK
+        value = west[:, at : at + BLOCK] if at < bases[0] else state[:, at - bases[0] : at - bases[0] + BLOCK]
         high = value.astype(jnp.bfloat16)
         low = (value - high.astype(jnp.float32)).astype(jnp.bfloat16)
         first = jnp.dot(stacked, high, preferred_element_type=jnp.float32)
@@ -264,34 +301,49 @@
             send[pl.ds((slot + 1) * chunk - spare, spare), :] = nothing
 
 
-def place_kernel(scale, ids, same, other, out, quadratic, lines, sems):
+def place_pieces(ids, slots, same, other, out, lines, sems):
     mine, chip = ids[0], ids[1]
-    slots = same.shape[0]
-    chunk = lines.shape[0] // slots // 2
-    short = 2 * chunk - (lines.shape[0] - out.shape[0])
-
-    def copies(slot):
-        source = lax.rem(chip + slots - slot, slots)
-        start = pl.multiple_of(source * 2 * chunk, 8)
-        rows = pl.ds(start, short)
-        rest = pl.ds(pl.multiple_of(start + short, 8), 2 * chunk - short)
-        return source, start, (
-            pltpu.make_async_copy(lines.at[rows], out.at[rows], sems.at[0, slot]),
-            pltpu.make_async_copy(lines.at[rest], out.at[rest], sems.at[1, slot]),
+    chunk = lines.shape[0] // len(slots) // 2
+    short = 2 * chunk - (4 * 2 * chunk - out.shape[0])
+    waits = []
+    for index, slot in enumerate(slots):
+        source = lax.rem(chip + 4 - slot, 4)
+        start = index * 2 * chunk
+        lines[pl.ds(start + mine, chunk, stride=2), :] = same[index, 0:chunk, :]
+        lines[pl.ds(start + 1 - mine, chunk, stride=2), :] = other[index, 0:chunk, :]
+        target = pl.multiple_of(source * 2 * chunk, 8)
+        main = pltpu.make_async_copy(
+            lines.at[pl.ds(start, short)], out.at[pl.ds(target, short)], sems.at[0, index]
         )
-
-    for slot in range(slots):
-        source, start, (main, extra) = copies(slot)
-        lines[pl.ds(start + mine, chunk, stride=2), :] = same[slot, 0:chunk, :]
-        lines[pl.ds(start + 1 - mine, chunk, stride=2), :] = other[slot, 0:chunk, :]
+        extra = pltpu.make_async_copy(
+            lines.at[pl.ds(start + short, 2 * chunk - short)],
+            out.at[pl.ds(pl.multiple_of(target + short, 8), 2 * chunk - short)],
+            sems.at[1, index],
+        )
         main.start()
-        pl.when(source < slots - 1)(extra.start)
-    terms = [same[slot, chunk : chunk + 8, :] for slot in range(slots)]
-    quadratic[0, 0] = jnp.max((terms[0] + terms[2]) + (terms[1] + terms[3])) * scale
-    for slot in range(slots):
-        source, start, (main, extra) = copies(slot)
+        pl.when(source < 3)(extra.start)
+        waits.append((source, main, extra))
+    return waits
+
+
+def wait_pieces(waits):
+    for source, main, extra in waits:
         main.wait()
-        pl.when(source < slots - 1)(extra.wait)
+        pl.when(source < 3)(extra.wait)
+
+
+def early_kernel(ids, same, other, out, lines, sems):
+    wait_pieces(place_pieces(ids, EARLY, same, other, out, lines, sems))
+
+
+def late_kernel(scale, ids, begun, early, same, other, out, quadratic, lines, sems):
+    waits = place_pieces(ids, LATE, same, other, out, lines, sems)
+    chunk = lines.shape[0] // len(LATE) // 2
+    near, far = [
+        pieces[0, chunk : chunk + 8, :] + pieces[1, chunk : chunk + 8, :] for pieces in (early, same)
+    ]
+    quadratic[0, 0] = jnp.max(near + far) * scale
+    wait_pieces(waits)
 
 
 def interleave(array):
@@ -353,29 +405,44 @@
         in_specs=[vmem] * 2,
         out_specs=(vmem,) * 6,
         compiler_params=params,
-        cost_estimate=pl.CostEstimate(flops=4_000_000_000, bytes_accessed=4_000_000, transcendentals=0),
+        cost_estimate=pl.CostEstimate(flops=0, bytes_accessed=7_000_000, transcendentals=0),
         name="interior",
     )(head, tail)
 
-    wide = own + 2 * HALO
     chunk = 56 * tiles // chips
+    west, seam = pl.pallas_call(
+        left_kernel,
+        out_shape=(
+            jax.ShapeDtypeStruct((64, HALO + half), jnp.float32),
+            jax.ShapeDtypeStruct((224, BLOCK + REACH), jnp.bfloat16),
+        ),
+        in_specs=[vmem] * 7,
+        out_specs=(vmem,) * 2,
+        scratch_shapes=[pltpu.VMEM((HALO // BLOCK, 2 * BLOCK, BLOCK), jnp.bfloat16)]
+        + [pltpu.VMEM((224, HALO + half + 2 * REACH), jnp.bfloat16)] * 4,
+        compiler_params=params,
+        cost_estimate=pl.CostEstimate(flops=0, bytes_accessed=7_000_000, transcendentals=0),
+        name="left",
+    )(left, *inside)
     terms = jax.ShapeDtypeStruct((chips * chunk + 8, LANES), jnp.float32)
-    wide_parts = pltpu.VMEM((224, wide + 2 * REACH), jnp.bfloat16)
     keep, send = pl.pallas_call(
-        smooth_kernel,
+        right_kernel,
         out_shape=(terms, terms),
-        in_specs=[smem] + [vmem] * 12,
+        in_specs=[smem] + [vmem] * 13,
         out_specs=(vmem, vmem),
         scratch_shapes=[
-            pltpu.VMEM((64, wide), jnp.float32),
-            pltpu.VMEM((2 * HALO // BLOCK, 2 * BLOCK, BLOCK), jnp.bfloat16),
-            wide_parts, wide_parts, wide_parts, wide_parts,
+            pltpu.VMEM((64, BLOCK + half + HALO), jnp.float32),
+            pltpu.VMEM((HALO // BLOCK, 2 * BLOCK, BLOCK), jnp.bfloat16),
+        ]
+        + [pltpu.VMEM((224, 2 * BLOCK + half + HALO + REACH), jnp.bfloat16)] * 4
+        + [
             pltpu.VMEM((64, 64), jnp.float32),
             pltpu.VMEM((56 * tiles, LANES), jnp.float32),
         ],
         compiler_params=params,
-        name="smooth",
-    )(ids, left, head, tail, right, vertical_root, ens_rows, *inside)
+        cost_estimate=pl.CostEstimate(flops=0, bytes_accessed=7_000_000, transcendentals=0),
+        name="right",
+    )(ids, right, head, tail, vertical_root, ens_rows, west, seam, *inside)
 
     def shift_chips(array, by):
         pairs = [(2 * z + c, 2 * ((z + by) % chips) + c) for z in range(chips) for c in range(2)]
@@ -392,24 +459,37 @@
     total = (pieces[0] + terms[1] + terms[2] + terms[3]) / (members - 1.0)
     total = jnp.concatenate([total, jnp.broadcast_to(jnp.sum(spread, axis=0), (8, LANES))], axis=0)
     copies = {by: shift_chips(total, by) for by in order}
-    same = jnp.stack([total, copies[1], copies[2], copies[3]])
-    other = lax.ppermute(same, "mem", twin)
+    sources = {0: total, **copies}
     scale = 1.0 / ((members - 1.0) * field.shape[0] * field.shape[1] * all_cells)
+    scratch = [
+        pltpu.VMEM((2 * chunk * 2, LANES), jnp.float32),
+        pltpu.SemaphoreType.DMA((2, 2)),
+    ]
+    early = jnp.stack([sources[by] for by in EARLY])
+    rows = pl.pallas_call(
+        early_kernel,
+        out_shape=jax.ShapeDtypeStruct(field_rows.shape, jnp.float32),
+        in_specs=[smem, vmem, vmem],
+        out_specs=hbm,
+        scratch_shapes=scratch,
+        compiler_params=params,
+        cost_estimate=pl.CostEstimate(flops=1_000_000, bytes_accessed=4_000_000, transcendentals=0),
+        name="early",
+    )(ids, early, lax.ppermute(early, "mem", twin))
+    late = jnp.stack([sources[by] for by in LATE])
     rows, quadratic = pl.pallas_call(
-        functools.partial(place_kernel, scale),
+        functools.partial(late_kernel, scale),
         out_shape=(
             jax.ShapeDtypeStruct(field_rows.shape, jnp.float32),
             jax.ShapeDtypeStruct((1, 1), jnp.float32),
         ),
-        in_specs=[smem, vmem, vmem],
+        in_specs=[smem, hbm, vmem, vmem, vmem],
         out_specs=(hbm, smem),
-        scratch_shapes=[
-            pltpu.VMEM((chips * chunk * 2, LANES), jnp.float32),
-            pltpu.SemaphoreType.DMA((2, chips)),
-        ],
+        scratch_shapes=scratch,
+        input_output_aliases={1: 0},
         compiler_params=params,
-        name="place",
-    )(ids, same, other)
+        name="late",
+    )(ids, rows, early, late, lax.ppermute(late, "mem", twin))
     product = rows.reshape(LEVELS, tiles, 2, LANES).transpose(2, 0, 1, 3).reshape(field.shape)
     return (product, quadratic.reshape(()))
 

time: 70.3 us -> 73.6 us (1.047)
  waiting for transfers between devices: 13.5 us -> 6.01 us
  local copies, waits for them, and re-layouts: 0.05 us -> 6.44 us
  Pallas kernels: 14.7 us -> 19.2 us
  blocking collectives: 14.3 us -> 10.2 us
  starting transfers between devices: 26.5 us -> 30.2 us
    unnamed x4 -> x20, local copies, waits for them, and re-layouts: 0.01 us -> 6.4 us
    ppermute x6, waiting for transfers between devices: 9.99 us -> 4.55 us  [shift_chips(): return lax.ppermute(array, 'mem', pairs)]
    ppermute x1 -> x2, starting transfers between devices: 1.65 us -> 5.99 us  [the longest x1 5.42 us: on_device(): lax.ppermute(early, 'mem', twin)]
    all_to_all x1, blocking collectives: 14.3 us -> 10.2 us  [on_device(): spread = lax.all_to_all(spread, 'patch', 0, 0)]
    pallas_call x2 -> x4, Pallas kernels: 9.19 us -> 12 us  [the longest x1 4.62 us: on_device(): pl.pallas_call(right_kernel, out_shape=(terms, terms), in_specs=[smem] +...]
    ppermute x1 -> x2, waiting for transfers between devices: 1.47 us -> 0.01 us  [the longest x1 0.01 us: on_device(): lax.ppermute(early, 'mem', twin)]
    pallas_call x1, Pallas kernels: 3.75 us -> 4.64 us  [on_device(): pl.pallas_call(interior_kernel, out_shape=(jax.ShapeDtypeStruct((own // B...]
    pallas_call x1, Pallas kernels: 1.8 us -> 2.58 us  [on_device(): pl.pallas_call(functools.partial(prepare_kernel, all_cells), out_shape=(s...]
  transfers between devices with their start and end apart: 10 -> 11, of which waited for: 6 -> 3; matrix products, arithmetic and copies ran while one was open for 0% -> 0% of each run, Pallas kernels for 5% -> 14%
where the time goes in v3:
time: 73.6 us; the launch traced here: 73.3 us
  starting transfers between devices  30.2 us (41%)
  Pallas kernels  19.2 us (26%)
  blocking collectives  10.2 us (14%)
  local copies, waits for them, and re-layouts  6.44 us (9%)
  waiting for transfers between devices  6.01 us (8%)
  between operations  0.95 us (1%)
    ppermute x6, starting transfers between devices, shift_chips(): return lax.ppermute(array, 'mem', pairs)  14.6 us
    all_to_all x1, blocking collectives, on_device(): spread = lax.all_to_all(spread, 'patch', 0, 0)  10.2 us
    unnamed x20, local copies, waits for them, and re-layouts  6.4 us
    ppermute x1, starting transfers between devices, on_device(): lax.ppermute(early, 'mem', twin)  5.42 us
    ppermute x1, starting transfers between devices, on_device(): lax.ppermute(head, 'patch', [((i + 1) % patches, i) for i in range(patche...  5.16 us
    pallas_call x1, Pallas kernels, on_device(): pl.pallas_call(interior_kernel, out_shape=(jax.ShapeDtypeStruct((own // B...  4.64 us
    pallas_call x1, Pallas kernels, on_device(): pl.pallas_call(right_kernel, out_shape=(terms, terms), in_specs=[smem] +...  4.62 us
    ppermute x6, waiting for transfers between devices, shift_chips(): return lax.ppermute(array, 'mem', pairs)  4.55 us
  transfers between devices with their start and end apart: 11, of which 3 were waited for; matrix products, arithmetic and copies ran while one was open for 0% of the time, Pallas kernels for 14%

profile of v3, /device:TPU:1, one launch (start us, length us, event | category | flops | bytes accessed | tf_op | source)
XLA Modules:
  0.0 73.3 jit_solution(11056345214187393699)
XLA Ops:
  0.6 2.6 %prepare.1 = (f32[64,1024]{1,0:T(8,128)}, f32[64,1024]{1,0:T(8,128)}) custom-call(s32[1]{0:T(128)} %bitcast.2.place, f32[1760,128]{1,0:T(8,128)} %bitcast.27, f32[1760,128]{1,0:T(8,128)} %bitcast.30, f32[1,2048]{1,0:T(1,128)} %bitcast.34, s32[7,2048]{1,0:T(8,128)} %neigh.1), custom_call_target="tpu_custom_call" | custom-call | tf_op jit(solution)/shard_map/prepare/pallas_call | solution.py:378
  3.2 2.1 %collective-permute-start.1 = (f32[64,1024]{1,0:T(8,128)}, f32[64,1024]{1,0:T(8,128)}, u32[]{:S(2)}, u32[]{:S(2)}) collective-permute-start(f32[64,1024]{1,0:T(8,128)} %get-tuple-element.21.tail), channel_id=1, source_target_pairs={{0,1},{1,2},{2,3},{3,4},{4,5},{5,6},{6,7},{7,8},{8,9},{9,10},{10,1... | collective-permute-start | bytes 786440 | tf_op jit(solution)/shard_map/ppermute | solution.py:394
  5.3 5.2 %collective-permute-start = (f32[64,1024]{1,0:T(8,128)}, f32[64,1024]{1,0:T(8,128)}, u32[]{:S(2)}, u32[]{:S(2)}) collective-permute-start(f32[64,1024]{1,0:T(8,128)} %get-tuple-element.20.head), channel_id=1, source_target_pairs={{1,0},{2,1},{3,2},{4,3},{5,4},{6,5},{7,6},{8,7},{9,8},{10,9},{11,1... | collective-permute-start | bytes 786440 | tf_op jit(solution)/shard_map/ppermute | solution.py:395
  10.5 4.6 %interior.1 = (bf16[8,512,256]{2,1,0:T(8,128)(2,1)S(1)}, f32[64,2048]{1,0:T(8,128)S(1)}, bf16[224,2048]{1,0:T(8,128)(2,1)S(1)}, bf16[224,2048]{1,0:T(8,128)(2,1)...) custom-call(f32[64,1024]{1,0:T(8,128)} %get-tuple-element.20.head, f32[64,1024]{1,0:T(8,128)} %get-tuple-element.21.tail), custom_call_target="tpu_custom_call" | custom-call | bytes 7000000 | tf_op jit(solution)/shard_map/interior/pallas_call | solution.py:398
  15.2 0.0 copy-start
  15.2 0.9 %copy-done = bf16[224,2048]{1,0:T(8,128)(2,1)} copy-done((bf16[224,2048]{1,0:T(8,128)(2,1)}, bf16[224,2048]{1,0:T(8,128)(2,1)S(1)}, u32[]{:S(2)}) %copy-start) | copy-done | bytes 917528
  16.1 0.0 copy-start.3
  16.1 1.0 %copy-done.3 = bf16[224,2048]{1,0:T(8,128)(2,1)} copy-done((bf16[224,2048]{1,0:T(8,128)(2,1)}, bf16[224,2048]{1,0:T(8,128)(2,1)S(1)}, u32[]{:S(2)}) %copy-start.3) | copy-done | bytes 917528
  17.1 0.0 copy-start.6
  17.1 0.9 %copy-done.6 = bf16[224,2048]{1,0:T(8,128)(2,1)} copy-done((bf16[224,2048]{1,0:T(8,128)(2,1)}, bf16[224,2048]{1,0:T(8,128)(2,1)S(1)}, u32[]{:S(2)}) %copy-start.6) | copy-done | bytes 917528
  18.0 0.1 pad_add_fusion.ids
  18.1 0.0 collective-permute-done.1.left
  18.1 0.0 copy-start.1
  18.1 1.2 %copy-done.1 = bf16[224,2048]{1,0:T(8,128)(2,1)S(1)} copy-done((bf16[224,2048]{1,0:T(8,128)(2,1)S(1)}, bf16[224,2048]{1,0:T(8,128)(2,1)}, u32[]{:S(2)}) %copy-start.1) | copy-done | bytes 917528
  19.3 0.0 copy-start.4
  19.3 1.2 %copy-done.4 = bf16[224,2048]{1,0:T(8,128)(2,1)S(1)} copy-done((bf16[224,2048]{1,0:T(8,128)(2,1)S(1)}, bf16[224,2048]{1,0:T(8,128)(2,1)}, u32[]{:S(2)}) %copy-start.4) | copy-done | bytes 917528
  20.4 0.0 copy-start.7
  20.4 1.2 %copy-done.7 = bf16[224,2048]{1,0:T(8,128)(2,1)S(1)} copy-done((bf16[224,2048]{1,0:T(8,128)(2,1)S(1)}, bf16[224,2048]{1,0:T(8,128)(2,1)}, u32[]{:S(2)}) %copy-start.7) | copy-done | bytes 917528
  21.6 0.0 copy-start.2
  21.6 0.0 copy-start.5
  21.6 0.0 copy-start.8
  21.6 0.0 copy-start.9
  21.6 4.1 %left.1 = (f32[64,2048]{1,0:T(8,128)S(1)}, bf16[224,384]{1,0:T(8,128)(2,1)S(1)}) custom-call(f32[64,1024]{1,0:T(8,128)} %collective-permute-done.1.left, bf16[8,512,256]{2,1,0:T(8,128)(2,1)S(1)} %get-tuple-element.22.inner, f32[64,2048]{1,0:T(8,128)S(1)} %get-tuple-element.23.done, bf16[224,2048]{1,0:T(8,128)(2,1)S(1)} %get-tuple-element.24.own0, ...), custom_call_target="tpu_custom_call" | custom-call | bytes 7000000 | tf_op jit(solution)/shard_map/left/pallas_call | solution.py:413
  25.8 0.0 collective-permute-done.right
  25.8 0.0 copy-done.2
  25.8 0.0 copy-done.5
  25.8 0.0 copy-done.8
  25.8 0.0 copy-done.9
  25.8 4.6 %right.1 = (f32[904,128]{1,0:T(8,128)S(1)}, f32[904,128]{1,0:T(8,128)S(1)}) custom-call(s32[2]{0:T(128)S(1)} %pad_add_fusion.ids, f32[64,1024]{1,0:T(8,128)} %collective-permute-done.right, f32[64,1024]{1,0:T(8,128)} %get-tuple-element.20.head, f32[64,1024]{1,0:T(8,128)} %get-tuple-element.21.tail, f32[55,55]{1,0:T(8,128)S(1)} %copy-done.9, ...), custom_call_target="tpu_custom_call" | custom-call | bytes 7000000 | tf_op jit(solution)/shard_map/right/pallas_call | solution.py:428
  30.5 2.4 %collective-permute-start.2 = (f32[904,128]{1,0:T(8,128)S(1)}, f32[904,128]{1,0:T(8,128)S(1)}, u32[]{:S(2)}, u32[]{:S(2)}) collective-permute-start(f32[904,128]{1,0:T(8,128)S(1)} %get-tuple-element.31), channel_id=1, source_target_pairs={{0,32},{32,0},{64,96},{96,64},{128,160},{160,128},{192,224},{224,1... | collective-permute-start | bytes 1388552 | tf_op jit(solution)/shard_map/ppermute | solution.py:453
  32.8 1.4 %collective-permute-done.2 = f32[904,128]{1,0:T(8,128)S(1)} collective-permute-done((f32[904,128]{1,0:T(8,128)S(1)}, f32[904,128]{1,0:T(8,128)S(1)}, u32[]{:S(2)}, u32[]{:S(2)}) %collective-permute-start.2) | collective-permute-done | bytes 462880 | tf_op jit(solution)/shard_map/ppermute | solution.py:453
  34.4 4.5 %collective-permute-start.5 = (f32[224,128]{1,0:T(8,128)S(1)}, f32[224,128]{1,0:T(8,128)S(1)}, u32[]{:S(2)}, u32[]{:S(2)}) collective-permute-start(f32[224,128]{1,0:T(8,128)S(1)} %get-tuple-element.38), channel_id=1, source_target_pairs={{0,192},{32,224},{64,0},{96,32},{128,64},{160,96},{192,128},{224,1... | collective-permute-start | bytes 344072 | tf_op jit(solution)/shard_map/ppermute | solution.py:449
  38.9 1.0 %collective-permute-start.4 = (f32[224,128]{1,0:T(8,128)S(1)}, f32[224,128]{1,0:T(8,128)S(1)}, u32[]{:S(2)}, u32[]{:S(2)}) collective-permute-start(f32[224,128]{1,0:T(8,128)S(1)} %get-tuple-element.39), channel_id=1, source_target_pairs={{0,128},{32,160},{64,192},{96,224},{128,0},{160,32},{192,64},{224,... | collective-permute-start | bytes 344072 | tf_op jit(solution)/shard_map/ppermute | solution.py:449
  39.9 2.3 %collective-permute-start.3 = (f32[224,128]{1,0:T(8,128)S(1)}, f32[224,128]{1,0:T(8,128)S(1)}, u32[]{:S(2)}, u32[]{:S(2)}) collective-permute-start(f32[224,128]{1,0:T(8,128)S(1)} %get-tuple-element.40), channel_id=1, source_target_pairs={{0,64},{32,96},{64,128},{96,160},{128,192},{160,224},{192,0},{224,... | collective-permute-start | bytes 344072 | tf_op jit(solution)/shard_map/ppermute | solution.py:449
  42.2 10.2 %all_to_all.5 = f32[32,1,128]{2,1,0:T(1,128)S(1)} all-to-all(f32[32,1,128]{2,1,0:T(1,128)S(1)} %broadcast_in_dim.14), channel_id=1, replica_groups=mesh['mem'=8,'patch'=32] {'patch'}, dimensions={0} | all-to-all | bytes 32768 | tf_op jit(solution)/shard_map/all_to_all | solution.py:457
  52.4 0.0 collective-permute-done.5
  52.4 0.0 collective-permute-done.4
  52.4 0.0 collective-permute-done.3
  52.4 0.1 reduce_sum.9
  52.5 3.2 %collective-permute-start.6 = (f32[232,128]{1,0:T(8,128)S(1)}, f32[232,128]{1,0:T(8,128)S(1)}, u32[]{:S(2)}, u32[]{:S(2)}) collective-permute-start(f32[232,128]{1,0:T(8,128)S(1)} %get-tuple-element.42), channel_id=1, source_target_pairs={{0,128},{32,160},{64,192},{96,224},{128,0},{160,32},{192,64},{224,... | collective-permute-start | bytes 356360 | tf_op jit(solution)/shard_map/ppermute | solution.py:449
  55.7 0.6 collective-permute-start.8
  56.3 3.0 %collective-permute-start.9 = (f32[232,128]{1,0:T(8,128)S(1)}, f32[232,128]{1,0:T(8,128)S(1)}, u32[]{:S(2)}, u32[]{:S(2)}) collective-permute-start(f32[232,128]{1,0:T(8,128)S(1)} %get-tuple-element.42), channel_id=1, source_target_pairs={{0,192},{32,224},{64,0},{96,32},{128,64},{160,96},{192,128},{224,1... | collective-permute-start | bytes 356360 | tf_op jit(solution)/shard_map/ppermute | solution.py:449
  59.3 1.0 %collective-permute-done.6 = f32[232,128]{1,0:T(8,128)S(1)} collective-permute-done((f32[232,128]{1,0:T(8,128)S(1)}, f32[232,128]{1,0:T(8,128)S(1)}, u32[]{:S(2)}, u32[]{:S(2)}) %collective-permute-start.6) | collective-permute-done | bytes 118816 | tf_op jit(solution)/shard_map/ppermute | solution.py:449
  60.3 5.4 %collective-permute-start.7 = (f32[2,232,128]{2,1,0:T(8,128)S(1)}, f32[2,232,128]{2,1,0:T(8,128)S(1)}, u32[]{:S(2)}, u32[]{:S(2)}) collective-permute-start(f32[2,232,128]{2,1,0:T(8,128)S(1)} %pad_maximum_fusion.same.early), channel_id=1, source_target_pairs={{0,32},{32,0},{64,96},{96,64},{128,160},{160,128},{192,224},{224,1... | collective-permute-start | bytes 712712 | tf_op jit(solution)/shard_map/ppermute | solution.py:478
  65.7 0.0 collective-permute-done.8
  65.7 3.5 %collective-permute-done.9 = f32[232,128]{1,0:T(8,128)S(1)} collective-permute-done((f32[232,128]{1,0:T(8,128)S(1)}, f32[232,128]{1,0:T(8,128)S(1)}, u32[]{:S(2)}, u32[]{:S(2)}) %collective-permute-start.9) | collective-permute-done | bytes 118816 | tf_op jit(solution)/shard_map/ppermute | solution.py:449
  69.3 0.6 collective-permute-start.10
  69.9 0.0 collective-permute-done.7.other
  69.9 1.4 %early.1.begun = f32[1760,128]{1,0:T(8,128)} custom-call(s32[2]{0:T(128)S(1)} %pad_add_fusion.ids, f32[2,232,128]{2,1,0:T(8,128)S(1)} %pad_maximum_fusion.same.early, f32[2,232,128]{2,1,0:T(8,128)S(1)} %collective-permute-done.7.other), custom_call_target="tpu_custom_call" | custom-call | flops 1000000 | bytes 4000000 | tf_op jit(solution)/shard_map/early/pallas_call | solution.py:469
  71.2 0.0 collective-permute-done.10.other
  71.3 1.9 %late.1 = (f32[1760,128]{1,0:T(8,128)}, f32[1,1]{1,0:T(1,128)}) custom-call(s32[2]{0:T(128)S(1)} %pad_add_fusion.ids, f32[1760,128]{1,0:T(8,128)} %early.1.begun, f32[2,232,128]{2,1,0:T(8,128)S(1)} %pad_maximum_fusion.same.early, f32[2,232,128]{2,1,0:T(8,128)S(1)} %pad_maximum_fusion.1.same, ...), custom_call_target="tpu_custom_call", output_to_operand_aliasing={{0}: (1, {})} | custom-call | tf_op jit(solution)/shard_map/late/pallas_call | solution.py:480
  (9 shorter events, 0.2 us)
Async XLA Ops:
  3.2 14.9 %collective-permute-start.1 = (f32[64,1024]{1,0:T(8,128)}, f32[64,1024]{1,0:T(8,128)}, u32[]{:S(2)}, u32[]{:S(2)}) collective-permute-start(f32[64,1024]{1,0:T(8,128)} %get-tuple-element.21.tail), channel_id=1, source_target_pairs={{0,1},{1,2},{2,3},{3,4},{4,5},{5,6},{6,7},{7,8},{8,9},{9,10},{10,1... | collective-permute-start | bytes 786440 | tf_op jit(solution)/shard_map/ppermute | solution.py:394
  5.3 20.4 %collective-permute-start = (f32[64,1024]{1,0:T(8,128)}, f32[64,1024]{1,0:T(8,128)}, u32[]{:S(2)}, u32[]{:S(2)}) collective-permute-start(f32[64,1024]{1,0:T(8,128)} %get-tuple-element.20.head), channel_id=1, source_target_pairs={{1,0},{2,1},{3,2},{4,3},{5,4},{6,5},{7,6},{8,7},{9,8},{10,9},{11,1... | collective-permute-start | bytes 786440 | tf_op jit(solution)/shard_map/ppermute | solution.py:395
  15.2 0.9 %copy-start = (bf16[224,2048]{1,0:T(8,128)(2,1)}, bf16[224,2048]{1,0:T(8,128)(2,1)S(1)}, u32[]{:S(2)}) copy-start(bf16[224,2048]{1,0:T(8,128)(2,1)S(1)} %get-tuple-element.25.own1) | copy-start | bytes 2752516
  16.1 1.0 %copy-start.3 = (bf16[224,2048]{1,0:T(8,128)(2,1)}, bf16[224,2048]{1,0:T(8,128)(2,1)S(1)}, u32[]{:S(2)}) copy-start(bf16[224,2048]{1,0:T(8,128)(2,1)S(1)} %get-tuple-element.26.own2) | copy-start | bytes 2752516
  17.1 0.9 %copy-start.6 = (bf16[224,2048]{1,0:T(8,128)(2,1)}, bf16[224,2048]{1,0:T(8,128)(2,1)S(1)}, u32[]{:S(2)}) copy-start(bf16[224,2048]{1,0:T(8,128)(2,1)S(1)} %get-tuple-element.27.own3) | copy-start | bytes 2752516
  18.1 1.2 %copy-start.1 = (bf16[224,2048]{1,0:T(8,128)(2,1)S(1)}, bf16[224,2048]{1,0:T(8,128)(2,1)}, u32[]{:S(2)}) copy-start(bf16[224,2048]{1,0:T(8,128)(2,1)} %copy-done) | copy-start | bytes 2752516
  19.3 1.2 %copy-start.4 = (bf16[224,2048]{1,0:T(8,128)(2,1)S(1)}, bf16[224,2048]{1,0:T(8,128)(2,1)}, u32[]{:S(2)}) copy-start(bf16[224,2048]{1,0:T(8,128)(2,1)} %copy-done.3) | copy-start | bytes 2752516
  20.4 1.2 %copy-start.7 = (bf16[224,2048]{1,0:T(8,128)(2,1)S(1)}, bf16[224,2048]{1,0:T(8,128)(2,1)}, u32[]{:S(2)}) copy-start(bf16[224,2048]{1,0:T(8,128)(2,1)} %copy-done.6) | copy-start | bytes 2752516
  21.6 4.2 %copy-start.2 = (bf16[224,2048]{1,0:T(8,128)(2,1)S(1)}, bf16[224,2048]{1,0:T(8,128)(2,1)}, u32[]{:S(2)}) copy-start(bf16[224,2048]{1,0:T(8,128)(2,1)} %copy-done) | copy-start | bytes 2752516
  21.6 4.2 %copy-start.5 = (bf16[224,2048]{1,0:T(8,128)(2,1)S(1)}, bf16[224,2048]{1,0:T(8,128)(2,1)}, u32[]{:S(2)}) copy-start(bf16[224,2048]{1,0:T(8,128)(2,1)} %copy-done.3) | copy-start | bytes 2752516
  21.6 4.2 %copy-start.8 = (f32[1,2,55,2048]{3,1,2,0:T(2,128)S(1)}, f32[1,2,55,2048]{3,1,2,0:T(2,128)}, u32[]{:S(2)}) copy-start(f32[1,2,55,2048]{3,1,2,0:T(2,128)} %param.5) | copy-start | bytes 2703364
  21.6 4.2 %copy-start.9 = (f32[55,55]{1,0:T(8,128)S(1)}, f32[55,55]{1,0:T(8,128)}, u32[]{:S(2)}) copy-start(f32[55,55]{1,0:T(8,128)} %root.1) | copy-start | bytes 36304
  30.5 3.8 %collective-permute-start.2 = (f32[904,128]{1,0:T(8,128)S(1)}, f32[904,128]{1,0:T(8,128)S(1)}, u32[]{:S(2)}, u32[]{:S(2)}) collective-permute-start(f32[904,128]{1,0:T(8,128)S(1)} %get-tuple-element.31), channel_id=1, source_target_pairs={{0,32},{32,0},{64,96},{96,64},{128,160},{160,128},{192,224},{224,1... | collective-permute-start | bytes 1388552 | tf_op jit(solution)/shard_map/ppermute | solution.py:453
  34.4 18.0 %collective-permute-start.5 = (f32[224,128]{1,0:T(8,128)S(1)}, f32[224,128]{1,0:T(8,128)S(1)}, u32[]{:S(2)}, u32[]{:S(2)}) collective-permute-start(f32[224,128]{1,0:T(8,128)S(1)} %get-tuple-element.38), channel_id=1, source_target_pairs={{0,192},{32,224},{64,0},{96,32},{128,64},{160,96},{192,128},{224,1... | collective-permute-start | bytes 344072 | tf_op jit(solution)/shard_map/ppermute | solution.py:449
  38.9 13.5 %collective-permute-start.4 = (f32[224,128]{1,0:T(8,128)S(1)}, f32[224,128]{1,0:T(8,128)S(1)}, u32[]{:S(2)}, u32[]{:S(2)}) collective-permute-start(f32[224,128]{1,0:T(8,128)S(1)} %get-tuple-element.39), channel_id=1, source_target_pairs={{0,128},{32,160},{64,192},{96,224},{128,0},{160,32},{192,64},{224,... | collective-permute-start | bytes 344072 | tf_op jit(solution)/shard_map/ppermute | solution.py:449
  39.9 12.5 %collective-permute-start.3 = (f32[224,128]{1,0:T(8,128)S(1)}, f32[224,128]{1,0:T(8,128)S(1)}, u32[]{:S(2)}, u32[]{:S(2)}) collective-permute-start(f32[224,128]{1,0:T(8,128)S(1)} %get-tuple-element.40), channel_id=1, source_target_pairs={{0,64},{32,96},{64,128},{96,160},{128,192},{160,224},{192,0},{224,... | collective-permute-start | bytes 344072 | tf_op jit(solution)/shard_map/ppermute | solution.py:449
  52.5 7.8 %collective-permute-start.6 = (f32[232,128]{1,0:T(8,128)S(1)}, f32[232,128]{1,0:T(8,128)S(1)}, u32[]{:S(2)}, u32[]{:S(2)}) collective-permute-start(f32[232,128]{1,0:T(8,128)S(1)} %get-tuple-element.42), channel_id=1, source_target_pairs={{0,128},{32,160},{64,192},{96,224},{128,0},{160,32},{192,64},{224,... | collective-permute-start | bytes 356360 | tf_op jit(solution)/shard_map/ppermute | solution.py:449
  55.7 10.0 %collective-permute-start.8 = (f32[232,128]{1,0:T(8,128)S(1)}, f32[232,128]{1,0:T(8,128)S(1)}, u32[]{:S(2)}, u32[]{:S(2)}) collective-permute-start(f32[232,128]{1,0:T(8,128)S(1)} %get-tuple-element.42), channel_id=1, source_target_pairs={{0,64},{32,96},{64,128},{96,160},{128,192},{160,224},{192,0},{224,... | collective-permute-start | bytes 356360 | tf_op jit(solution)/shard_map/ppermute | solution.py:449
  56.3 13.0 %collective-permute-start.9 = (f32[232,128]{1,0:T(8,128)S(1)}, f32[232,128]{1,0:T(8,128)S(1)}, u32[]{:S(2)}, u32[]{:S(2)}) collective-permute-start(f32[232,128]{1,0:T(8,128)S(1)} %get-tuple-element.42), channel_id=1, source_target_pairs={{0,192},{32,224},{64,0},{96,32},{128,64},{160,96},{192,128},{224,1... | collective-permute-start | bytes 356360 | tf_op jit(solution)/shard_map/ppermute | solution.py:449
  60.3 9.6 %collective-permute-start.7 = (f32[2,232,128]{2,1,0:T(8,128)S(1)}, f32[2,232,128]{2,1,0:T(8,128)S(1)}, u32[]{:S(2)}, u32[]{:S(2)}) collective-permute-start(f32[2,232,128]{2,1,0:T(8,128)S(1)} %pad_maximum_fusion.same.early), channel_id=1, source_target_pairs={{0,32},{32,0},{64,96},{96,64},{128,160},{160,128},{192,224},{224,1... | collective-permute-start | bytes 712712 | tf_op jit(solution)/shard_map/ppermute | solution.py:478
  69.3 1.9 %collective-permute-start.10 = (f32[2,232,128]{2,1,0:T(8,128)S(1)}, f32[2,232,128]{2,1,0:T(8,128)S(1)}, u32[]{:S(2)}, u32[]{:S(2)}) collective-permute-start(f32[2,232,128]{2,1,0:T(8,128)S(1)} %pad_maximum_fusion.1.same), channel_id=1, source_target_pairs={{0,32},{32,0},{64,96},{96,64},{128,160},{160,128},{192,224},{224,1... | collective-permute-start | bytes 712712 | tf_op jit(solution)/shard_map/ppermute | solution.py:492

commit v4 on v3

--- a/solution.py
+++ b/solution.py
@@ -126,15 +126,40 @@
     return range(skip, count - skip)
 
 
-def interior_kernel(head, tail, adj, state, buf0, buf1, buf2, buf3):
+def seams(own, side):
+    packed = 0
+    for step in range(STEPS - 1):
+        low = interior_blocks(step, own // BLOCK)[0] * BLOCK
+        high = low + REACH + (BLOCK if step % 2 == 0 else 0)
+        if side:
+            yield step, own - high, own - low, packed
+        else:
+            yield step, low, high, packed
+        packed += high - low
+
+
+def packed_columns(own):
+    return sum(high - low for _, low, high, _ in seams(own, 0))
+
+
+def interior_kernel(
+    head, tail, near_adj, far_adj, near_state, far_state, near_parts, far_parts, values,
+    adj, state, buf0, buf1, buf2, buf3,
+):
     bufs = (buf0, buf1, buf2, buf3)
     blocks = adj.shape[0]
+    own = blocks * BLOCK
     half = blocks // 2
     for block in range(blocks):
         source, at = (head, block * BLOCK) if block < half else (tail, (block - half) * BLOCK)
 
         def store(down, across, value):
-            adj[block, down * LANES : (down + 1) * LANES, across * LANES : (across + 1) * LANES] = value
+            spot = (slice(down * LANES, (down + 1) * LANES), slice(across * LANES, (across + 1) * LANES))
+            adj[block, *spot] = value
+            if block < half:
+                near_adj[block, *spot] = value
+            if block >= half - 1:
+                far_adj[block - (half - 1), *spot] = value
 
         value = source[:, at : at + BLOCK]
         build_block(value[56:63], store)
@@ -142,6 +167,7 @@
         here = block * BLOCK
         state[0:56, here : here + BLOCK] = value[0:56]
         state[56:64, here : here + BLOCK] = jnp.broadcast_to(coeff, (8, BLOCK))
+        values[:, here : here + BLOCK] = value[0:56]
         store_parts(buf0, here, split(value[0:56], coeff))
     for step in range(1, STEPS - 1):
         whole = interior_blocks(step, blocks)
@@ -151,6 +177,11 @@
             places.append((low * BLOCK + REACH, REACH, lambda: adj[low, REACH:, REACH:], False))
             places.append((high * BLOCK, REACH, lambda: adj[high, : BLOCK + REACH, :REACH], False))
         sweep(state, bufs[(step - 1) % 4], bufs[step % 4], (0, 0), places)
+    near_state[...] = state[:, 0 : own // 2]
+    far_state[...] = state[:, own // 2 :]
+    for side, parts in ((0, near_parts), (1, far_parts)):
+        for step, low, high, packed in seams(own, side):
+            parts[:, packed : packed + high - low] = bufs[step % 4][:, low:high]
 
 
 def load_halo(part, at, state, outer, buf, bases):
@@ -169,31 +200,23 @@
         build_block(value[56:63], store)
 
 
-def carry_over(owns, bufs, side, bases):
-    own = owns[0].shape[1]
-    for step in range(STEPS - 1):
-        low = interior_blocks(step, own // BLOCK)[0] * BLOCK
-        if step % 2 == 0:
-            high = low + BLOCK + REACH
-        else:
-            high = low + REACH
-        if side:
-            low, high = own - high, own - low
-        at = HALO - bases[1]
-        bufs[step % 4][:, at + low : at + high] = owns[step % 4][:, low:high]
-
-
-def left_kernel(left, inner, done, own0, own1, own2, own3, state, seam, outer, buf0, buf1, buf2, buf3):
-    own = done.shape[1]
+def carry_over(parts, bufs, own, side, bases):
+    at = HALO - bases[1]
+    for step, low, high, packed in seams(own, side):
+        bufs[step % 4][:, at + low : at + high] = parts[:, packed : packed + high - low]
+
+
+def left_kernel(left, inner, done, parts, state, seam, outer, buf0, buf1, buf2, buf3):
+    own = 2 * done.shape[1]
     bases = (0, -REACH)
     bufs = (buf0, buf1, buf2, buf3)
     fringe = HALO // BLOCK
     middle = fringe + own // BLOCK // 2
-    state[:, HALO:] = done[:, 0 : own // 2]
+    state[:, HALO:] = done[...]
     edge = jnp.zeros((224, REACH), jnp.bfloat16)
     buf0[:, 0:REACH] = edge
     buf2[:, 2 * REACH : 3 * REACH] = edge
-    carry_over((own0, own1, own2, own3), bufs, 0, bases)
+    carry_over(parts, bufs, own, 0, bases)
     load_halo(left, 0, state, outer, buf0, bases)
     for step in range(1, STEPS + 1):
         inside = interior_blocks(step, own // BLOCK)
@@ -211,10 +234,10 @@
 
 
 def right_kernel(
-    ids, right, head, tail, root, ens, west, seam, inner, done, own0, own1, own2, own3,
+    ids, right, root, ens, west, seam, inner, done, parts, values,
     keep, send, state, outer, buf0, buf1, buf2, buf3, square, rowed,
 ):
-    own = done.shape[1]
+    own = 2 * done.shape[1]
     wide = own + 2 * HALO
     tiles = own // LANES
     blocks = wide // BLOCK
@@ -223,11 +246,11 @@
     bases = ((middle - 1) * BLOCK, (middle - 2) * BLOCK)
     bufs = (buf0, buf1, buf2, buf3)
     state[:, 0:BLOCK] = west[:, (middle - 1) * BLOCK :]
-    state[:, BLOCK : BLOCK + own // 2] = done[:, own // 2 :]
+    state[:, BLOCK : BLOCK + own // 2] = done[...]
     edge = jnp.zeros((224, REACH), jnp.bfloat16)
     buf0[:, wide - bases[1] :] = edge
     buf2[:, wide - 2 * REACH - bases[1] : wide - REACH - bases[1]] = edge
-    carry_over((own0, own1, own2, own3), bufs, 1, bases)
+    carry_over(parts, bufs, own, 1, bases)
     load_halo(right, HALO + own, state, outer, buf0, bases)
     for step in range(1, STEPS + 1):
         inside = interior_blocks(step, own // BLOCK)
@@ -236,7 +259,7 @@
             (
                 block * BLOCK, BLOCK,
                 functools.partial(
-                    lambda b: inner[b - fringe] if b < blocks - fringe else outer[b - (blocks - fringe)], block
+                    lambda b: inner[b - (middle - 1)] if b < blocks - fringe else outer[b - (blocks - fringe)], block
                 ), True,
             )
             for block in range(start, blocks - step // 2)
@@ -264,9 +287,8 @@
         first = jnp.dot(stacked, high, preferred_element_type=jnp.float32)
         second = jnp.dot(matrix_high, low, preferred_element_type=jnp.float32)
         smoothed = first[0:LEVELS] + (first[64 : 64 + LEVELS] + second[0:LEVELS])
-        source = head if block < own // BLOCK // 2 else tail
-        at = (block * BLOCK) % head.shape[1]
-        total = total + jnp.sum(source[0:LEVELS, at : at + BLOCK] * smoothed, axis=0, keepdims=True)
+        at = block * BLOCK
+        total = total + jnp.sum(values[0:LEVELS, at : at + BLOCK] * smoothed, axis=0, keepdims=True)
         for tile in range(BLOCK // LANES):
             spot = block * (BLOCK // LANES) + tile
             rowed[pl.ds(spot, LEVELS, stride=tiles), :] = smoothed[:, tile * LANES : (tile + 1) * LANES]
@@ -394,16 +416,22 @@
     left = lax.ppermute(tail, "patch", [(i, (i + 1) % patches) for i in range(patches)])
     right = lax.ppermute(head, "patch", [((i + 1) % patches, i) for i in range(patches)])
 
-    parts = jax.ShapeDtypeStruct((224, own), jnp.bfloat16)
-    inside = pl.pallas_call(
+    blocks = own // BLOCK
+    adjacency = (2 * BLOCK, BLOCK)
+    packed = jax.ShapeDtypeStruct((224, packed_columns(own)), jnp.bfloat16)
+    half_state = jax.ShapeDtypeStruct((64, half), jnp.float32)
+    near_adj, far_adj, near_state, far_state, near_parts, far_parts, values = pl.pallas_call(
         interior_kernel,
         out_shape=(
-            jax.ShapeDtypeStruct((own // BLOCK, 2 * BLOCK, BLOCK), jnp.bfloat16),
-            jax.ShapeDtypeStruct((64, own), jnp.float32),
-            parts, parts, parts, parts,
+            jax.ShapeDtypeStruct((blocks // 2, *adjacency), jnp.bfloat16),
+            jax.ShapeDtypeStruct((blocks // 2 + 1, *adjacency), jnp.bfloat16),
+            half_state, half_state, packed, packed,
+            jax.ShapeDtypeStruct((56, own), jnp.float32),
         ),
         in_specs=[vmem] * 2,
-        out_specs=(vmem,) * 6,
+        out_specs=(vmem,) * 7,
+        scratch_shapes=[pltpu.VMEM((blocks, *adjacency), jnp.bfloat16), pltpu.VMEM((64, own), jnp.float32)]
+        + [pltpu.VMEM((224, own), jnp.bfloat16)] * 4,
         compiler_params=params,
         cost_estimate=pl.CostEstimate(flops=0, bytes_accessed=7_000_000, transcendentals=0),
         name="interior",
@@ -416,19 +444,19 @@
             jax.ShapeDtypeStruct((64, HALO + half), jnp.float32),
             jax.ShapeDtypeStruct((224, BLOCK + REACH), jnp.bfloat16),
         ),
-        in_specs=[vmem] * 7,
+        in_specs=[vmem] * 4,
         out_specs=(vmem,) * 2,
         scratch_shapes=[pltpu.VMEM((HALO // BLOCK, 2 * BLOCK, BLOCK), jnp.bfloat16)]
         + [pltpu.VMEM((224, HALO + half + 2 * REACH), jnp.bfloat16)] * 4,
         compiler_params=params,
         cost_estimate=pl.CostEstimate(flops=0, bytes_accessed=7_000_000, transcendentals=0),
         name="left",
-    )(left, *inside)
+    )(left, near_adj, near_state, near_parts)
     terms = jax.ShapeDtypeStruct((chips * chunk + 8, LANES), jnp.float32)
     keep, send = pl.pallas_call(
         right_kernel,
         out_shape=(terms, terms),
-        in_specs=[smem] + [vmem] * 13,
+        in_specs=[smem] + [vmem] * 9,
         out_specs=(vmem, vmem),
         scratch_shapes=[
             pltpu.VMEM((64, BLOCK + half + HALO), jnp.float32),
@@ -442,7 +470,7 @@
         compiler_params=params,
         cost_estimate=pl.CostEstimate(flops=0, bytes_accessed=7_000_000, transcendentals=0),
         name="right",
-    )(ids, right, head, tail, vertical_root, ens_rows, west, seam, *inside)
+    )(ids, right, vertical_root, ens_rows, west, seam, far_adj, far_state, far_parts, values)
 
     def shift_chips(array, by):
         pairs = [(2 * z + c, 2 * ((z + by) % chips) + c) for z in range(chips) for c in range(2)]

time: 73.6 us -> 74.1 us (level)
  local copies, waits for them, and re-layouts: 6.44 us -> 7.27 us
  starting transfers between devices: 30.2 us -> 31 us
  waiting for transfers between devices: 6.01 us -> 5.22 us
    unnamed x20 -> x24, local copies, waits for them, and re-layouts: 6.4 us -> 7.23 us
    ppermute x6, waiting for transfers between devices: 4.55 us -> 3.76 us  [shift_chips(): return lax.ppermute(array, 'mem', pairs)]
where the time goes in v4:
time: 74.1 us; the launch traced here: 73.8 us
  starting transfers between devices  31 us (42%)
  Pallas kernels  18.9 us (26%)
  blocking collectives  10.2 us (14%)
  local copies, waits for them, and re-layouts  7.27 us (10%)
  waiting for transfers between devices  5.22 us (7%)
  between operations  0.95 us (1%)
    ppermute x6, starting transfers between devices, shift_chips(): return lax.ppermute(array, 'mem', pairs)  14.8 us
    all_to_all x1, blocking collectives, on_device(): spread = lax.all_to_all(spread, 'patch', 0, 0)  10.2 us
    unnamed x24, local copies, waits for them, and re-layouts  7.23 us
    ppermute x1, starting transfers between devices, on_device(): lax.ppermute(early, 'mem', twin)  5.77 us
    ppermute x1, starting transfers between devices, on_device(): lax.ppermute(head, 'patch', [((i + 1) % patches, i) for i in range(patche...  5.16 us
    pallas_call x1, Pallas kernels, on_device(): pl.pallas_call(interior_kernel, out_shape=(jax.ShapeDtypeStruct((blocks /...  4.96 us
    pallas_call x1, Pallas kernels, on_device(): pl.pallas_call(left_kernel, out_shape=(jax.ShapeDtypeStruct((64, HALO + h...  4.08 us
    pallas_call x1, Pallas kernels, on_device(): pl.pallas_call(right_kernel, out_shape=(terms, terms), in_specs=[smem] +...  4.04 us
  transfers between devices with their start and end apart: 11, of which 3 were waited for; matrix products, arithmetic and copies ran while one was open for 0% of the time, Pallas kernels for 14%

profile of v4, /device:TPU:1, one launch (start us, length us, event | category | flops | bytes accessed | tf_op | source)
XLA Modules:
  0.0 73.8 jit_solution(17630983907333740)
XLA Ops:
  0.6 2.6 %prepare.1 = (f32[64,1024]{1,0:T(8,128)}, f32[64,1024]{1,0:T(8,128)}) custom-call(s32[1]{0:T(128)} %bitcast.2.place, f32[1760,128]{1,0:T(8,128)} %bitcast.27, f32[1760,128]{1,0:T(8,128)} %bitcast.30, f32[1,2048]{1,0:T(1,128)} %bitcast.34, s32[7,2048]{1,0:T(8,128)} %neigh.1), custom_call_target="tpu_custom_call" | custom-call | tf_op jit(solution)/shard_map/prepare/pallas_call | solution.py:400
  3.2 2.1 %collective-permute-start.1 = (f32[64,1024]{1,0:T(8,128)}, f32[64,1024]{1,0:T(8,128)}, u32[]{:S(2)}, u32[]{:S(2)}) collective-permute-start(f32[64,1024]{1,0:T(8,128)} %get-tuple-element.22.tail), channel_id=1, source_target_pairs={{0,1},{1,2},{2,3},{3,4},{4,5},{5,6},{6,7},{7,8},{8,9},{9,10},{10,1... | collective-permute-start | bytes 786440 | tf_op jit(solution)/shard_map/ppermute | solution.py:416
  5.4 5.2 %collective-permute-start = (f32[64,1024]{1,0:T(8,128)}, f32[64,1024]{1,0:T(8,128)S(1)}, u32[]{:S(2)}, u32[]{:S(2)}) collective-permute-start(f32[64,1024]{1,0:T(8,128)} %get-tuple-element.21.head), channel_id=1, source_target_pairs={{1,0},{2,1},{3,2},{4,3},{5,4},{6,5},{7,6},{8,7},{9,8},{10,9},{11,1... | collective-permute-start | bytes 786440 | tf_op jit(solution)/shard_map/ppermute | solution.py:417
  10.5 0.0 copy-start.11
  10.5 5.0 %interior.1 = (bf16[4,512,256]{2,1,0:T(8,128)(2,1)S(1)}, bf16[5,512,256]{2,1,0:T(8,128)(2,1)S(1)}, f32[64,1024]{1,0:T(8,128)S(1)}, f32[64,1024]{1,0:T(8,128)S(1)...) custom-call(f32[64,1024]{1,0:T(8,128)} %get-tuple-element.21.head, ...), custom_call_target="tpu_custom_call" | custom-call | bytes 7000000 | tf_op jit(solution)/shard_map/interior/pallas_call | solution.py:423
  15.5 0.0 copy-start.1
  15.5 0.9 %copy-done.1 = bf16[224,1920]{1,0:T(8,128)(2,1)} copy-done((bf16[224,1920]{1,0:T(8,128)(2,1)}, bf16[224,1920]{1,0:T(8,128)(2,1)S(1)}, u32[]{:S(2)}) %copy-start.1) | copy-done | bytes 860184
  16.4 0.0 copy-start.3
  16.4 0.9 %copy-done.3 = bf16[224,1920]{1,0:T(8,128)(2,1)} copy-done((bf16[224,1920]{1,0:T(8,128)(2,1)}, bf16[224,1920]{1,0:T(8,128)(2,1)S(1)}, u32[]{:S(2)}) %copy-start.3) | copy-done | bytes 860184
  17.3 0.0 copy-start.5
  17.3 0.8 %copy-done.5 = f32[56,2048]{1,0:T(8,128)} copy-done((f32[56,2048]{1,0:T(8,128)}, f32[56,2048]{1,0:T(8,128)S(1)}, u32[]{:S(2)}) %copy-start.5) | copy-done | bytes 458776
  18.1 0.0 copy-start.7
  18.1 0.7 copy-done.7
  18.8 0.0 copy-start.9
  18.8 0.7 copy-done.9
  19.6 0.0 copy-start
  19.6 0.0 copy-start.2
  19.6 0.1 pad_add_fusion.ids
  19.6 0.0 collective-permute-done.1.left
  19.6 0.0 copy-start.4
  19.6 1.3 %copy-done.4 = bf16[224,1920]{1,0:T(8,128)(2,1)S(1)} copy-done((bf16[224,1920]{1,0:T(8,128)(2,1)S(1)}, bf16[224,1920]{1,0:T(8,128)(2,1)}, u32[]{:S(2)}) %copy-start.4) | copy-done | bytes 860184
  20.9 0.0 copy-start.10
  20.9 0.9 %copy-done.10 = f32[64,1024]{1,0:T(8,128)S(1)} copy-done((f32[64,1024]{1,0:T(8,128)S(1)}, f32[64,1024]{1,0:T(8,128)}, u32[]{:S(2)}) %copy-start.10) | copy-done | bytes 262168
  21.9 0.0 copy-start.6
  21.9 4.1 %left.1 = (f32[64,2048]{1,0:T(8,128)S(1)}, bf16[224,384]{1,0:T(8,128)(2,1)S(1)}) custom-call(f32[64,1024]{1,0:T(8,128)} %collective-permute-done.1.left, bf16[4,512,256]{2,1,0:T(8,128)(2,1)S(1)} %get-tuple-element.23.inner, f32[64,1024]{1,0:T(8,128)S(1)} %copy-done.10, bf16[224,1920]{1,0:T(8,128)(2,1)S(1)} %copy-done.4), custom_call_target="tpu_custom_call" | custom-call | bytes 7000000 | tf_op jit(solution)/shard_map/left/pallas_call | solution.py:441
  26.0 0.0 collective-permute-done.right
  26.0 0.0 copy-done.11
  26.0 0.0 copy-done
  26.0 0.0 copy-done.2
  26.0 0.0 copy-done.6
  26.0 0.0 copy-start.8
  26.0 0.9 %copy-done.8 = f32[64,1024]{1,0:T(8,128)S(1)} copy-done((f32[64,1024]{1,0:T(8,128)S(1)}, f32[64,1024]{1,0:T(8,128)}, u32[]{:S(2)}) %copy-start.8) | copy-done | bytes 262168
  27.0 4.0 %right.1 = (f32[904,128]{1,0:T(8,128)S(1)}, f32[904,128]{1,0:T(8,128)S(1)}) custom-call(s32[2]{0:T(128)S(1)} %pad_add_fusion.ids, f32[64,1024]{1,0:T(8,128)S(1)} %collective-permute-done.right, f32[55,55]{1,0:T(8,128)S(1)} %copy-done.11, f32[1760,128]{1,0:T(8,128)S(1)} %bitcast.28, f32[64,2048]{1,0:T(8,128)S(1)} %get-tuple-element.26.west, ...), custom_call_target="tpu_custom_call" | custom-call | bytes 7000000 | tf_op jit(solution)/shard_map/right/pallas_call | solution.py:456
  31.0 2.6 %collective-permute-start.2 = (f32[904,128]{1,0:T(8,128)S(1)}, f32[904,128]{1,0:T(8,128)S(1)}, u32[]{:S(2)}, u32[]{:S(2)}) collective-permute-start(f32[904,128]{1,0:T(8,128)S(1)} %get-tuple-element.33), channel_id=1, source_target_pairs={{0,32},{32,0},{64,96},{96,64},{128,160},{160,128},{192,224},{224,1... | collective-permute-start | bytes 1388552 | tf_op jit(solution)/shard_map/ppermute | solution.py:481
  33.6 1.4 %collective-permute-done.2 = f32[904,128]{1,0:T(8,128)S(1)} collective-permute-done((f32[904,128]{1,0:T(8,128)S(1)}, f32[904,128]{1,0:T(8,128)S(1)}, u32[]{:S(2)}, u32[]{:S(2)}) %collective-permute-start.2) | collective-permute-done | bytes 462880 | tf_op jit(solution)/shard_map/ppermute | solution.py:481
  35.0 0.1 add.13
  35.1 4.4 %collective-permute-start.5 = (f32[224,128]{1,0:T(8,128)S(1)}, f32[224,128]{1,0:T(8,128)S(1)}, u32[]{:S(2)}, u32[]{:S(2)}) collective-permute-start(f32[224,128]{1,0:T(8,128)S(1)} %get-tuple-element.40), channel_id=1, source_target_pairs={{0,192},{32,224},{64,0},{96,32},{128,64},{160,96},{192,128},{224,1... | collective-permute-start | bytes 344072 | tf_op jit(solution)/shard_map/ppermute | solution.py:477
  39.5 1.0 %collective-permute-start.4 = (f32[224,128]{1,0:T(8,128)S(1)}, f32[224,128]{1,0:T(8,128)S(1)}, u32[]{:S(2)}, u32[]{:S(2)}) collective-permute-start(f32[224,128]{1,0:T(8,128)S(1)} %get-tuple-element.41), channel_id=1, source_target_pairs={{0,128},{32,160},{64,192},{96,224},{128,0},{160,32},{192,64},{224,... | collective-permute-start | bytes 344072 | tf_op jit(solution)/shard_map/ppermute | solution.py:477
  40.5 2.3 %collective-permute-start.3 = (f32[224,128]{1,0:T(8,128)S(1)}, f32[224,128]{1,0:T(8,128)S(1)}, u32[]{:S(2)}, u32[]{:S(2)}) collective-permute-start(f32[224,128]{1,0:T(8,128)S(1)} %get-tuple-element.42), channel_id=1, source_target_pairs={{0,64},{32,96},{64,128},{96,160},{128,192},{160,224},{192,0},{224,... | collective-permute-start | bytes 344072 | tf_op jit(solution)/shard_map/ppermute | solution.py:477
  42.7 10.2 %all_to_all.5 = f32[32,1,128]{2,1,0:T(1,128)S(1)} all-to-all(f32[32,1,128]{2,1,0:T(1,128)S(1)} %broadcast_in_dim.14), channel_id=1, replica_groups=mesh['mem'=8,'patch'=32] {'patch'}, dimensions={0} | all-to-all | bytes 32768 | tf_op jit(solution)/shard_map/all_to_all | solution.py:485
  52.9 0.0 collective-permute-done.5
  52.9 0.0 collective-permute-done.4
  52.9 0.0 collective-permute-done.3
  53.0 0.1 reduce_sum.9
  53.1 3.6 %collective-permute-start.6 = (f32[232,128]{1,0:T(8,128)S(1)}, f32[232,128]{1,0:T(8,128)S(1)}, u32[]{:S(2)}, u32[]{:S(2)}) collective-permute-start(f32[232,128]{1,0:T(8,128)S(1)} %get-tuple-element.44), channel_id=1, source_target_pairs={{0,128},{32,160},{64,192},{96,224},{128,0},{160,32},{192,64},{224,... | collective-permute-start | bytes 356360 | tf_op jit(solution)/shard_map/ppermute | solution.py:477
  56.7 0.1 collective-permute-start.8
  56.8 3.4 %collective-permute-start.9 = (f32[232,128]{1,0:T(8,128)S(1)}, f32[232,128]{1,0:T(8,128)S(1)}, u32[]{:S(2)}, u32[]{:S(2)}) collective-permute-start(f32[232,128]{1,0:T(8,128)S(1)} %get-tuple-element.44), channel_id=1, source_target_pairs={{0,192},{32,224},{64,0},{96,32},{128,64},{160,96},{192,128},{224,1... | collective-permute-start | bytes 356360 | tf_op jit(solution)/shard_map/ppermute | solution.py:477
  60.3 0.6 collective-permute-done.6
  60.9 5.8 %collective-permute-start.7 = (f32[2,232,128]{2,1,0:T(8,128)S(1)}, f32[2,232,128]{2,1,0:T(8,128)S(1)}, u32[]{:S(2)}, u32[]{:S(2)}) collective-permute-start(f32[2,232,128]{2,1,0:T(8,128)S(1)} %pad_maximum_fusion.same.early), channel_id=1, source_target_pairs={{0,32},{32,0},{64,96},{96,64},{128,160},{160,128},{192,224},{224,1... | collective-permute-start | bytes 712712 | tf_op jit(solution)/shard_map/ppermute | solution.py:506
  66.7 0.0 collective-permute-done.8
  66.7 3.2 %collective-permute-done.9 = f32[232,128]{1,0:T(8,128)S(1)} collective-permute-done((f32[232,128]{1,0:T(8,128)S(1)}, f32[232,128]{1,0:T(8,128)S(1)}, u32[]{:S(2)}, u32[]{:S(2)}) %collective-permute-start.9) | collective-permute-done | bytes 118816 | tf_op jit(solution)/shard_map/ppermute | solution.py:477
  69.9 0.6 collective-permute-start.10
  70.4 0.0 collective-permute-done.7.other
  70.4 1.4 %early.1.begun = f32[1760,128]{1,0:T(8,128)} custom-call(s32[2]{0:T(128)S(1)} %pad_add_fusion.ids, f32[2,232,128]{2,1,0:T(8,128)S(1)} %pad_maximum_fusion.same.early, f32[2,232,128]{2,1,0:T(8,128)S(1)} %collective-permute-done.7.other), custom_call_target="tpu_custom_call" | custom-call | flops 1000000 | bytes 4000000 | tf_op jit(solution)/shard_map/early/pallas_call | solution.py:497
  71.8 0.0 collective-permute-done.10.other
  71.8 1.9 %late.1 = (f32[1760,128]{1,0:T(8,128)}, f32[1,1]{1,0:T(1,128)}) custom-call(s32[2]{0:T(128)S(1)} %pad_add_fusion.ids, f32[1760,128]{1,0:T(8,128)} %early.1.begun, f32[2,232,128]{2,1,0:T(8,128)S(1)} %pad_maximum_fusion.same.early, f32[2,232,128]{2,1,0:T(8,128)S(1)} %pad_maximum_fusion.1.same, ...), custom_call_target="tpu_custom_call", output_to_operand_aliasing={{0}: (1, {})} | custom-call | tf_op jit(solution)/shard_map/late/pallas_call | solution.py:508
  (8 shorter events, 0.1 us)
Async XLA Ops:
  3.2 16.4 %collective-permute-start.1 = (f32[64,1024]{1,0:T(8,128)}, f32[64,1024]{1,0:T(8,128)}, u32[]{:S(2)}, u32[]{:S(2)}) collective-permute-start(f32[64,1024]{1,0:T(8,128)} %get-tuple-element.22.tail), channel_id=1, source_target_pairs={{0,1},{1,2},{2,3},{3,4},{4,5},{5,6},{6,7},{7,8},{8,9},{9,10},{10,1... | collective-permute-start | bytes 786440 | tf_op jit(solution)/shard_map/ppermute | solution.py:416
  5.4 20.6 %collective-permute-start = (f32[64,1024]{1,0:T(8,128)}, f32[64,1024]{1,0:T(8,128)S(1)}, u32[]{:S(2)}, u32[]{:S(2)}) collective-permute-start(f32[64,1024]{1,0:T(8,128)} %get-tuple-element.21.head), channel_id=1, source_target_pairs={{1,0},{2,1},{3,2},{4,3},{5,4},{6,5},{7,6},{8,7},{9,8},{10,9},{11,1... | collective-permute-start | bytes 786440 | tf_op jit(solution)/shard_map/ppermute | solution.py:417
  10.5 15.4 %copy-start.11 = (f32[55,55]{1,0:T(8,128)S(1)}, f32[55,55]{1,0:T(8,128)}, u32[]{:S(2)}) copy-start(f32[55,55]{1,0:T(8,128)} %root.1) | copy-start | bytes 36304
  15.5 0.9 %copy-start.1 = (bf16[224,1920]{1,0:T(8,128)(2,1)}, bf16[224,1920]{1,0:T(8,128)(2,1)S(1)}, u32[]{:S(2)}) copy-start(bf16[224,1920]{1,0:T(8,128)(2,1)S(1)} %get-tuple-element.30.parts) | copy-start | bytes 2580484
  16.4 0.9 %copy-start.3 = (bf16[224,1920]{1,0:T(8,128)(2,1)}, bf16[224,1920]{1,0:T(8,128)(2,1)S(1)}, u32[]{:S(2)}) copy-start(bf16[224,1920]{1,0:T(8,128)(2,1)S(1)} %get-tuple-element.25.parts) | copy-start | bytes 2580484
  17.3 0.8 %copy-start.5 = (f32[56,2048]{1,0:T(8,128)}, f32[56,2048]{1,0:T(8,128)S(1)}, u32[]{:S(2)}) copy-start(f32[56,2048]{1,0:T(8,128)S(1)} %get-tuple-element.31.values) | copy-start | bytes 1376260
  18.1 0.7 copy-start.7
  18.8 0.7 copy-start.9
  19.6 6.4 %copy-start = (f32[1,2,55,2048]{3,1,2,0:T(2,128)S(1)}, f32[1,2,55,2048]{3,1,2,0:T(2,128)}, u32[]{:S(2)}) copy-start(f32[1,2,55,2048]{3,1,2,0:T(2,128)} %param.5) | copy-start | bytes 2703364
  19.6 6.4 %copy-start.2 = (bf16[224,1920]{1,0:T(8,128)(2,1)S(1)}, bf16[224,1920]{1,0:T(8,128)(2,1)}, u32[]{:S(2)}) copy-start(bf16[224,1920]{1,0:T(8,128)(2,1)} %copy-done.1) | copy-start | bytes 2580484
  19.6 1.3 %copy-start.4 = (bf16[224,1920]{1,0:T(8,128)(2,1)S(1)}, bf16[224,1920]{1,0:T(8,128)(2,1)}, u32[]{:S(2)}) copy-start(bf16[224,1920]{1,0:T(8,128)(2,1)} %copy-done.3) | copy-start | bytes 2580484
  20.9 0.9 %copy-start.10 = (f32[64,1024]{1,0:T(8,128)S(1)}, f32[64,1024]{1,0:T(8,128)}, u32[]{:S(2)}) copy-start(f32[64,1024]{1,0:T(8,128)} %copy-done.9) | copy-start | bytes 786436
  21.9 4.1 %copy-start.6 = (f32[56,2048]{1,0:T(8,128)S(1)}, f32[56,2048]{1,0:T(8,128)}, u32[]{:S(2)}) copy-start(f32[56,2048]{1,0:T(8,128)} %copy-done.5) | copy-start | bytes 1376260
  26.0 1.0 %copy-start.8 = (f32[64,1024]{1,0:T(8,128)S(1)}, f32[64,1024]{1,0:T(8,128)}, u32[]{:S(2)}) copy-start(f32[64,1024]{1,0:T(8,128)} %copy-done.7) | copy-start | bytes 786436
  31.0 4.0 %collective-permute-start.2 = (f32[904,128]{1,0:T(8,128)S(1)}, f32[904,128]{1,0:T(8,128)S(1)}, u32[]{:S(2)}, u32[]{:S(2)}) collective-permute-start(f32[904,128]{1,0:T(8,128)S(1)} %get-tuple-element.33), channel_id=1, source_target_pairs={{0,32},{32,0},{64,96},{96,64},{128,160},{160,128},{192,224},{224,1... | collective-permute-start | bytes 1388552 | tf_op jit(solution)/shard_map/ppermute | solution.py:481
  35.1 17.8 %collective-permute-start.5 = (f32[224,128]{1,0:T(8,128)S(1)}, f32[224,128]{1,0:T(8,128)S(1)}, u32[]{:S(2)}, u32[]{:S(2)}) collective-permute-start(f32[224,128]{1,0:T(8,128)S(1)} %get-tuple-element.40), channel_id=1, source_target_pairs={{0,192},{32,224},{64,0},{96,32},{128,64},{160,96},{192,128},{224,1... | collective-permute-start | bytes 344072 | tf_op jit(solution)/shard_map/ppermute | solution.py:477
  39.5 13.5 %collective-permute-start.4 = (f32[224,128]{1,0:T(8,128)S(1)}, f32[224,128]{1,0:T(8,128)S(1)}, u32[]{:S(2)}, u32[]{:S(2)}) collective-permute-start(f32[224,128]{1,0:T(8,128)S(1)} %get-tuple-element.41), channel_id=1, source_target_pairs={{0,128},{32,160},{64,192},{96,224},{128,0},{160,32},{192,64},{224,... | collective-permute-start | bytes 344072 | tf_op jit(solution)/shard_map/ppermute | solution.py:477
  40.5 12.5 %collective-permute-start.3 = (f32[224,128]{1,0:T(8,128)S(1)}, f32[224,128]{1,0:T(8,128)S(1)}, u32[]{:S(2)}, u32[]{:S(2)}) collective-permute-start(f32[224,128]{1,0:T(8,128)S(1)} %get-tuple-element.42), channel_id=1, source_target_pairs={{0,64},{32,96},{64,128},{96,160},{128,192},{160,224},{192,0},{224,... | collective-permute-start | bytes 344072 | tf_op jit(solution)/shard_map/ppermute | solution.py:477
  53.1 7.8 %collective-permute-start.6 = (f32[232,128]{1,0:T(8,128)S(1)}, f32[232,128]{1,0:T(8,128)S(1)}, u32[]{:S(2)}, u32[]{:S(2)}) collective-permute-start(f32[232,128]{1,0:T(8,128)S(1)} %get-tuple-element.44), channel_id=1, source_target_pairs={{0,128},{32,160},{64,192},{96,224},{128,0},{160,32},{192,64},{224,... | collective-permute-start | bytes 356360 | tf_op jit(solution)/shard_map/ppermute | solution.py:477
  56.7 10.0 %collective-permute-start.8 = (f32[232,128]{1,0:T(8,128)S(1)}, f32[232,128]{1,0:T(8,128)S(1)}, u32[]{:S(2)}, u32[]{:S(2)}) collective-permute-start(f32[232,128]{1,0:T(8,128)S(1)} %get-tuple-element.44), channel_id=1, source_target_pairs={{0,64},{32,96},{64,128},{96,160},{128,192},{160,224},{192,0},{224,... | collective-permute-start | bytes 356360 | tf_op jit(solution)/shard_map/ppermute | solution.py:477
  56.8 13.0 %collective-permute-start.9 = (f32[232,128]{1,0:T(8,128)S(1)}, f32[232,128]{1,0:T(8,128)S(1)}, u32[]{:S(2)}, u32[]{:S(2)}) collective-permute-start(f32[232,128]{1,0:T(8,128)S(1)} %get-tuple-element.44), channel_id=1, source_target_pairs={{0,192},{32,224},{64,0},{96,32},{128,64},{160,96},{192,128},{224,1... | collective-permute-start | bytes 356360 | tf_op jit(solution)/shard_map/ppermute | solution.py:477
  60.9 9.6 %collective-permute-start.7 = (f32[2,232,128]{2,1,0:T(8,128)S(1)}, f32[2,232,128]{2,1,0:T(8,128)S(1)}, u32[]{:S(2)}, u32[]{:S(2)}) collective-permute-start(f32[2,232,128]{2,1,0:T(8,128)S(1)} %pad_maximum_fusion.same.early), channel_id=1, source_target_pairs={{0,32},{32,0},{64,96},{96,64},{128,160},{160,128},{192,224},{224,1... | collective-permute-start | bytes 712712 | tf_op jit(solution)/shard_map/ppermute | solution.py:506
  69.9 1.9 %collective-permute-start.10 = (f32[2,232,128]{2,1,0:T(8,128)S(1)}, f32[2,232,128]{2,1,0:T(8,128)S(1)}, u32[]{:S(2)}, u32[]{:S(2)}) collective-permute-start(f32[2,232,128]{2,1,0:T(8,128)S(1)} %pad_maximum_fusion.1.same), channel_id=1, source_target_pairs={{0,32},{32,0},{64,96},{96,64},{128,160},{160,128},{192,224},{224,1... | collective-permute-start | bytes 712712 | tf_op jit(solution)/shard_map/ppermute | solution.py:520

commit v5 on v4

--- a/solution.py
+++ b/solution.py
@@ -143,8 +143,8 @@
 
 
 def interior_kernel(
-    head, tail, near_adj, far_adj, near_state, far_state, near_parts, far_parts, values,
-    adj, state, buf0, buf1, buf2, buf3,
+    head, tail, root, near_adj, far_adj, near_state, far_state, near_parts, far_parts,
+    near_values, far_values, near_square, far_square, adj, state, buf0, buf1, buf2, buf3, padded,
 ):
     bufs = (buf0, buf1, buf2, buf3)
     blocks = adj.shape[0]
@@ -167,7 +167,11 @@
         here = block * BLOCK
         state[0:56, here : here + BLOCK] = value[0:56]
         state[56:64, here : here + BLOCK] = jnp.broadcast_to(coeff, (8, BLOCK))
-        values[:, here : here + BLOCK] = value[0:56]
+        if block < half - 1:
+            near_values[:, here : here + BLOCK] = value[0:56]
+        else:
+            there = here - (half - 1) * BLOCK
+            far_values[:, there : there + BLOCK] = value[0:56]
         store_parts(buf0, here, split(value[0:56], coeff))
     for step in range(1, STEPS - 1):
         whole = interior_blocks(step, blocks)
@@ -177,6 +181,15 @@
             places.append((low * BLOCK + REACH, REACH, lambda: adj[low, REACH:, REACH:], False))
             places.append((high * BLOCK, REACH, lambda: adj[high, : BLOCK + REACH, :REACH], False))
         sweep(state, bufs[(step - 1) % 4], bufs[step % 4], (0, 0), places)
+    padded[...] = jnp.zeros(padded.shape, jnp.float32)
+    padded[0:LEVELS, 0:LEVELS] = root[...]
+    matrix = lax.dot_general(
+        padded[...], padded[...], (((1,), (1,)), ((), ())),
+        precision=lax.Precision.HIGHEST, preferred_element_type=jnp.float32,
+    )
+    matrix_high = matrix.astype(jnp.bfloat16)
+    matrix_low = (matrix - matrix_high.astype(jnp.float32)).astype(jnp.bfloat16)
+    near_square[...] = far_square[...] = jnp.concatenate([matrix_high, matrix_low], axis=0)
     near_state[...] = state[:, 0 : own // 2]
     far_state[...] = state[:, own // 2 :]
     for side, parts in ((0, near_parts), (1, far_parts)):
@@ -206,7 +219,15 @@
         bufs[step % 4][:, at + low : at + high] = parts[:, packed : packed + high - low]
 
 
-def left_kernel(left, inner, done, parts, state, seam, outer, buf0, buf1, buf2, buf3):
+def level_product(square, value):
+    high = value.astype(jnp.bfloat16)
+    low = (value - high.astype(jnp.float32)).astype(jnp.bfloat16)
+    first = jnp.dot(square[...], high, preferred_element_type=jnp.float32)
+    second = jnp.dot(square[0:64, :], low, preferred_element_type=jnp.float32)
+    return first[0:64] + (first[64:128] + second)
+
+
+def left_kernel(left, inner, done, parts, values, square, state, seam, outer, buf0, buf1, buf2, buf3):
     own = 2 * done.shape[1]
     bases = (0, -REACH)
     bufs = (buf0, buf1, buf2, buf3)
@@ -231,11 +252,19 @@
         sweep(state, bufs[(step - 1) % 4], bufs[step % 4] if step < STEPS else None, bases, places)
     low = (middle - 1) * BLOCK - REACH - bases[1]
     seam[...] = bufs[(STEPS - 1) % 4][:, low : low + BLOCK + REACH]
+    total = jnp.zeros((1, BLOCK), jnp.float32)
+    for block in range(own // BLOCK // 2 - 1):
+        here = slice(HALO + block * BLOCK, HALO + (block + 1) * BLOCK)
+        smoothed = level_product(square, state[:, here])
+        state[:, here] = smoothed
+        at = block * BLOCK
+        total = total + jnp.sum(values[0:LEVELS, at : at + BLOCK] * smoothed[0:LEVELS], axis=0, keepdims=True)
+    state[56:57, 0:BLOCK] = total
 
 
 def right_kernel(
-    ids, right, root, ens, west, seam, inner, done, parts, values,
-    keep, send, state, outer, buf0, buf1, buf2, buf3, square, rowed,
+    core, place, right, ens, west, seam, inner, done, parts, values, square,
+    keep, send, state, outer, buf0, buf1, buf2, buf3, rowed,
 ):
     own = 2 * done.shape[1]
     wide = own + 2 * HALO
@@ -269,26 +298,15 @@
             bufs[(step - 1) % 4][:, low : low + BLOCK + REACH] = seam[...]
         sweep(state, bufs[(step - 1) % 4], bufs[step % 4] if step < STEPS else None, bases, places)
 
-    square[...] = jnp.zeros(square.shape, jnp.float32)
-    square[0:LEVELS, 0:LEVELS] = root[...]
-    matrix = lax.dot_general(
-        square[...], square[...], (((1,), (1,)), ((), ())),
-        precision=lax.Precision.HIGHEST, preferred_element_type=jnp.float32,
-    )
-    matrix_high = matrix.astype(jnp.bfloat16)
-    matrix_low = (matrix - matrix_high.astype(jnp.float32)).astype(jnp.bfloat16)
-    stacked = jnp.concatenate([matrix_high, matrix_low], axis=0)
-    total = jnp.zeros((1, BLOCK), jnp.float32)
+    total = west[56:57, 0:BLOCK]
     for block in range(own // BLOCK):
         at = (fringe + block) * BLOCK
-        value = west[:, at : at + BLOCK] if at < bases[0] else state[:, at - bases[0] : at - bases[0] + BLOCK]
-        high = value.astype(jnp.bfloat16)
-        low = (value - high.astype(jnp.float32)).astype(jnp.bfloat16)
-        first = jnp.dot(stacked, high, preferred_element_type=jnp.float32)
-        second = jnp.dot(matrix_high, low, preferred_element_type=jnp.float32)
-        smoothed = first[0:LEVELS] + (first[64 : 64 + LEVELS] + second[0:LEVELS])
-        at = block * BLOCK
-        total = total + jnp.sum(values[0:LEVELS, at : at + BLOCK] * smoothed, axis=0, keepdims=True)
+        if at < bases[0]:
+            smoothed = west[0:LEVELS, at : at + BLOCK]
+        else:
+            smoothed = level_product(square, state[:, at - bases[0] : at - bases[0] + BLOCK])[0:LEVELS]
+            there = at - bases[0]
+            total = total + jnp.sum(values[0:LEVELS, there : there + BLOCK] * smoothed, axis=0, keepdims=True)
         for tile in range(BLOCK // LANES):
             spot = block * (BLOCK // LANES) + tile
             rowed[pl.ds(spot, LEVELS, stride=tiles), :] = smoothed[:, tile * LANES : (tile + 1) * LANES]
@@ -297,7 +315,7 @@
     spot = pl.ds(slots * chunk, 8)
     keep[spot, :] = send[spot, :] = jnp.broadcast_to(jnp.sum(total, axis=1, keepdims=True), (8, LANES))
 
-    mine, chip = ids[0], ids[1]
+    mine, chip = core[0], place[0]
     spare = slots * chunk - LEVELS * tiles
 
     def products(slot, start, first, count):
@@ -323,8 +341,8 @@
             send[pl.ds((slot + 1) * chunk - spare, spare), :] = nothing
 
 
-def place_pieces(ids, slots, same, other, out, lines, sems):
-    mine, chip = ids[0], ids[1]
+def place_pieces(core, place, slots, same, other, out, lines, sems):
+    mine, chip = core[0], place[0]
     chunk = lines.shape[0] // len(slots) // 2
     short = 2 * chunk - (4 * 2 * chunk - out.shape[0])
     waits = []
@@ -354,12 +372,12 @@
         pl.when(source < 3)(extra.wait)
 
 
-def early_kernel(ids, same, other, out, lines, sems):
-    wait_pieces(place_pieces(ids, EARLY, same, other, out, lines, sems))
-
-
-def late_kernel(scale, ids, begun, early, same, other, out, quadratic, lines, sems):
-    waits = place_pieces(ids, LATE, same, other, out, lines, sems)
+def early_kernel(core, place, same, other, out, lines, sems):
+    wait_pieces(place_pieces(core, place, EARLY, same, other, out, lines, sems))
+
+
+def late_kernel(scale, core, place, begun, early, same, other, out, quadratic, lines, sems):
+    waits = place_pieces(core, place, LATE, same, other, out, lines, sems)
     chunk = lines.shape[0] // len(LATE) // 2
     near, far = [
         pieces[0, chunk : chunk + 8, :] + pieces[1, chunk : chunk + 8, :] for pieces in (early, same)
@@ -388,7 +406,10 @@
     params = pltpu.CompilerParams(vmem_limit_bytes=32 * 1024 * 1024)
     place = (lax.axis_index("patch") * own).astype(jnp.int32).reshape(1)
     member = lax.axis_index("mem")
-    ids = jnp.stack([lax.rem(member, 2), member // 2]).astype(jnp.int32)
+    ids = [
+        jnp.bitwise_and(member, 1).astype(jnp.int32).reshape(1),
+        lax.shift_right_logical(member, 1).astype(jnp.int32).reshape(1),
+    ]
     ens_rows = interleave(ensemble[0])
     field_rows = interleave(field)
 
@@ -420,22 +441,26 @@
     adjacency = (2 * BLOCK, BLOCK)
     packed = jax.ShapeDtypeStruct((224, packed_columns(own)), jnp.bfloat16)
     half_state = jax.ShapeDtypeStruct((64, half), jnp.float32)
-    near_adj, far_adj, near_state, far_state, near_parts, far_parts, values = pl.pallas_call(
+    squared = jax.ShapeDtypeStruct((128, 64), jnp.bfloat16)
+    inside = pl.pallas_call(
         interior_kernel,
         out_shape=(
             jax.ShapeDtypeStruct((blocks // 2, *adjacency), jnp.bfloat16),
             jax.ShapeDtypeStruct((blocks // 2 + 1, *adjacency), jnp.bfloat16),
             half_state, half_state, packed, packed,
-            jax.ShapeDtypeStruct((56, own), jnp.float32),
+            jax.ShapeDtypeStruct((56, half - BLOCK), jnp.float32),
+            jax.ShapeDtypeStruct((56, half + BLOCK), jnp.float32),
+            squared, squared,
         ),
-        in_specs=[vmem] * 2,
-        out_specs=(vmem,) * 7,
+        in_specs=[vmem] * 3,
+        out_specs=(vmem,) * 10,
         scratch_shapes=[pltpu.VMEM((blocks, *adjacency), jnp.bfloat16), pltpu.VMEM((64, own), jnp.float32)]
-        + [pltpu.VMEM((224, own), jnp.bfloat16)] * 4,
+        + [pltpu.VMEM((224, own), jnp.bfloat16)] * 4
+        + [pltpu.VMEM((64, 64), jnp.float32)],
         compiler_params=params,
-        cost_estimate=pl.CostEstimate(flops=0, bytes_accessed=7_000_000, transcendentals=0),
+        cost_estimate=pl.CostEstimate(flops=4_000_000_000, bytes_accessed=4_000_000, transcendentals=0),
         name="interior",
-    )(head, tail)
+    )(head, tail, vertical_root)
 
     chunk = 56 * tiles // chips
     west, seam = pl.pallas_call(
@@ -444,33 +469,30 @@
             jax.ShapeDtypeStruct((64, HALO + half), jnp.float32),
             jax.ShapeDtypeStruct((224, BLOCK + REACH), jnp.bfloat16),
         ),
-        in_specs=[vmem] * 4,
+        in_specs=[vmem] * 6,
         out_specs=(vmem,) * 2,
         scratch_shapes=[pltpu.VMEM((HALO // BLOCK, 2 * BLOCK, BLOCK), jnp.bfloat16)]
         + [pltpu.VMEM((224, HALO + half + 2 * REACH), jnp.bfloat16)] * 4,
         compiler_params=params,
         cost_estimate=pl.CostEstimate(flops=0, bytes_accessed=7_000_000, transcendentals=0),
         name="left",
-    )(left, near_adj, near_state, near_parts)
+    )(left, *inside[0::2])
     terms = jax.ShapeDtypeStruct((chips * chunk + 8, LANES), jnp.float32)
     keep, send = pl.pallas_call(
         right_kernel,
         out_shape=(terms, terms),
-        in_specs=[smem] + [vmem] * 9,
+        in_specs=[smem] * 2 + [vmem] * 9,
         out_specs=(vmem, vmem),
         scratch_shapes=[
             pltpu.VMEM((64, BLOCK + half + HALO), jnp.float32),
             pltpu.VMEM((HALO // BLOCK, 2 * BLOCK, BLOCK), jnp.bfloat16),
         ]
         + [pltpu.VMEM((224, 2 * BLOCK + half + HALO + REACH), jnp.bfloat16)] * 4
-        + [
-            pltpu.VMEM((64, 64), jnp.float32),
-            pltpu.VMEM((56 * tiles, LANES), jnp.float32),
-        ],
+        + [pltpu.VMEM((56 * tiles, LANES), jnp.float32)],
         compiler_params=params,
         cost_estimate=pl.CostEstimate(flops=0, bytes_accessed=7_000_000, transcendentals=0),
         name="right",
-    )(ids, right, vertical_root, ens_rows, west, seam, far_adj, far_state, far_parts, values)
+    )(*ids, right, ens_rows, west, seam, *inside[1::2])
 
     def shift_chips(array, by):
         pairs = [(2 * z + c, 2 * ((z + by) % chips) + c) for z in range(chips) for c in range(2)]
@@ -497,13 +519,13 @@
     rows = pl.pallas_call(
         early_kernel,
         out_shape=jax.ShapeDtypeStruct(field_rows.shape, jnp.float32),
-        in_specs=[smem, vmem, vmem],
+        in_specs=[smem, smem, vmem, vmem],
         out_specs=hbm,
         scratch_shapes=scratch,
         compiler_params=params,
         cost_estimate=pl.CostEstimate(flops=1_000_000, bytes_accessed=4_000_000, transcendentals=0),
         name="early",
-    )(ids, early, lax.ppermute(early, "mem", twin))
+    )(*ids, early, lax.ppermute(early, "mem", twin))
     late = jnp.stack([sources[by] for by in LATE])
     rows, quadratic = pl.pallas_call(
         functools.partial(late_kernel, scale),
@@ -511,13 +533,13 @@
             jax.ShapeDtypeStruct(field_rows.shape, jnp.float32),
             jax.ShapeDtypeStruct((1, 1), jnp.float32),
         ),
-        in_specs=[smem, hbm, vmem, vmem, vmem],
+        in_specs=[smem, smem, hbm, vmem, vmem, vmem],
         out_specs=(hbm, smem),
         scratch_shapes=scratch,
-        input_output_aliases={1: 0},
+        input_output_aliases={2: 0},
         compiler_params=params,
         name="late",
-    )(ids, rows, early, late, lax.ppermute(late, "mem", twin))
+    )(*ids, rows, early, late, lax.ppermute(late, "mem", twin))
     product = rows.reshape(LEVELS, tiles, 2, LANES).transpose(2, 0, 1, 3).reshape(field.shape)
     return (product, quadratic.reshape(()))
 

time: 74.1 us -> 65.3 us (0.88)
  local copies, waits for them, and re-layouts: 7.27 us -> 0.05 us
  Pallas kernels: 18.9 us -> 14.8 us
  starting transfers between devices: 31 us -> 33.3 us
    unnamed x24 -> x4, local copies, waits for them, and re-layouts: 7.23 us -> 0.01 us
    ppermute x1, starting transfers between devices: 5.77 us -> 7.07 us  [on_device(): lax.ppermute(early, 'mem', twin)]
    ppermute x6, waiting for transfers between devices: 3.76 us -> 2.58 us  [shift_chips(): return lax.ppermute(array, 'mem', pairs)]
    pallas_call x1, Pallas kernels: 4.96 us -> 3.93 us  [on_device(): pl.pallas_call(interior_kernel, out_shape=(jax.ShapeDtypeStruct((blocks /...]
    pallas_call x1, Pallas kernels: 2.6 us -> 1.8 us  [on_device(): pl.pallas_call(functools.partial(prepare_kernel, all_cells), out_shape=(s...]
  transfers between devices with their start and end apart: 11 -> 11, of which waited for: 3 -> 5; matrix products, arithmetic and copies ran while one was open for 0% -> 0% of each run, Pallas kernels for 14% -> 12%
where the time goes in v5:
time: 65.3 us; the launch traced here: 65.1 us
  starting transfers between devices  33.3 us (51%)
  Pallas kernels  14.8 us (23%)
  blocking collectives  10.9 us (17%)
  waiting for transfers between devices  4.98 us (8%)
  between operations  0.91 us (1%)
    ppermute x6, starting transfers between devices, shift_chips(): return lax.ppermute(array, 'mem', pairs)  15.3 us
    all_to_all x1, blocking collectives, on_device(): spread = lax.all_to_all(spread, 'patch', 0, 0)  10.9 us
    ppermute x1, starting transfers between devices, on_device(): lax.ppermute(early, 'mem', twin)  7.07 us
    ppermute x1, starting transfers between devices, on_device(): lax.ppermute(head, 'patch', [((i + 1) % patches, i) for i in range(patche...  5.16 us
    pallas_call x1, Pallas kernels, on_device(): pl.pallas_call(interior_kernel, out_shape=(jax.ShapeDtypeStruct((blocks /...  3.93 us
    pallas_call x1, Pallas kernels, on_device(): pl.pallas_call(right_kernel, out_shape=(terms, terms), in_specs=[smem] *...  3.57 us
    pallas_call x1, Pallas kernels, on_device(): pl.pallas_call(left_kernel, out_shape=(jax.ShapeDtypeStruct((64, HALO + h...  3.35 us
    ppermute x1, starting transfers between devices, on_device(): pair_sum = keep + lax.ppermute(send, 'mem', twin)  3 us
  transfers between devices with their start and end apart: 11, of which 5 were waited for; matrix products, arithmetic and copies ran while one was open for 0% of the time, Pallas kernels for 12%

profile of v5, /device:TPU:1, one launch (start us, length us, event | category | flops | bytes accessed | tf_op | source)
XLA Modules:
  0.0 65.1 jit_solution(14972724840334790300)
XLA Ops:
  0.6 0.0 copy-start.1
  0.6 1.8 %prepare.1 = (f32[64,1024]{1,0:T(8,128)S(1)}, f32[64,1024]{1,0:T(8,128)S(1)}) custom-call(s32[1]{0:T(128)} %bitcast.2.place, f32[1760,128]{1,0:T(8,128)} %bitcast.27, f32[1760,128]{1,0:T(8,128)} %bitcast.30, f32[1,2048]{1,0:T(1,128)} %bitcast.34, s32[7,2048]{1,0:T(8,128)} %neigh.1), custom_call_target="tpu_custom_call" | custom-call | tf_op jit(solution)/shard_map/prepare/pallas_call | solution.py:421
  2.5 2.1 %collective-permute-start.1 = (f32[64,1024]{1,0:T(8,128)S(1)}, f32[64,1024]{1,0:T(8,128)S(1)}, u32[]{:S(2)}, u32[]{:S(2)}) collective-permute-start(f32[64,1024]{1,0:T(8,128)S(1)} %get-tuple-element.25.tail), channel_id=1, source_target_pairs={{0,1},{1,2},{2,3},{3,4},{4,5},{5,6},{6,7},{7,8},{8,9},{9,10},{10,1... | collective-permute-start | bytes 786440 | tf_op jit(solution)/shard_map/ppermute | solution.py:437
  4.6 5.2 %collective-permute-start = (f32[64,1024]{1,0:T(8,128)S(1)}, f32[64,1024]{1,0:T(8,128)S(1)}, u32[]{:S(2)}, u32[]{:S(2)}) collective-permute-start(f32[64,1024]{1,0:T(8,128)S(1)} %get-tuple-element.24.head), channel_id=1, source_target_pairs={{1,0},{2,1},{3,2},{4,3},{5,4},{6,5},{7,6},{8,7},{9,8},{10,9},{11,1... | collective-permute-start | bytes 786440 | tf_op jit(solution)/shard_map/ppermute | solution.py:438
  9.7 0.0 copy-done.1
  9.7 3.9 %interior.1 = (bf16[4,512,256]{2,1,0:T(8,128)(2,1)S(1)}, bf16[5,512,256]{2,1,0:T(8,128)(2,1)S(1)}, f32[64,1024]{1,0:T(8,128)S(1)}, f32[64,1024]{1,0:T(8,128)S(1)...) custom-call(f32[64,1024]{1,0:T(8,128)S(1)} %get-tuple-element.24.hea, ...), custom_call_target="tpu_custom_call" | custom-call | flops 4000000000 | bytes 4000000 | tf_op jit(solution)/shard_map/interior/pallas_call | solution.py:445
  13.7 0.5 collective-permute-done.1.left
  14.2 0.0 copy-start
  14.2 3.3 %left.1 = (f32[64,2048]{1,0:T(8,128)S(1)}, bf16[224,384]{1,0:T(8,128)(2,1)S(1)}) custom-call(f32[64,1024]{1,0:T(8,128)S(1)} %collective-permute-done.1.left, bf16[4,512,256]{2,1,0:T(8,128)(2,1)S(1)} %get-tuple-element.26.inner, f32[64,1024]{1,0:T(8,128)S(1)} %get-tuple-element.27.done, bf16[224,1920]{1,0:T(8,128)(2,1)S(1)} %get-tuple-element.28.parts, ...), custom_call_target="tpu_custom_call" | custom-call | bytes 7000000 | tf_op jit(solution)/shard_map/left/pallas_call | solution.py:466
  17.5 0.0 collective-permute-done.right
  17.5 0.0 copy-done
  17.6 3.6 %right.1 = (f32[904,128]{1,0:T(8,128)S(1)}, f32[904,128]{1,0:T(8,128)S(1)}) custom-call(s32[1]{0:T(128)} %bitcast.core, s32[1]{0:T(128)} %bitcast.1.place, f32[64,1024]{1,0:T(8,128)S(1)} %collective-permute-done.right, f32[1760,128]{1,0:T(8,128)S(1)} %bitcast.28, f32[64,2048]{1,0:T(8,128)S(1)} %get-tuple-element.31.west, ...), custom_call_target="tpu_custom_call" | custom-call | bytes 7000000 | tf_op jit(solution)/shard_map/right/pallas_call | solution.py:481
  21.1 3.0 %collective-permute-start.2 = (f32[904,128]{1,0:T(8,128)S(1)}, f32[904,128]{1,0:T(8,128)S(1)}, u32[]{:S(2)}, u32[]{:S(2)}) collective-permute-start(f32[904,128]{1,0:T(8,128)S(1)} %get-tuple-element.39), channel_id=1, source_target_pairs={{0,32},{32,0},{64,96},{96,64},{128,160},{160,128},{192,224},{224,1... | collective-permute-start | bytes 1388552 | tf_op jit(solution)/shard_map/ppermute | solution.py:503
  24.1 1.4 %collective-permute-done.2 = f32[904,128]{1,0:T(8,128)S(1)} collective-permute-done((f32[904,128]{1,0:T(8,128)S(1)}, f32[904,128]{1,0:T(8,128)S(1)}, u32[]{:S(2)}, u32[]{:S(2)}) %collective-permute-start.2) | collective-permute-done | bytes 462880 | tf_op jit(solution)/shard_map/ppermute | solution.py:503
  25.6 0.1 add.12
  25.7 3.1 %collective-permute-start.3 = (f32[224,128]{1,0:T(8,128)S(1)}, f32[224,128]{1,0:T(8,128)S(1)}, u32[]{:S(2)}, u32[]{:S(2)}) collective-permute-start(f32[224,128]{1,0:T(8,128)S(1)} %get-tuple-element.48), channel_id=1, source_target_pairs={{0,64},{32,96},{64,128},{96,160},{128,192},{160,224},{192,0},{224,... | collective-permute-start | bytes 344072 | tf_op jit(solution)/shard_map/ppermute | solution.py:499
  28.7 4.5 %collective-permute-start.4 = (f32[224,128]{1,0:T(8,128)S(1)}, f32[224,128]{1,0:T(8,128)S(1)}, u32[]{:S(2)}, u32[]{:S(2)}) collective-permute-start(f32[224,128]{1,0:T(8,128)S(1)} %get-tuple-element.47), channel_id=1, source_target_pairs={{0,128},{32,160},{64,192},{96,224},{128,0},{160,32},{192,64},{224,... | collective-permute-start | bytes 344072 | tf_op jit(solution)/shard_map/ppermute | solution.py:499
  33.3 2.4 %collective-permute-start.5 = (f32[224,128]{1,0:T(8,128)S(1)}, f32[224,128]{1,0:T(8,128)S(1)}, u32[]{:S(2)}, u32[]{:S(2)}) collective-permute-start(f32[224,128]{1,0:T(8,128)S(1)} %get-tuple-element.46), channel_id=1, source_target_pairs={{0,192},{32,224},{64,0},{96,32},{128,64},{160,96},{192,128},{224,1... | collective-permute-start | bytes 344072 | tf_op jit(solution)/shard_map/ppermute | solution.py:499
  35.7 10.9 %all_to_all.5 = f32[32,1,128]{2,1,0:T(1,128)S(1)} all-to-all(f32[32,1,128]{2,1,0:T(1,128)S(1)} %broadcast_in_dim.14), channel_id=1, replica_groups=mesh['mem'=8,'patch'=32] {'patch'}, dimensions={0} | all-to-all | bytes 32768 | tf_op jit(solution)/shard_map/all_to_all | solution.py:507
  46.5 0.0 collective-permute-done.3
  46.5 0.0 collective-permute-done.4
  46.6 0.0 collective-permute-done.5
  46.6 0.1 reduce_sum.9
  46.7 1.8 %collective-permute-start.6 = (f32[232,128]{1,0:T(8,128)S(1)}, f32[232,128]{1,0:T(8,128)S(1)}, u32[]{:S(2)}, u32[]{:S(2)}) collective-permute-start(f32[232,128]{1,0:T(8,128)S(1)} %get-tuple-element.50), channel_id=1, source_target_pairs={{0,128},{32,160},{64,192},{96,224},{128,0},{160,32},{192,64},{224,... | collective-permute-start | bytes 356360 | tf_op jit(solution)/shard_map/ppermute | solution.py:499
  48.5 1.9 %collective-permute-start.8 = (f32[232,128]{1,0:T(8,128)S(1)}, f32[232,128]{1,0:T(8,128)S(1)}, u32[]{:S(2)}, u32[]{:S(2)}) collective-permute-start(f32[232,128]{1,0:T(8,128)S(1)} %get-tuple-element.50), channel_id=1, source_target_pairs={{0,64},{32,96},{64,128},{96,160},{128,192},{160,224},{192,0},{224,... | collective-permute-start | bytes 356360 | tf_op jit(solution)/shard_map/ppermute | solution.py:499
  50.4 1.7 %collective-permute-start.9 = (f32[232,128]{1,0:T(8,128)S(1)}, f32[232,128]{1,0:T(8,128)S(1)}, u32[]{:S(2)}, u32[]{:S(2)}) collective-permute-start(f32[232,128]{1,0:T(8,128)S(1)} %get-tuple-element.50), channel_id=1, source_target_pairs={{0,192},{32,224},{64,0},{96,32},{128,64},{160,96},{192,128},{224,1... | collective-permute-start | bytes 356360 | tf_op jit(solution)/shard_map/ppermute | solution.py:499
  52.1 2.5 %collective-permute-done.6 = f32[232,128]{1,0:T(8,128)S(1)} collective-permute-done((f32[232,128]{1,0:T(8,128)S(1)}, f32[232,128]{1,0:T(8,128)S(1)}, u32[]{:S(2)}, u32[]{:S(2)}) %collective-permute-start.6) | collective-permute-done | bytes 118816 | tf_op jit(solution)/shard_map/ppermute | solution.py:499
  54.6 7.1 %collective-permute-start.7 = (f32[2,232,128]{2,1,0:T(8,128)S(1)}, f32[2,232,128]{2,1,0:T(8,128)S(1)}, u32[]{:S(2)}, u32[]{:S(2)}) collective-permute-start(f32[2,232,128]{2,1,0:T(8,128)S(1)} %pad_maximum_fusion.same.early), channel_id=1, source_target_pairs={{0,32},{32,0},{64,96},{96,64},{128,160},{160,128},{192,224},{224,1... | collective-permute-start | bytes 712712 | tf_op jit(solution)/shard_map/ppermute | solution.py:528
  61.7 0.0 collective-permute-done.8
  61.7 0.1 collective-permute-done.9
  61.8 0.6 collective-permute-start.10
  62.4 0.4 collective-permute-done.7.other
  62.8 0.8 %early.1.begun = f32[1760,128]{1,0:T(8,128)} custom-call(s32[1]{0:T(128)} %bitcast.core, s32[1]{0:T(128)} %bitcast.1.place, f32[2,232,128]{2,1,0:T(8,128)S(1)} %pad_maximum_fusion.same.early, f32[2,232,128]{2,1,0:T(8,128)S(1)} %collective-permute-done.7.other), custom_call_target="tpu_custom_call" | custom-call | flops 1000000 | bytes 4000000 | tf_op jit(solution)/shard_map/early/pallas_call | solution.py:519
  63.6 0.0 collective-permute-done.10.other
  63.6 1.3 %late.1 = (f32[1760,128]{1,0:T(8,128)}, f32[1,1]{1,0:T(1,128)}) custom-call(s32[1]{0:T(128)} %bitcast.core, s32[1]{0:T(128)} %bitcast.1.place, f32[1760,128]{1,0:T(8,128)} %early.1.begun, f32[2,232,128]{2,1,0:T(8,128)S(1)} %pad_maximum_fusion.same.early, f32[2,232,128]{2,1,0:T(8,128)S(1)} %pad_maximum_fusion.1.same, ...), custom_call_target="tpu_custom_call", output_to_operand_aliasing={{0}: (2, {})} | custom-call | tf_op jit(solution)/shard_map/late/pallas_call | solution.py:530
  (8 shorter events, 0.2 us)
Async XLA Ops:
  0.6 9.1 %copy-start.1 = (f32[55,55]{1,0:T(8,128)S(1)}, f32[55,55]{1,0:T(8,128)}, u32[]{:S(2)}) copy-start(f32[55,55]{1,0:T(8,128)} %root.1) | copy-start | bytes 36304
  2.5 11.7 %collective-permute-start.1 = (f32[64,1024]{1,0:T(8,128)S(1)}, f32[64,1024]{1,0:T(8,128)S(1)}, u32[]{:S(2)}, u32[]{:S(2)}) collective-permute-start(f32[64,1024]{1,0:T(8,128)S(1)} %get-tuple-element.25.tail), channel_id=1, source_target_pairs={{0,1},{1,2},{2,3},{3,4},{4,5},{5,6},{6,7},{7,8},{8,9},{9,10},{10,1... | collective-permute-start | bytes 786440 | tf_op jit(solution)/shard_map/ppermute | solution.py:437
  4.6 13.0 %collective-permute-start = (f32[64,1024]{1,0:T(8,128)S(1)}, f32[64,1024]{1,0:T(8,128)S(1)}, u32[]{:S(2)}, u32[]{:S(2)}) collective-permute-start(f32[64,1024]{1,0:T(8,128)S(1)} %get-tuple-element.24.head), channel_id=1, source_target_pairs={{1,0},{2,1},{3,2},{4,3},{5,4},{6,5},{7,6},{8,7},{9,8},{10,9},{11,1... | collective-permute-start | bytes 786440 | tf_op jit(solution)/shard_map/ppermute | solution.py:438
  14.2 3.4 %copy-start = (f32[1,2,55,2048]{3,1,2,0:T(2,128)S(1)}, f32[1,2,55,2048]{3,1,2,0:T(2,128)}, u32[]{:S(2)}) copy-start(f32[1,2,55,2048]{3,1,2,0:T(2,128)} %param.5) | copy-start | bytes 2703364
  21.1 4.5 %collective-permute-start.2 = (f32[904,128]{1,0:T(8,128)S(1)}, f32[904,128]{1,0:T(8,128)S(1)}, u32[]{:S(2)}, u32[]{:S(2)}) collective-permute-start(f32[904,128]{1,0:T(8,128)S(1)} %get-tuple-element.39), channel_id=1, source_target_pairs={{0,32},{32,0},{64,96},{96,64},{128,160},{160,128},{192,224},{224,1... | collective-permute-start | bytes 1388552 | tf_op jit(solution)/shard_map/ppermute | solution.py:503
  25.7 20.9 %collective-permute-start.3 = (f32[224,128]{1,0:T(8,128)S(1)}, f32[224,128]{1,0:T(8,128)S(1)}, u32[]{:S(2)}, u32[]{:S(2)}) collective-permute-start(f32[224,128]{1,0:T(8,128)S(1)} %get-tuple-element.48), channel_id=1, source_target_pairs={{0,64},{32,96},{64,128},{96,160},{128,192},{160,224},{192,0},{224,... | collective-permute-start | bytes 344072 | tf_op jit(solution)/shard_map/ppermute | solution.py:499
  28.7 17.8 %collective-permute-start.4 = (f32[224,128]{1,0:T(8,128)S(1)}, f32[224,128]{1,0:T(8,128)S(1)}, u32[]{:S(2)}, u32[]{:S(2)}) collective-permute-start(f32[224,128]{1,0:T(8,128)S(1)} %get-tuple-element.47), channel_id=1, source_target_pairs={{0,128},{32,160},{64,192},{96,224},{128,0},{160,32},{192,64},{224,... | collective-permute-start | bytes 344072 | tf_op jit(solution)/shard_map/ppermute | solution.py:499
  33.3 13.3 %collective-permute-start.5 = (f32[224,128]{1,0:T(8,128)S(1)}, f32[224,128]{1,0:T(8,128)S(1)}, u32[]{:S(2)}, u32[]{:S(2)}) collective-permute-start(f32[224,128]{1,0:T(8,128)S(1)} %get-tuple-element.46), channel_id=1, source_target_pairs={{0,192},{32,224},{64,0},{96,32},{128,64},{160,96},{192,128},{224,1... | collective-permute-start | bytes 344072 | tf_op jit(solution)/shard_map/ppermute | solution.py:499
  46.7 7.9 %collective-permute-start.6 = (f32[232,128]{1,0:T(8,128)S(1)}, f32[232,128]{1,0:T(8,128)S(1)}, u32[]{:S(2)}, u32[]{:S(2)}) collective-permute-start(f32[232,128]{1,0:T(8,128)S(1)} %get-tuple-element.50), channel_id=1, source_target_pairs={{0,128},{32,160},{64,192},{96,224},{128,0},{160,32},{192,64},{224,... | collective-permute-start | bytes 356360 | tf_op jit(solution)/shard_map/ppermute | solution.py:499
  48.5 13.2 %collective-permute-start.8 = (f32[232,128]{1,0:T(8,128)S(1)}, f32[232,128]{1,0:T(8,128)S(1)}, u32[]{:S(2)}, u32[]{:S(2)}) collective-permute-start(f32[232,128]{1,0:T(8,128)S(1)} %get-tuple-element.50), channel_id=1, source_target_pairs={{0,64},{32,96},{64,128},{96,160},{128,192},{160,224},{192,0},{224,... | collective-permute-start | bytes 356360 | tf_op jit(solution)/shard_map/ppermute | solution.py:499
  50.4 11.4 %collective-permute-start.9 = (f32[232,128]{1,0:T(8,128)S(1)}, f32[232,128]{1,0:T(8,128)S(1)}, u32[]{:S(2)}, u32[]{:S(2)}) collective-permute-start(f32[232,128]{1,0:T(8,128)S(1)} %get-tuple-element.50), channel_id=1, source_target_pairs={{0,192},{32,224},{64,0},{96,32},{128,64},{160,96},{192,128},{224,1... | collective-permute-start | bytes 356360 | tf_op jit(solution)/shard_map/ppermute | solution.py:499
  54.6 8.2 %collective-permute-start.7 = (f32[2,232,128]{2,1,0:T(8,128)S(1)}, f32[2,232,128]{2,1,0:T(8,128)S(1)}, u32[]{:S(2)}, u32[]{:S(2)}) collective-permute-start(f32[2,232,128]{2,1,0:T(8,128)S(1)} %pad_maximum_fusion.same.early), channel_id=1, source_target_pairs={{0,32},{32,0},{64,96},{96,64},{128,160},{160,128},{192,224},{224,1... | collective-permute-start | bytes 712712 | tf_op jit(solution)/shard_map/ppermute | solution.py:528
  61.8 1.8 %collective-permute-start.10 = (f32[2,232,128]{2,1,0:T(8,128)S(1)}, f32[2,232,128]{2,1,0:T(8,128)S(1)}, u32[]{:S(2)}, u32[]{:S(2)}) collective-permute-start(f32[2,232,128]{2,1,0:T(8,128)S(1)} %pad_maximum_fusion.1.same), channel_id=1, source_target_pairs={{0,32},{32,0},{64,96},{96,64},{128,160},{160,128},{192,224},{224,1... | collective-permute-start | bytes 712712 | tf_op jit(solution)/shard_map/ppermute | solution.py:542

commit v6 on v5

--- a/solution.py
+++ b/solution.py
@@ -372,18 +372,18 @@
         pl.when(source < 3)(extra.wait)
 
 
-def early_kernel(core, place, same, other, out, lines, sems):
-    wait_pieces(place_pieces(core, place, EARLY, same, other, out, lines, sems))
-
-
-def late_kernel(scale, core, place, begun, early, same, other, out, quadratic, lines, sems):
-    waits = place_pieces(core, place, LATE, same, other, out, lines, sems)
-    chunk = lines.shape[0] // len(LATE) // 2
+def early_kernel(scale, core, place, same, other, late, out, quadratic, lines, sems):
+    waits = place_pieces(core, place, EARLY, same, other, out, lines, sems)
+    chunk = lines.shape[0] // len(EARLY) // 2
     near, far = [
-        pieces[0, chunk : chunk + 8, :] + pieces[1, chunk : chunk + 8, :] for pieces in (early, same)
+        pieces[0, chunk : chunk + 8, :] + pieces[1, chunk : chunk + 8, :] for pieces in (same, late)
     ]
     quadratic[0, 0] = jnp.max(near + far) * scale
     wait_pieces(waits)
+
+
+def late_kernel(core, place, begun, same, other, out, lines, sems):
+    wait_pieces(place_pieces(core, place, LATE, same, other, out, lines, sems))
 
 
 def interleave(array):
@@ -516,30 +516,30 @@
         pltpu.SemaphoreType.DMA((2, 2)),
     ]
     early = jnp.stack([sources[by] for by in EARLY])
-    rows = pl.pallas_call(
-        early_kernel,
-        out_shape=jax.ShapeDtypeStruct(field_rows.shape, jnp.float32),
-        in_specs=[smem, smem, vmem, vmem],
-        out_specs=hbm,
+    late = jnp.stack([sources[by] for by in LATE])
+    rows, quadratic = pl.pallas_call(
+        functools.partial(early_kernel, scale),
+        out_shape=(
+            jax.ShapeDtypeStruct(field_rows.shape, jnp.float32),
+            jax.ShapeDtypeStruct((1, 1), jnp.float32),
+        ),
+        in_specs=[smem, smem, vmem, vmem, vmem],
+        out_specs=(hbm, smem),
         scratch_shapes=scratch,
         compiler_params=params,
         cost_estimate=pl.CostEstimate(flops=1_000_000, bytes_accessed=4_000_000, transcendentals=0),
         name="early",
-    )(*ids, early, lax.ppermute(early, "mem", twin))
-    late = jnp.stack([sources[by] for by in LATE])
-    rows, quadratic = pl.pallas_call(
-        functools.partial(late_kernel, scale),
-        out_shape=(
-            jax.ShapeDtypeStruct(field_rows.shape, jnp.float32),
-            jax.ShapeDtypeStruct((1, 1), jnp.float32),
-        ),
-        in_specs=[smem, smem, hbm, vmem, vmem, vmem],
-        out_specs=(hbm, smem),
+    )(*ids, early, lax.ppermute(early, "mem", twin), late)
+    rows = pl.pallas_call(
+        late_kernel,
+        out_shape=jax.ShapeDtypeStruct(field_rows.shape, jnp.float32),
+        in_specs=[smem, smem, hbm, vmem, vmem],
+        out_specs=hbm,
         scratch_shapes=scratch,
         input_output_aliases={2: 0},
         compiler_params=params,
         name="late",
-    )(*ids, rows, early, late, lax.ppermute(late, "mem", twin))
+    )(*ids, rows, late, lax.ppermute(late, "mem", twin))
     product = rows.reshape(LEVELS, tiles, 2, LANES).transpose(2, 0, 1, 3).reshape(field.shape)
     return (product, quadratic.reshape(()))
 

time: 65.3 us -> 65.3 us (level)
  transfers between devices with their start and end apart: 11 -> 11, of which waited for: 5 -> 5; matrix products, arithmetic and copies ran while one was open for 0% -> 0% of each run, Pallas kernels for 12% -> 13%
where the time goes in v6:
time: 65.3 us; the launch traced here: 65.1 us
  starting transfers between devices  33.3 us (51%)
  Pallas kernels  14.8 us (23%)
  blocking collectives  10.9 us (17%)
  waiting for transfers between devices  4.98 us (8%)
  between operations  0.91 us (1%)
    ppermute x6, starting transfers between devices, shift_chips(): return lax.ppermute(array, 'mem', pairs)  15.3 us
    all_to_all x1, blocking collectives, on_device(): spread = lax.all_to_all(spread, 'patch', 0, 0)  10.9 us
    ppermute x1, starting transfers between devices, on_device(): lax.ppermute(early, 'mem', twin)  7.08 us
    ppermute x1, starting transfers between devices, on_device(): lax.ppermute(head, 'patch', [((i + 1) % patches, i) for i in range(patche...  5.16 us
    pallas_call x1, Pallas kernels, on_device(): pl.pallas_call(interior_kernel, out_shape=(jax.ShapeDtypeStruct((blocks /...  3.93 us
    pallas_call x1, Pallas kernels, on_device(): pl.pallas_call(right_kernel, out_shape=(terms, terms), in_specs=[smem] *...  3.57 us
    pallas_call x1, Pallas kernels, on_device(): pl.pallas_call(left_kernel, out_shape=(jax.ShapeDtypeStruct((64, HALO + h...  3.35 us
    ppermute x1, starting transfers between devices, on_device(): pair_sum = keep + lax.ppermute(send, 'mem', twin)  3 us
  transfers between devices with their start and end apart: 11, of which 5 were waited for; matrix products, arithmetic and copies ran while one was open for 0% of the time, Pallas kernels for 13%

profile of v6, /device:TPU:1, one launch (start us, length us, event | category | flops | bytes accessed | tf_op | source)
XLA Modules:
  0.0 65.1 jit_solution(2293738073012526774)
XLA Ops:
  0.6 0.0 copy-start.1
  0.6 1.8 %prepare.1 = (f32[64,1024]{1,0:T(8,128)S(1)}, f32[64,1024]{1,0:T(8,128)S(1)}) custom-call(s32[1]{0:T(128)} %bitcast.2.place, f32[1760,128]{1,0:T(8,128)} %bitcast.27, f32[1760,128]{1,0:T(8,128)} %bitcast.29, f32[1,2048]{1,0:T(1,128)} %bitcast.34, s32[7,2048]{1,0:T(8,128)} %neigh.1), custom_call_target="tpu_custom_call" | custom-call | tf_op jit(solution)/shard_map/prepare/pallas_call | solution.py:421
  2.5 2.1 %collective-permute-start.1 = (f32[64,1024]{1,0:T(8,128)S(1)}, f32[64,1024]{1,0:T(8,128)S(1)}, u32[]{:S(2)}, u32[]{:S(2)}) collective-permute-start(f32[64,1024]{1,0:T(8,128)S(1)} %get-tuple-element.25.tail), channel_id=1, source_target_pairs={{0,1},{1,2},{2,3},{3,4},{4,5},{5,6},{6,7},{7,8},{8,9},{9,10},{10,1... | collective-permute-start | bytes 786440 | tf_op jit(solution)/shard_map/ppermute | solution.py:437
  4.6 5.2 %collective-permute-start = (f32[64,1024]{1,0:T(8,128)S(1)}, f32[64,1024]{1,0:T(8,128)S(1)}, u32[]{:S(2)}, u32[]{:S(2)}) collective-permute-start(f32[64,1024]{1,0:T(8,128)S(1)} %get-tuple-element.24.head), channel_id=1, source_target_pairs={{1,0},{2,1},{3,2},{4,3},{5,4},{6,5},{7,6},{8,7},{9,8},{10,9},{11,1... | collective-permute-start | bytes 786440 | tf_op jit(solution)/shard_map/ppermute | solution.py:438
  9.7 0.0 copy-done.1
  9.7 3.9 %interior.1 = (bf16[4,512,256]{2,1,0:T(8,128)(2,1)S(1)}, bf16[5,512,256]{2,1,0:T(8,128)(2,1)S(1)}, f32[64,1024]{1,0:T(8,128)S(1)}, f32[64,1024]{1,0:T(8,128)S(1)...) custom-call(f32[64,1024]{1,0:T(8,128)S(1)} %get-tuple-element.24.hea, ...), custom_call_target="tpu_custom_call" | custom-call | flops 4000000000 | bytes 4000000 | tf_op jit(solution)/shard_map/interior/pallas_call | solution.py:445
  13.7 0.5 collective-permute-done.1.left
  14.2 0.0 copy-start
  14.2 3.3 %left.1 = (f32[64,2048]{1,0:T(8,128)S(1)}, bf16[224,384]{1,0:T(8,128)(2,1)S(1)}) custom-call(f32[64,1024]{1,0:T(8,128)S(1)} %collective-permute-done.1.left, bf16[4,512,256]{2,1,0:T(8,128)(2,1)S(1)} %get-tuple-element.26.inner, f32[64,1024]{1,0:T(8,128)S(1)} %get-tuple-element.27.done, bf16[224,1920]{1,0:T(8,128)(2,1)S(1)} %get-tuple-element.28.parts, ...), custom_call_target="tpu_custom_call" | custom-call | bytes 7000000 | tf_op jit(solution)/shard_map/left/pallas_call | solution.py:466
  17.5 0.0 collective-permute-done.right
  17.5 0.0 copy-done
  17.6 3.6 %right.1 = (f32[904,128]{1,0:T(8,128)S(1)}, f32[904,128]{1,0:T(8,128)S(1)}) custom-call(s32[1]{0:T(128)} %bitcast.core, s32[1]{0:T(128)} %bitcast.1.place, f32[64,1024]{1,0:T(8,128)S(1)} %collective-permute-done.right, f32[1760,128]{1,0:T(8,128)S(1)} %bitcast.28, f32[64,2048]{1,0:T(8,128)S(1)} %get-tuple-element.31.west, ...), custom_call_target="tpu_custom_call" | custom-call | bytes 7000000 | tf_op jit(solution)/shard_map/right/pallas_call | solution.py:481
  21.1 3.0 %collective-permute-start.2 = (f32[904,128]{1,0:T(8,128)S(1)}, f32[904,128]{1,0:T(8,128)S(1)}, u32[]{:S(2)}, u32[]{:S(2)}) collective-permute-start(f32[904,128]{1,0:T(8,128)S(1)} %get-tuple-element.39), channel_id=1, source_target_pairs={{0,32},{32,0},{64,96},{96,64},{128,160},{160,128},{192,224},{224,1... | collective-permute-start | bytes 1388552 | tf_op jit(solution)/shard_map/ppermute | solution.py:503
  24.1 1.4 %collective-permute-done.2 = f32[904,128]{1,0:T(8,128)S(1)} collective-permute-done((f32[904,128]{1,0:T(8,128)S(1)}, f32[904,128]{1,0:T(8,128)S(1)}, u32[]{:S(2)}, u32[]{:S(2)}) %collective-permute-start.2) | collective-permute-done | bytes 462880 | tf_op jit(solution)/shard_map/ppermute | solution.py:503
  25.6 0.1 add.12
  25.7 3.1 %collective-permute-start.3 = (f32[224,128]{1,0:T(8,128)S(1)}, f32[224,128]{1,0:T(8,128)S(1)}, u32[]{:S(2)}, u32[]{:S(2)}) collective-permute-start(f32[224,128]{1,0:T(8,128)S(1)} %get-tuple-element.48), channel_id=1, source_target_pairs={{0,64},{32,96},{64,128},{96,160},{128,192},{160,224},{192,0},{224,... | collective-permute-start | bytes 344072 | tf_op jit(solution)/shard_map/ppermute | solution.py:499
  28.7 4.5 %collective-permute-start.4 = (f32[224,128]{1,0:T(8,128)S(1)}, f32[224,128]{1,0:T(8,128)S(1)}, u32[]{:S(2)}, u32[]{:S(2)}) collective-permute-start(f32[224,128]{1,0:T(8,128)S(1)} %get-tuple-element.47), channel_id=1, source_target_pairs={{0,128},{32,160},{64,192},{96,224},{128,0},{160,32},{192,64},{224,... | collective-permute-start | bytes 344072 | tf_op jit(solution)/shard_map/ppermute | solution.py:499
  33.3 2.4 %collective-permute-start.5 = (f32[224,128]{1,0:T(8,128)S(1)}, f32[224,128]{1,0:T(8,128)S(1)}, u32[]{:S(2)}, u32[]{:S(2)}) collective-permute-start(f32[224,128]{1,0:T(8,128)S(1)} %get-tuple-element.46), channel_id=1, source_target_pairs={{0,192},{32,224},{64,0},{96,32},{128,64},{160,96},{192,128},{224,1... | collective-permute-start | bytes 344072 | tf_op jit(solution)/shard_map/ppermute | solution.py:499
  35.7 10.9 %all_to_all.5 = f32[32,1,128]{2,1,0:T(1,128)S(1)} all-to-all(f32[32,1,128]{2,1,0:T(1,128)S(1)} %broadcast_in_dim.14), channel_id=1, replica_groups=mesh['mem'=8,'patch'=32] {'patch'}, dimensions={0} | all-to-all | bytes 32768 | tf_op jit(solution)/shard_map/all_to_all | solution.py:507
  46.5 0.0 collective-permute-done.3
  46.5 0.0 collective-permute-done.4
  46.6 0.0 collective-permute-done.5
  46.6 0.1 reduce_sum.9
  46.7 1.8 %collective-permute-start.6 = (f32[232,128]{1,0:T(8,128)S(1)}, f32[232,128]{1,0:T(8,128)S(1)}, u32[]{:S(2)}, u32[]{:S(2)}) collective-permute-start(f32[232,128]{1,0:T(8,128)S(1)} %get-tuple-element.50), channel_id=1, source_target_pairs={{0,128},{32,160},{64,192},{96,224},{128,0},{160,32},{192,64},{224,... | collective-permute-start | bytes 356360 | tf_op jit(solution)/shard_map/ppermute | solution.py:499
  48.5 1.9 %collective-permute-start.8 = (f32[232,128]{1,0:T(8,128)S(1)}, f32[232,128]{1,0:T(8,128)S(1)}, u32[]{:S(2)}, u32[]{:S(2)}) collective-permute-start(f32[232,128]{1,0:T(8,128)S(1)} %get-tuple-element.50), channel_id=1, source_target_pairs={{0,64},{32,96},{64,128},{96,160},{128,192},{160,224},{192,0},{224,... | collective-permute-start | bytes 356360 | tf_op jit(solution)/shard_map/ppermute | solution.py:499
  50.4 1.7 %collective-permute-start.9 = (f32[232,128]{1,0:T(8,128)S(1)}, f32[232,128]{1,0:T(8,128)S(1)}, u32[]{:S(2)}, u32[]{:S(2)}) collective-permute-start(f32[232,128]{1,0:T(8,128)S(1)} %get-tuple-element.50), channel_id=1, source_target_pairs={{0,192},{32,224},{64,0},{96,32},{128,64},{160,96},{192,128},{224,1... | collective-permute-start | bytes 356360 | tf_op jit(solution)/shard_map/ppermute | solution.py:499
  52.1 2.5 %collective-permute-done.6 = f32[232,128]{1,0:T(8,128)S(1)} collective-permute-done((f32[232,128]{1,0:T(8,128)S(1)}, f32[232,128]{1,0:T(8,128)S(1)}, u32[]{:S(2)}, u32[]{:S(2)}) %collective-permute-start.6) | collective-permute-done | bytes 118816 | tf_op jit(solution)/shard_map/ppermute | solution.py:499
  54.6 7.1 %collective-permute-start.7 = (f32[2,232,128]{2,1,0:T(8,128)S(1)}, f32[2,232,128]{2,1,0:T(8,128)S(1)}, u32[]{:S(2)}, u32[]{:S(2)}) collective-permute-start(f32[2,232,128]{2,1,0:T(8,128)S(1)} %pad_maximum_fusion.same), channel_id=1, source_target_pairs={{0,32},{32,0},{64,96},{96,64},{128,160},{160,128},{192,224},{224,1... | collective-permute-start | bytes 712712 | tf_op jit(solution)/shard_map/ppermute | solution.py:532
  61.7 0.0 collective-permute-done.8
  61.7 0.1 collective-permute-done.9
  61.8 0.6 collective-permute-start.10
  62.4 0.4 collective-permute-done.7.other
  62.8 1.3 %early.1 = (f32[1760,128]{1,0:T(8,128)}, f32[1,1]{1,0:T(1,128)}) custom-call(s32[1]{0:T(128)} %bitcast.core, s32[1]{0:T(128)} %bitcast.1.place, f32[2,232,128]{2,1,0:T(8,128)S(1)} %pad_maximum_fusion.same, f32[2,232,128]{2,1,0:T(8,128)S(1)} %collective-permute-done.7.other, f32[2,232,128]{2,1,0:T(8,128)S(1)} %pad_maximum_fusion.1.late.same), custom_call_target="tpu_custom_call" | custom-call | flops 1000000 | bytes 4000000 | tf_op jit(solution)/shard_map/early/pallas_call | solution.py:520
  64.1 0.0 collective-permute-done.10.other
  64.1 0.8 %late.1 = f32[1760,128]{1,0:T(8,128)} custom-call(s32[1]{0:T(128)} %bitcast.core, s32[1]{0:T(128)} %bitcast.1.place, f32[1760,128]{1,0:T(8,128)} %get-tuple-element.44.begun, f32[2,232,128]{2,1,0:T(8,128)S(1)} %pad_maximum_fusion.1.late.same, f32[2,232,128]{2,1,0:T(8,128)S(1)} %collective-permute-done.10.other), custom_call_target="tpu_custom_call", output_to_operand_aliasing={{}: (2, {})} | custom-call | tf_op jit(solution)/shard_map/late/pallas_call | solution.py:533
  (8 shorter events, 0.1 us)
Async XLA Ops:
  0.6 9.1 %copy-start.1 = (f32[55,55]{1,0:T(8,128)S(1)}, f32[55,55]{1,0:T(8,128)}, u32[]{:S(2)}) copy-start(f32[55,55]{1,0:T(8,128)} %root.1) | copy-start | bytes 36304
  2.5 11.7 %collective-permute-start.1 = (f32[64,1024]{1,0:T(8,128)S(1)}, f32[64,1024]{1,0:T(8,128)S(1)}, u32[]{:S(2)}, u32[]{:S(2)}) collective-permute-start(f32[64,1024]{1,0:T(8,128)S(1)} %get-tuple-element.25.tail), channel_id=1, source_target_pairs={{0,1},{1,2},{2,3},{3,4},{4,5},{5,6},{6,7},{7,8},{8,9},{9,10},{10,1... | collective-permute-start | bytes 786440 | tf_op jit(solution)/shard_map/ppermute | solution.py:437
  4.6 13.0 %collective-permute-start = (f32[64,1024]{1,0:T(8,128)S(1)}, f32[64,1024]{1,0:T(8,128)S(1)}, u32[]{:S(2)}, u32[]{:S(2)}) collective-permute-start(f32[64,1024]{1,0:T(8,128)S(1)} %get-tuple-element.24.head), channel_id=1, source_target_pairs={{1,0},{2,1},{3,2},{4,3},{5,4},{6,5},{7,6},{8,7},{9,8},{10,9},{11,1... | collective-permute-start | bytes 786440 | tf_op jit(solution)/shard_map/ppermute | solution.py:438
  14.2 3.4 %copy-start = (f32[1,2,55,2048]{3,1,2,0:T(2,128)S(1)}, f32[1,2,55,2048]{3,1,2,0:T(2,128)}, u32[]{:S(2)}) copy-start(f32[1,2,55,2048]{3,1,2,0:T(2,128)} %param.5) | copy-start | bytes 2703364
  21.1 4.5 %collective-permute-start.2 = (f32[904,128]{1,0:T(8,128)S(1)}, f32[904,128]{1,0:T(8,128)S(1)}, u32[]{:S(2)}, u32[]{:S(2)}) collective-permute-start(f32[904,128]{1,0:T(8,128)S(1)} %get-tuple-element.39), channel_id=1, source_target_pairs={{0,32},{32,0},{64,96},{96,64},{128,160},{160,128},{192,224},{224,1... | collective-permute-start | bytes 1388552 | tf_op jit(solution)/shard_map/ppermute | solution.py:503
  25.7 20.9 %collective-permute-start.3 = (f32[224,128]{1,0:T(8,128)S(1)}, f32[224,128]{1,0:T(8,128)S(1)}, u32[]{:S(2)}, u32[]{:S(2)}) collective-permute-start(f32[224,128]{1,0:T(8,128)S(1)} %get-tuple-element.48), channel_id=1, source_target_pairs={{0,64},{32,96},{64,128},{96,160},{128,192},{160,224},{192,0},{224,... | collective-permute-start | bytes 344072 | tf_op jit(solution)/shard_map/ppermute | solution.py:499
  28.7 17.8 %collective-permute-start.4 = (f32[224,128]{1,0:T(8,128)S(1)}, f32[224,128]{1,0:T(8,128)S(1)}, u32[]{:S(2)}, u32[]{:S(2)}) collective-permute-start(f32[224,128]{1,0:T(8,128)S(1)} %get-tuple-element.47), channel_id=1, source_target_pairs={{0,128},{32,160},{64,192},{96,224},{128,0},{160,32},{192,64},{224,... | collective-permute-start | bytes 344072 | tf_op jit(solution)/shard_map/ppermute | solution.py:499
  33.3 13.3 %collective-permute-start.5 = (f32[224,128]{1,0:T(8,128)S(1)}, f32[224,128]{1,0:T(8,128)S(1)}, u32[]{:S(2)}, u32[]{:S(2)}) collective-permute-start(f32[224,128]{1,0:T(8,128)S(1)} %get-tuple-element.46), channel_id=1, source_target_pairs={{0,192},{32,224},{64,0},{96,32},{128,64},{160,96},{192,128},{224,1... | collective-permute-start | bytes 344072 | tf_op jit(solution)/shard_map/ppermute | solution.py:499
  46.7 7.9 %collective-permute-start.6 = (f32[232,128]{1,0:T(8,128)S(1)}, f32[232,128]{1,0:T(8,128)S(1)}, u32[]{:S(2)}, u32[]{:S(2)}) collective-permute-start(f32[232,128]{1,0:T(8,128)S(1)} %get-tuple-element.50), channel_id=1, source_target_pairs={{0,128},{32,160},{64,192},{96,224},{128,0},{160,32},{192,64},{224,... | collective-permute-start | bytes 356360 | tf_op jit(solution)/shard_map/ppermute | solution.py:499
  48.5 13.2 %collective-permute-start.8 = (f32[232,128]{1,0:T(8,128)S(1)}, f32[232,128]{1,0:T(8,128)S(1)}, u32[]{:S(2)}, u32[]{:S(2)}) collective-permute-start(f32[232,128]{1,0:T(8,128)S(1)} %get-tuple-element.50), channel_id=1, source_target_pairs={{0,64},{32,96},{64,128},{96,160},{128,192},{160,224},{192,0},{224,... | collective-permute-start | bytes 356360 | tf_op jit(solution)/shard_map/ppermute | solution.py:499
  50.4 11.4 %collective-permute-start.9 = (f32[232,128]{1,0:T(8,128)S(1)}, f32[232,128]{1,0:T(8,128)S(1)}, u32[]{:S(2)}, u32[]{:S(2)}) collective-permute-start(f32[232,128]{1,0:T(8,128)S(1)} %get-tuple-element.50), channel_id=1, source_target_pairs={{0,192},{32,224},{64,0},{96,32},{128,64},{160,96},{192,128},{224,1... | collective-permute-start | bytes 356360 | tf_op jit(solution)/shard_map/ppermute | solution.py:499
  54.6 8.2 %collective-permute-start.7 = (f32[2,232,128]{2,1,0:T(8,128)S(1)}, f32[2,232,128]{2,1,0:T(8,128)S(1)}, u32[]{:S(2)}, u32[]{:S(2)}) collective-permute-start(f32[2,232,128]{2,1,0:T(8,128)S(1)} %pad_maximum_fusion.same), channel_id=1, source_target_pairs={{0,32},{32,0},{64,96},{96,64},{128,160},{160,128},{192,224},{224,1... | collective-permute-start | bytes 712712 | tf_op jit(solution)/shard_map/ppermute | solution.py:532
  61.8 2.4 %collective-permute-start.10 = (f32[2,232,128]{2,1,0:T(8,128)S(1)}, f32[2,232,128]{2,1,0:T(8,128)S(1)}, u32[]{:S(2)}, u32[]{:S(2)}) collective-permute-start(f32[2,232,128]{2,1,0:T(8,128)S(1)} %pad_maximum_fusion.1.late.same), channel_id=1, source_target_pairs={{0,32},{32,0},{64,96},{96,64},{128,160},{160,128},{192,224},{224,1... | collective-permute-start | bytes 712712 | tf_op jit(solution)/shard_map/ppermute | solution.py:542

commit v7 on v6

--- a/solution.py
+++ b/solution.py
@@ -17,50 +17,50 @@
 
 
 def prepare_kernel(
-    all_cells, place, ens, field, diff, neigh, head, tail, ens_in, field_in, diff_in, neigh_in, sems
+    all_cells, part, place, ens, field, diff, neigh, out, ens_in, field_in, diff_in, neigh_in, sems
 ):
-    own = diff.shape[1]
-    tiles = own // LANES
-    half = own // 2
-    start = place[0]
+    tiles = ens.shape[1] // 2
+    half = diff.shape[1] // 2
+    cols = pl.ds(part * half, half)
     levels = (0, 16, 32, 48, LEVELS)
     copies = []
     for turn in range(4):
-        rows = pl.ds(levels[turn] * 2 * tiles, (levels[turn + 1] - levels[turn]) * 2 * tiles)
-        copies.append((
-            pltpu.make_async_copy(ens.at[rows], ens_in.at[rows], sems.at[0, turn]),
-            pltpu.make_async_copy(field.at[rows], field_in.at[rows], sems.at[1, turn]),
+        rows = pl.ds(levels[turn], levels[turn + 1] - levels[turn])
+        copies.append(tuple(
+            pltpu.make_async_copy(
+                source.at[rows, pl.ds(part * tiles, tiles)], target.at[rows], sems.at[which, turn]
+            )
+            for which, (source, target) in enumerate(((ens, ens_in), (field, field_in)))
         ))
     others = (
-        pltpu.make_async_copy(neigh, neigh_in, sems.at[2, 0]),
-        pltpu.make_async_copy(diff, diff_in, sems.at[2, 1]),
+        pltpu.make_async_copy(neigh.at[:, cols], neigh_in, sems.at[2, 0]),
+        pltpu.make_async_copy(diff.at[:, cols], diff_in, sems.at[2, 1]),
     )
     for copy in others + copies[0] + copies[1] + copies[2] + copies[3]:
         copy.start()
     for copy in others:
         copy.wait()
-    for part, out in ((0, head), (1, tail)):
-        cols = pl.ds(part * half, half)
-        out[55:56, :] = jnp.ones((1, half), jnp.float32)
-        cell = lax.broadcasted_iota(jnp.int32, (7, half), 1) + (start + part * half)
-        shift = neigh_in[:, cols] - cell
-        shift = jnp.where(shift > all_cells // 2, shift - all_cells, shift)
-        shift = jnp.where(shift < -(all_cells // 2), shift + all_cells, shift)
-        out[56:63, :] = shift.astype(jnp.float32)
-        out[63:64, :] = diff_in[:, cols]
+    out[55:56, :] = jnp.ones((1, half), jnp.float32)
+    cell = lax.broadcasted_iota(jnp.int32, (7, half), 1) + (place[0] + part * half)
+    shift = neigh_in[...] - cell
+    shift = jnp.where(shift > all_cells // 2, shift - all_cells, shift)
+    shift = jnp.where(shift < -(all_cells // 2), shift + all_cells, shift)
+    out[56:63, :] = shift.astype(jnp.float32)
+    out[63:64, :] = diff_in[...]
+    ens_flat = ens_in.reshape(LEVELS * tiles, LANES)
+    field_flat = field_in.reshape(LEVELS * tiles, LANES)
     for turn in range(4):
         for copy in copies[turn]:
             copy.wait()
         low, high = levels[turn], levels[turn + 1]
-        rows = pl.ds(low * 2 * tiles, (high - low) * 2 * tiles)
-        ens_in[rows, :] = ens_in[rows, :] * field_in[rows, :]
-        for part, out in ((0, head), (1, tail)):
-            for tile in range(tiles // 2):
-                at = low * 2 * tiles + 2 * (part * (tiles // 2) + tile)
-                out[low:high, tile * LANES : (tile + 1) * LANES] = (
-                    ens_in[pl.ds(at, high - low, stride=2 * tiles), :]
-                    + ens_in[pl.ds(at + 1, high - low, stride=2 * tiles), :]
-                )
+        rows = pl.ds(low * tiles, (high - low) * tiles)
+        ens_flat[rows, :] = ens_flat[rows, :] * field_flat[rows, :]
+        for tile in range(tiles // 2):
+            at = low * tiles + 2 * tile
+            out[low:high, tile * LANES : (tile + 1) * LANES] = (
+                ens_flat[pl.ds(at, high - low, stride=tiles), :]
+                + ens_flat[pl.ds(at + 1, high - low, stride=tiles), :]
+            )
 
 
 def build_block(shift, store):
@@ -415,24 +415,31 @@
 
     in_hbm = [
         pltpu.with_memory_space_constraint(array, pltpu.HBM)
-        for array in (ens_rows, field_rows, diffusivity.reshape(1, own), neighbours)
+        for array in (
+            ens_rows.reshape(LEVELS, 2 * tiles, LANES),
+            field_rows.reshape(LEVELS, 2 * tiles, LANES),
+            diffusivity.reshape(1, own),
+            neighbours,
+        )
     ]
-    side = jax.ShapeDtypeStruct((64, half), jnp.float32)
-    head, tail = pl.pallas_call(
-        functools.partial(prepare_kernel, all_cells),
-        out_shape=(side, side),
-        in_specs=[smem, hbm, hbm, hbm, hbm],
-        out_specs=(vmem, vmem),
-        scratch_shapes=[
-            pltpu.VMEM(ens_rows.shape, jnp.float32),
-            pltpu.VMEM(ens_rows.shape, jnp.float32),
-            pltpu.VMEM((1, own), jnp.float32),
-            pltpu.VMEM((7, own), jnp.int32),
-            pltpu.SemaphoreType.DMA((3, 4)),
-        ],
-        compiler_params=params,
-        name="prepare",
-    )(place, *in_hbm)
+    tail, head = [
+        pl.pallas_call(
+            functools.partial(prepare_kernel, all_cells, part),
+            out_shape=jax.ShapeDtypeStruct((64, half), jnp.float32),
+            in_specs=[smem, hbm, hbm, hbm, hbm],
+            out_specs=vmem,
+            scratch_shapes=[
+                pltpu.VMEM((LEVELS, tiles, LANES), jnp.float32),
+                pltpu.VMEM((LEVELS, tiles, LANES), jnp.float32),
+                pltpu.VMEM((1, half), jnp.float32),
+                pltpu.VMEM((7, half), jnp.int32),
+                pltpu.SemaphoreType.DMA((3, 4)),
+            ],
+            compiler_params=params,
+            name=name,
+        )(place, *in_hbm)
+        for part, name in ((1, "tail"), (0, "head"))
+    ]
 
     left = lax.ppermute(tail, "patch", [(i, (i + 1) % patches) for i in range(patches)])
     right = lax.ppermute(head, "patch", [((i + 1) % patches, i) for i in range(patches)])

time: 65.3 us -> 66.2 us (1.014)
  starting transfers between devices: 33.3 us -> 30.6 us
  blocking collectives: 10.9 us -> 12.4 us
  Pallas kernels: 14.8 us -> 15.8 us
  waiting for transfers between devices: 4.98 us -> 5.94 us
    ppermute x6, waiting for transfers between devices: 2.59 us -> 4.28 us  [shift_chips(): return lax.ppermute(array, 'mem', pairs)]
    all_to_all x1, blocking collectives: 10.9 us -> 12.4 us  [on_device(): spread = lax.all_to_all(spread, 'patch', 0, 0)]
    ppermute x1, starting transfers between devices: 7.08 us -> 5.9 us  [on_device(): lax.ppermute(early, 'mem', twin)]
    pallas_call x1 -> x2, Pallas kernels: 1.8 us -> 2.86 us  [on_device(): pl.pallas_call(functools.partial(prepare_kernel, all_cells, part), out_sh...]
    ppermute x6, starting transfers between devices: 15.3 us -> 14.4 us  [shift_chips(): return lax.ppermute(array, 'mem', pairs)]
  transfers between devices with their start and end apart: 11 -> 11, of which waited for: 5 -> 4; matrix products, arithmetic and copies ran while one was open for 0% -> 0% of each run, Pallas kernels for 13% -> 15%
where the time goes in v7:
time: 66.2 us; the launch traced here: 66 us
  starting transfers between devices  30.6 us (46%)
  Pallas kernels  15.8 us (24%)
  blocking collectives  12.4 us (19%)
  waiting for transfers between devices  5.94 us (9%)
  between operations  0.93 us (1%)
    ppermute x6, starting transfers between devices, shift_chips(): return lax.ppermute(array, 'mem', pairs)  14.4 us
    all_to_all x1, blocking collectives, on_device(): spread = lax.all_to_all(spread, 'patch', 0, 0)  12.4 us
    ppermute x1, starting transfers between devices, on_device(): lax.ppermute(early, 'mem', twin)  5.9 us
    ppermute x1, starting transfers between devices, on_device(): lax.ppermute(head, 'patch', [((i + 1) % patches, i) for i in range(patche...  5.16 us
    ppermute x6, waiting for transfers between devices, shift_chips(): return lax.ppermute(array, 'mem', pairs)  4.28 us
    pallas_call x1, Pallas kernels, on_device(): pl.pallas_call(interior_kernel, out_shape=(jax.ShapeDtypeStruct((blocks /...  3.93 us
    pallas_call x1, Pallas kernels, on_device(): pl.pallas_call(right_kernel, out_shape=(terms, terms), in_specs=[smem] *...  3.57 us
    pallas_call x1, Pallas kernels, on_device(): pl.pallas_call(left_kernel, out_shape=(jax.ShapeDtypeStruct((64, HALO + h...  3.35 us
  transfers between devices with their start and end apart: 11, of which 4 were waited for; matrix products, arithmetic and copies ran while one was open for 0% of the time, Pallas kernels for 15%

profile of v7, /device:TPU:1, one launch (start us, length us, event | category | flops | bytes accessed | tf_op | source)
XLA Modules:
  0.0 66.0 jit_solution(1278236859461589863)
XLA Ops:
  0.6 1.4 %tail.1 = f32[64,1024]{1,0:T(8,128)S(1)} custom-call(s32[1]{0:T(128)} %bitcast.2.place, f32[55,32,128]{2,1,0:T(8,128)} %bitcast.29, f32[55,32,128]{2,1,0:T(8,128)} %bitcast.32, f32[1,2048]{1,0:T(1,128)} %bitcast.38, s32[7,2048]{1,0:T(8,128)} %neigh.3), custom_call_target="tpu_custom_call" | custom-call | tf_op jit(solution)/shard_map/tail/pallas_call | solution.py:426
  2.1 0.0 copy-start.1
  2.1 2.1 %collective-permute-start.1 = (f32[64,1024]{1,0:T(8,128)S(1)}, f32[64,1024]{1,0:T(8,128)S(1)}, u32[]{:S(2)}, u32[]{:S(2)}) collective-permute-start(f32[64,1024]{1,0:T(8,128)S(1)} %tail.1), channel_id=1, source_target_pairs={{0,1},{1,2},{2,3},{3,4},{4,5},{5,6},{6,7},{7,8},{8,9},{9,10},{10,1... | collective-permute-start | bytes 786440 | tf_op jit(solution)/shard_map/ppermute | solution.py:444
  4.2 1.4 %head.1 = f32[64,1024]{1,0:T(8,128)S(1)} custom-call(s32[1]{0:T(128)} %bitcast.2.place, f32[55,32,128]{2,1,0:T(8,128)} %bitcast.30, f32[55,32,128]{2,1,0:T(8,128)} %bitcast.33, f32[1,2048]{1,0:T(1,128)} %bitcast.39, s32[7,2048]{1,0:T(8,128)} %neigh.3), custom_call_target="tpu_custom_call" | custom-call | tf_op jit(solution)/shard_map/head/pallas_call | solution.py:426
  5.6 5.2 %collective-permute-start = (f32[64,1024]{1,0:T(8,128)S(1)}, f32[64,1024]{1,0:T(8,128)S(1)}, u32[]{:S(2)}, u32[]{:S(2)}) collective-permute-start(f32[64,1024]{1,0:T(8,128)S(1)} %head.1), channel_id=1, source_target_pairs={{1,0},{2,1},{3,2},{4,3},{5,4},{6,5},{7,6},{8,7},{9,8},{10,9},{11,1... | collective-permute-start | bytes 786440 | tf_op jit(solution)/shard_map/ppermute | solution.py:445
  10.8 0.0 copy-done.1
  10.8 3.9 %interior.1 = (bf16[4,512,256]{2,1,0:T(8,128)(2,1)S(1)}, bf16[5,512,256]{2,1,0:T(8,128)(2,1)S(1)}, f32[64,1024]{1,0:T(8,128)S(1)}, f32[64,1024]{1,0:T(8,128)S(1)...) custom-call(f32[64,1024]{1,0:T(8,128)S(1)} %head.1, ...), custom_call_target="tpu_custom_call" | custom-call | flops 4000000000 | bytes 4000000 | tf_op jit(solution)/shard_map/interior/pallas_call | solution.py:452
  14.7 0.0 collective-permute-done.1.left
  14.8 0.0 copy-start
  14.8 3.4 %left.1 = (f32[64,2048]{1,0:T(8,128)S(1)}, bf16[224,384]{1,0:T(8,128)(2,1)S(1)}) custom-call(f32[64,1024]{1,0:T(8,128)S(1)} %collective-permute-done.1.left, bf16[4,512,256]{2,1,0:T(8,128)(2,1)S(1)} %get-tuple-element.22.inner, f32[64,1024]{1,0:T(8,128)S(1)} %get-tuple-element.23.done, bf16[224,1920]{1,0:T(8,128)(2,1)S(1)} %get-tuple-element.24.parts, ...), custom_call_target="tpu_custom_call" | custom-call | bytes 7000000 | tf_op jit(solution)/shard_map/left/pallas_call | solution.py:473
  18.1 0.0 collective-permute-done.right
  18.1 0.0 copy-done
  18.1 3.6 %right.1 = (f32[904,128]{1,0:T(8,128)S(1)}, f32[904,128]{1,0:T(8,128)S(1)}) custom-call(s32[1]{0:T(128)} %bitcast.core, s32[1]{0:T(128)} %bitcast.1.place, f32[64,1024]{1,0:T(8,128)S(1)} %collective-permute-done.right, f32[1760,128]{1,0:T(8,128)S(1)} %bitcast.31, f32[64,2048]{1,0:T(8,128)S(1)} %get-tuple-element.27.west, ...), custom_call_target="tpu_custom_call" | custom-call | bytes 7000000 | tf_op jit(solution)/shard_map/right/pallas_call | solution.py:488
  21.7 2.5 %collective-permute-start.2 = (f32[904,128]{1,0:T(8,128)S(1)}, f32[904,128]{1,0:T(8,128)S(1)}, u32[]{:S(2)}, u32[]{:S(2)}) collective-permute-start(f32[904,128]{1,0:T(8,128)S(1)} %get-tuple-element.35), channel_id=1, source_target_pairs={{0,32},{32,0},{64,96},{96,64},{128,160},{160,128},{192,224},{224,1... | collective-permute-start | bytes 1388552 | tf_op jit(solution)/shard_map/ppermute | solution.py:510
  24.2 1.4 %collective-permute-done.2 = f32[904,128]{1,0:T(8,128)S(1)} collective-permute-done((f32[904,128]{1,0:T(8,128)S(1)}, f32[904,128]{1,0:T(8,128)S(1)}, u32[]{:S(2)}, u32[]{:S(2)}) %collective-permute-start.2) | collective-permute-done | bytes 462880 | tf_op jit(solution)/shard_map/ppermute | solution.py:510
  25.6 0.1 add.12
  25.7 2.7 %collective-permute-start.3 = (f32[224,128]{1,0:T(8,128)S(1)}, f32[224,128]{1,0:T(8,128)S(1)}, u32[]{:S(2)}, u32[]{:S(2)}) collective-permute-start(f32[224,128]{1,0:T(8,128)S(1)} %get-tuple-element.44), channel_id=1, source_target_pairs={{0,64},{32,96},{64,128},{96,160},{128,192},{160,224},{192,0},{224,... | collective-permute-start | bytes 344072 | tf_op jit(solution)/shard_map/ppermute | solution.py:506
  28.4 4.5 %collective-permute-start.4 = (f32[224,128]{1,0:T(8,128)S(1)}, f32[224,128]{1,0:T(8,128)S(1)}, u32[]{:S(2)}, u32[]{:S(2)}) collective-permute-start(f32[224,128]{1,0:T(8,128)S(1)} %get-tuple-element.43), channel_id=1, source_target_pairs={{0,128},{32,160},{64,192},{96,224},{128,0},{160,32},{192,64},{224,... | collective-permute-start | bytes 344072 | tf_op jit(solution)/shard_map/ppermute | solution.py:506
  32.9 2.4 %collective-permute-start.5 = (f32[224,128]{1,0:T(8,128)S(1)}, f32[224,128]{1,0:T(8,128)S(1)}, u32[]{:S(2)}, u32[]{:S(2)}) collective-permute-start(f32[224,128]{1,0:T(8,128)S(1)} %get-tuple-element.42), channel_id=1, source_target_pairs={{0,192},{32,224},{64,0},{96,32},{128,64},{160,96},{192,128},{224,1... | collective-permute-start | bytes 344072 | tf_op jit(solution)/shard_map/ppermute | solution.py:506
  35.3 12.4 %all_to_all.5 = f32[32,1,128]{2,1,0:T(1,128)S(1)} all-to-all(f32[32,1,128]{2,1,0:T(1,128)S(1)} %broadcast_in_dim.14), channel_id=1, replica_groups=mesh['mem'=8,'patch'=32] {'patch'}, dimensions={0} | all-to-all | bytes 32768 | tf_op jit(solution)/shard_map/all_to_all | solution.py:514
  47.7 0.0 collective-permute-done.3
  47.7 0.0 collective-permute-done.4
  47.7 0.0 collective-permute-done.5
  47.7 0.1 reduce_sum.9
  47.8 1.3 %collective-permute-start.6 = (f32[232,128]{1,0:T(8,128)S(1)}, f32[232,128]{1,0:T(8,128)S(1)}, u32[]{:S(2)}, u32[]{:S(2)}) collective-permute-start(f32[232,128]{1,0:T(8,128)S(1)} %get-tuple-element.46), channel_id=1, source_target_pairs={{0,128},{32,160},{64,192},{96,224},{128,0},{160,32},{192,64},{224,... | collective-permute-start | bytes 356360 | tf_op jit(solution)/shard_map/ppermute | solution.py:506
  49.1 1.2 %collective-permute-start.8 = (f32[232,128]{1,0:T(8,128)S(1)}, f32[232,128]{1,0:T(8,128)S(1)}, u32[]{:S(2)}, u32[]{:S(2)}) collective-permute-start(f32[232,128]{1,0:T(8,128)S(1)} %get-tuple-element.46), channel_id=1, source_target_pairs={{0,64},{32,96},{64,128},{96,160},{128,192},{160,224},{192,0},{224,... | collective-permute-start | bytes 356360 | tf_op jit(solution)/shard_map/ppermute | solution.py:506
  50.4 2.3 %collective-permute-start.9 = (f32[232,128]{1,0:T(8,128)S(1)}, f32[232,128]{1,0:T(8,128)S(1)}, u32[]{:S(2)}, u32[]{:S(2)}) collective-permute-start(f32[232,128]{1,0:T(8,128)S(1)} %get-tuple-element.46), channel_id=1, source_target_pairs={{0,192},{32,224},{64,0},{96,32},{128,64},{160,96},{192,128},{224,1... | collective-permute-start | bytes 356360 | tf_op jit(solution)/shard_map/ppermute | solution.py:506
  52.7 4.0 %collective-permute-done.6 = f32[232,128]{1,0:T(8,128)S(1)} collective-permute-done((f32[232,128]{1,0:T(8,128)S(1)}, f32[232,128]{1,0:T(8,128)S(1)}, u32[]{:S(2)}, u32[]{:S(2)}) %collective-permute-start.6) | collective-permute-done | bytes 118816 | tf_op jit(solution)/shard_map/ppermute | solution.py:506
  56.7 5.9 %collective-permute-start.7 = (f32[2,232,128]{2,1,0:T(8,128)S(1)}, f32[2,232,128]{2,1,0:T(8,128)S(1)}, u32[]{:S(2)}, u32[]{:S(2)}) collective-permute-start(f32[2,232,128]{2,1,0:T(8,128)S(1)} %pad_maximum_fusion.same), channel_id=1, source_target_pairs={{0,32},{32,0},{64,96},{96,64},{128,160},{160,128},{192,224},{224,1... | collective-permute-start | bytes 712712 | tf_op jit(solution)/shard_map/ppermute | solution.py:539
  62.6 0.0 collective-permute-done.8
  62.6 0.3 collective-permute-done.9
  62.9 0.6 collective-permute-start.10
  63.5 0.2 collective-permute-done.7.other
  63.7 1.3 %early.1 = (f32[1760,128]{1,0:T(8,128)}, f32[1,1]{1,0:T(1,128)}) custom-call(s32[1]{0:T(128)} %bitcast.core, s32[1]{0:T(128)} %bitcast.1.place, f32[2,232,128]{2,1,0:T(8,128)S(1)} %pad_maximum_fusion.same, f32[2,232,128]{2,1,0:T(8,128)S(1)} %collective-permute-done.7.other, f32[2,232,128]{2,1,0:T(8,128)S(1)} %pad_maximum_fusion.1.late.same), custom_call_target="tpu_custom_call" | custom-call | flops 1000000 | bytes 4000000 | tf_op jit(solution)/shard_map/early/pallas_call | solution.py:527
  65.0 0.0 collective-permute-done.10.other
  65.0 0.8 %late.1 = f32[1760,128]{1,0:T(8,128)} custom-call(s32[1]{0:T(128)} %bitcast.core, s32[1]{0:T(128)} %bitcast.1.place, f32[1760,128]{1,0:T(8,128)} %get-tuple-element.40.begun, f32[2,232,128]{2,1,0:T(8,128)S(1)} %pad_maximum_fusion.1.late.same, f32[2,232,128]{2,1,0:T(8,128)S(1)} %collective-permute-done.10.other), custom_call_target="tpu_custom_call", output_to_operand_aliasing={{}: (2, {})} | custom-call | tf_op jit(solution)/shard_map/late/pallas_call | solution.py:540
  (8 shorter events, 0.1 us)
Async XLA Ops:
  2.1 8.7 %copy-start.1 = (f32[55,55]{1,0:T(8,128)S(1)}, f32[55,55]{1,0:T(8,128)}, u32[]{:S(2)}) copy-start(f32[55,55]{1,0:T(8,128)} %root.1) | copy-start | bytes 36304
  2.1 12.7 %collective-permute-start.1 = (f32[64,1024]{1,0:T(8,128)S(1)}, f32[64,1024]{1,0:T(8,128)S(1)}, u32[]{:S(2)}, u32[]{:S(2)}) collective-permute-start(f32[64,1024]{1,0:T(8,128)S(1)} %tail.1), channel_id=1, source_target_pairs={{0,1},{1,2},{2,3},{3,4},{4,5},{5,6},{6,7},{7,8},{8,9},{9,10},{10,1... | collective-permute-start | bytes 786440 | tf_op jit(solution)/shard_map/ppermute | solution.py:444
  5.6 12.5 %collective-permute-start = (f32[64,1024]{1,0:T(8,128)S(1)}, f32[64,1024]{1,0:T(8,128)S(1)}, u32[]{:S(2)}, u32[]{:S(2)}) collective-permute-start(f32[64,1024]{1,0:T(8,128)S(1)} %head.1), channel_id=1, source_target_pairs={{1,0},{2,1},{3,2},{4,3},{5,4},{6,5},{7,6},{8,7},{9,8},{10,9},{11,1... | collective-permute-start | bytes 786440 | tf_op jit(solution)/shard_map/ppermute | solution.py:445
  14.8 3.4 %copy-start = (f32[1,2,55,2048]{3,1,2,0:T(2,128)S(1)}, f32[1,2,55,2048]{3,1,2,0:T(2,128)}, u32[]{:S(2)}) copy-start(f32[1,2,55,2048]{3,1,2,0:T(2,128)} %param.5) | copy-start | bytes 2703364
  21.7 3.9 %collective-permute-start.2 = (f32[904,128]{1,0:T(8,128)S(1)}, f32[904,128]{1,0:T(8,128)S(1)}, u32[]{:S(2)}, u32[]{:S(2)}) collective-permute-start(f32[904,128]{1,0:T(8,128)S(1)} %get-tuple-element.35), channel_id=1, source_target_pairs={{0,32},{32,0},{64,96},{96,64},{128,160},{160,128},{192,224},{224,1... | collective-permute-start | bytes 1388552 | tf_op jit(solution)/shard_map/ppermute | solution.py:510
  25.7 22.0 %collective-permute-start.3 = (f32[224,128]{1,0:T(8,128)S(1)}, f32[224,128]{1,0:T(8,128)S(1)}, u32[]{:S(2)}, u32[]{:S(2)}) collective-permute-start(f32[224,128]{1,0:T(8,128)S(1)} %get-tuple-element.44), channel_id=1, source_target_pairs={{0,64},{32,96},{64,128},{96,160},{128,192},{160,224},{192,0},{224,... | collective-permute-start | bytes 344072 | tf_op jit(solution)/shard_map/ppermute | solution.py:506
  28.4 19.3 %collective-permute-start.4 = (f32[224,128]{1,0:T(8,128)S(1)}, f32[224,128]{1,0:T(8,128)S(1)}, u32[]{:S(2)}, u32[]{:S(2)}) collective-permute-start(f32[224,128]{1,0:T(8,128)S(1)} %get-tuple-element.43), channel_id=1, source_target_pairs={{0,128},{32,160},{64,192},{96,224},{128,0},{160,32},{192,64},{224,... | collective-permute-start | bytes 344072 | tf_op jit(solution)/shard_map/ppermute | solution.py:506
  32.9 14.8 %collective-permute-start.5 = (f32[224,128]{1,0:T(8,128)S(1)}, f32[224,128]{1,0:T(8,128)S(1)}, u32[]{:S(2)}, u32[]{:S(2)}) collective-permute-start(f32[224,128]{1,0:T(8,128)S(1)} %get-tuple-element.42), channel_id=1, source_target_pairs={{0,192},{32,224},{64,0},{96,32},{128,64},{160,96},{192,128},{224,1... | collective-permute-start | bytes 344072 | tf_op jit(solution)/shard_map/ppermute | solution.py:506
  47.8 8.8 %collective-permute-start.6 = (f32[232,128]{1,0:T(8,128)S(1)}, f32[232,128]{1,0:T(8,128)S(1)}, u32[]{:S(2)}, u32[]{:S(2)}) collective-permute-start(f32[232,128]{1,0:T(8,128)S(1)} %get-tuple-element.46), channel_id=1, source_target_pairs={{0,128},{32,160},{64,192},{96,224},{128,0},{160,32},{192,64},{224,... | collective-permute-start | bytes 356360 | tf_op jit(solution)/shard_map/ppermute | solution.py:506
  49.1 13.5 %collective-permute-start.8 = (f32[232,128]{1,0:T(8,128)S(1)}, f32[232,128]{1,0:T(8,128)S(1)}, u32[]{:S(2)}, u32[]{:S(2)}) collective-permute-start(f32[232,128]{1,0:T(8,128)S(1)} %get-tuple-element.46), channel_id=1, source_target_pairs={{0,64},{32,96},{64,128},{96,160},{128,192},{160,224},{192,0},{224,... | collective-permute-start | bytes 356360 | tf_op jit(solution)/shard_map/ppermute | solution.py:506
  50.4 12.5 %collective-permute-start.9 = (f32[232,128]{1,0:T(8,128)S(1)}, f32[232,128]{1,0:T(8,128)S(1)}, u32[]{:S(2)}, u32[]{:S(2)}) collective-permute-start(f32[232,128]{1,0:T(8,128)S(1)} %get-tuple-element.46), channel_id=1, source_target_pairs={{0,192},{32,224},{64,0},{96,32},{128,64},{160,96},{192,128},{224,1... | collective-permute-start | bytes 356360 | tf_op jit(solution)/shard_map/ppermute | solution.py:506
  56.7 7.0 %collective-permute-start.7 = (f32[2,232,128]{2,1,0:T(8,128)S(1)}, f32[2,232,128]{2,1,0:T(8,128)S(1)}, u32[]{:S(2)}, u32[]{:S(2)}) collective-permute-start(f32[2,232,128]{2,1,0:T(8,128)S(1)} %pad_maximum_fusion.same), channel_id=1, source_target_pairs={{0,32},{32,0},{64,96},{96,64},{128,160},{160,128},{192,224},{224,1... | collective-permute-start | bytes 712712 | tf_op jit(solution)/shard_map/ppermute | solution.py:539
  62.9 2.1 %collective-permute-start.10 = (f32[2,232,128]{2,1,0:T(8,128)S(1)}, f32[2,232,128]{2,1,0:T(8,128)S(1)}, u32[]{:S(2)}, u32[]{:S(2)}) collective-permute-start(f32[2,232,128]{2,1,0:T(8,128)S(1)} %pad_maximum_fusion.1.late.same), channel_id=1, source_target_pairs={{0,32},{32,0},{64,96},{96,64},{128,160},{160,128},{192,224},{224,1... | collective-permute-start | bytes 712712 | tf_op jit(solution)/shard_map/ppermute | solution.py:549

commit v8 on v5

--- a/solution.py
+++ b/solution.py
@@ -249,6 +249,9 @@
             )
             for block in range(step // 2, stop)
         ]
+        if step % 2:
+            at, matrix = places[0][0] + REACH, functools.partial(lambda b: outer[b, REACH:, REACH:], step // 2)
+            places[0] = (at, REACH, matrix, True)
         sweep(state, bufs[(step - 1) % 4], bufs[step % 4] if step < STEPS else None, bases, places)
     low = (middle - 1) * BLOCK - REACH - bases[1]
     seam[...] = bufs[(STEPS - 1) % 4][:, low : low + BLOCK + REACH]
@@ -293,6 +296,9 @@
             )
             for block in range(start, blocks - step // 2)
         ]
+        if step % 2:
+            matrix = functools.partial(lambda b: outer[b, : BLOCK + REACH, :REACH], fringe - 1 - step // 2)
+            places[-1] = (places[-1][0], REACH, matrix, True)
         if step == STEPS:
             low = (middle - 1) * BLOCK - REACH - bases[1]
             bufs[(step - 1) % 4][:, low : low + BLOCK + REACH] = seam[...]

time: 65.3 us -> 65.2 us (level)
  no operation moved by 1% of the time
where the time goes in v8:
time: 65.2 us; the launch traced here: 65.1 us
  starting transfers between devices  33.2 us (51%)
  Pallas kernels  14.7 us (23%)
  blocking collectives  10.9 us (17%)
  waiting for transfers between devices  5.01 us (8%)
  between operations  0.91 us (1%)
    ppermute x6, starting transfers between devices, shift_chips(): return lax.ppermute(array, 'mem', pairs)  15.5 us
    all_to_all x1, blocking collectives, on_device(): spread = lax.all_to_all(spread, 'patch', 0, 0)  10.9 us
    ppermute x1, starting transfers between devices, on_device(): lax.ppermute(early, 'mem', twin)  7.05 us
    ppermute x1, starting transfers between devices, on_device(): lax.ppermute(head, 'patch', [((i + 1) % patches, i) for i in range(patche...  5.16 us
    pallas_call x1, Pallas kernels, on_device(): pl.pallas_call(interior_kernel, out_shape=(jax.ShapeDtypeStruct((blocks /...  3.93 us
    pallas_call x1, Pallas kernels, on_device(): pl.pallas_call(right_kernel, out_shape=(terms, terms), in_specs=[smem] *...  3.55 us
    pallas_call x1, Pallas kernels, on_device(): pl.pallas_call(left_kernel, out_shape=(jax.ShapeDtypeStruct((64, HALO + h...  3.32 us
    ppermute x1, starting transfers between devices, on_device(): pair_sum = keep + lax.ppermute(send, 'mem', twin)  2.82 us
  transfers between devices with their start and end apart: 11, of which 5 were waited for; matrix products, arithmetic and copies ran while one was open for 0% of the time, Pallas kernels for 12%

profile of v8, /device:TPU:1, one launch (start us, length us, event | category | flops | bytes accessed | tf_op | source)
XLA Modules:
  0.0 65.1 jit_solution(11755160229631250144)
XLA Ops:
  0.6 0.0 copy-start.1
  0.6 1.8 %prepare.1 = (f32[64,1024]{1,0:T(8,128)S(1)}, f32[64,1024]{1,0:T(8,128)S(1)}) custom-call(s32[1]{0:T(128)} %bitcast.2.place, f32[1760,128]{1,0:T(8,128)} %bitcast.27, f32[1760,128]{1,0:T(8,128)} %bitcast.30, f32[1,2048]{1,0:T(1,128)} %bitcast.34, s32[7,2048]{1,0:T(8,128)} %neigh.1), custom_call_target="tpu_custom_call" | custom-call | tf_op jit(solution)/shard_map/prepare/pallas_call | solution.py:427
  2.5 2.1 %collective-permute-start.1 = (f32[64,1024]{1,0:T(8,128)S(1)}, f32[64,1024]{1,0:T(8,128)S(1)}, u32[]{:S(2)}, u32[]{:S(2)}) collective-permute-start(f32[64,1024]{1,0:T(8,128)S(1)} %get-tuple-element.25.tail), channel_id=1, source_target_pairs={{0,1},{1,2},{2,3},{3,4},{4,5},{5,6},{6,7},{7,8},{8,9},{9,10},{10,1... | collective-permute-start | bytes 786440 | tf_op jit(solution)/shard_map/ppermute | solution.py:443
  4.6 5.2 %collective-permute-start = (f32[64,1024]{1,0:T(8,128)S(1)}, f32[64,1024]{1,0:T(8,128)S(1)}, u32[]{:S(2)}, u32[]{:S(2)}) collective-permute-start(f32[64,1024]{1,0:T(8,128)S(1)} %get-tuple-element.24.head), channel_id=1, source_target_pairs={{1,0},{2,1},{3,2},{4,3},{5,4},{6,5},{7,6},{8,7},{9,8},{10,9},{11,1... | collective-permute-start | bytes 786440 | tf_op jit(solution)/shard_map/ppermute | solution.py:444
  9.7 0.0 copy-done.1
  9.7 3.9 %interior.1 = (bf16[4,512,256]{2,1,0:T(8,128)(2,1)S(1)}, bf16[5,512,256]{2,1,0:T(8,128)(2,1)S(1)}, f32[64,1024]{1,0:T(8,128)S(1)}, f32[64,1024]{1,0:T(8,128)S(1)...) custom-call(f32[64,1024]{1,0:T(8,128)S(1)} %get-tuple-element.24.hea, ...), custom_call_target="tpu_custom_call" | custom-call | flops 4000000000 | bytes 4000000 | tf_op jit(solution)/shard_map/interior/pallas_call | solution.py:451
  13.7 0.5 collective-permute-done.1.left
  14.2 0.0 copy-start
  14.2 3.3 %left.1 = (f32[64,2048]{1,0:T(8,128)S(1)}, bf16[224,384]{1,0:T(8,128)(2,1)S(1)}) custom-call(f32[64,1024]{1,0:T(8,128)S(1)} %collective-permute-done.1.left, bf16[4,512,256]{2,1,0:T(8,128)(2,1)S(1)} %get-tuple-element.26.inner, f32[64,1024]{1,0:T(8,128)S(1)} %get-tuple-element.27.done, bf16[224,1920]{1,0:T(8,128)(2,1)S(1)} %get-tuple-element.28.parts, ...), custom_call_target="tpu_custom_call" | custom-call | bytes 7000000 | tf_op jit(solution)/shard_map/left/pallas_call | solution.py:472
  17.5 0.0 collective-permute-done.right
  17.5 0.0 copy-done
  17.5 3.6 %right.1 = (f32[904,128]{1,0:T(8,128)S(1)}, f32[904,128]{1,0:T(8,128)S(1)}) custom-call(s32[1]{0:T(128)} %bitcast.core, s32[1]{0:T(128)} %bitcast.1.place, f32[64,1024]{1,0:T(8,128)S(1)} %collective-permute-done.right, f32[1760,128]{1,0:T(8,128)S(1)} %bitcast.28, f32[64,2048]{1,0:T(8,128)S(1)} %get-tuple-element.31.west, ...), custom_call_target="tpu_custom_call" | custom-call | bytes 7000000 | tf_op jit(solution)/shard_map/right/pallas_call | solution.py:487
  21.1 2.8 %collective-permute-start.2 = (f32[904,128]{1,0:T(8,128)S(1)}, f32[904,128]{1,0:T(8,128)S(1)}, u32[]{:S(2)}, u32[]{:S(2)}) collective-permute-start(f32[904,128]{1,0:T(8,128)S(1)} %get-tuple-element.39), channel_id=1, source_target_pairs={{0,32},{32,0},{64,96},{96,64},{128,160},{160,128},{192,224},{224,1... | collective-permute-start | bytes 1388552 | tf_op jit(solution)/shard_map/ppermute | solution.py:509
  23.9 1.4 %collective-permute-done.2 = f32[904,128]{1,0:T(8,128)S(1)} collective-permute-done((f32[904,128]{1,0:T(8,128)S(1)}, f32[904,128]{1,0:T(8,128)S(1)}, u32[]{:S(2)}, u32[]{:S(2)}) %collective-permute-start.2) | collective-permute-done | bytes 462880 | tf_op jit(solution)/shard_map/ppermute | solution.py:509
  25.4 0.1 add.12
  25.4 3.2 %collective-permute-start.3 = (f32[224,128]{1,0:T(8,128)S(1)}, f32[224,128]{1,0:T(8,128)S(1)}, u32[]{:S(2)}, u32[]{:S(2)}) collective-permute-start(f32[224,128]{1,0:T(8,128)S(1)} %get-tuple-element.48), channel_id=1, source_target_pairs={{0,64},{32,96},{64,128},{96,160},{128,192},{160,224},{192,0},{224,... | collective-permute-start | bytes 344072 | tf_op jit(solution)/shard_map/ppermute | solution.py:505
  28.7 4.5 %collective-permute-start.4 = (f32[224,128]{1,0:T(8,128)S(1)}, f32[224,128]{1,0:T(8,128)S(1)}, u32[]{:S(2)}, u32[]{:S(2)}) collective-permute-start(f32[224,128]{1,0:T(8,128)S(1)} %get-tuple-element.47), channel_id=1, source_target_pairs={{0,128},{32,160},{64,192},{96,224},{128,0},{160,32},{192,64},{224,... | collective-permute-start | bytes 344072 | tf_op jit(solution)/shard_map/ppermute | solution.py:505
  33.2 2.4 %collective-permute-start.5 = (f32[224,128]{1,0:T(8,128)S(1)}, f32[224,128]{1,0:T(8,128)S(1)}, u32[]{:S(2)}, u32[]{:S(2)}) collective-permute-start(f32[224,128]{1,0:T(8,128)S(1)} %get-tuple-element.46), channel_id=1, source_target_pairs={{0,192},{32,224},{64,0},{96,32},{128,64},{160,96},{192,128},{224,1... | collective-permute-start | bytes 344072 | tf_op jit(solution)/shard_map/ppermute | solution.py:505
  35.6 10.9 %all_to_all.5 = f32[32,1,128]{2,1,0:T(1,128)S(1)} all-to-all(f32[32,1,128]{2,1,0:T(1,128)S(1)} %broadcast_in_dim.14), channel_id=1, replica_groups=mesh['mem'=8,'patch'=32] {'patch'}, dimensions={0} | all-to-all | bytes 32768 | tf_op jit(solution)/shard_map/all_to_all | solution.py:513
  46.5 0.0 collective-permute-done.3
  46.5 0.0 collective-permute-done.4
  46.5 0.0 collective-permute-done.5
  46.5 0.1 reduce_sum.9
  46.7 1.8 %collective-permute-start.6 = (f32[232,128]{1,0:T(8,128)S(1)}, f32[232,128]{1,0:T(8,128)S(1)}, u32[]{:S(2)}, u32[]{:S(2)}) collective-permute-start(f32[232,128]{1,0:T(8,128)S(1)} %get-tuple-element.50), channel_id=1, source_target_pairs={{0,128},{32,160},{64,192},{96,224},{128,0},{160,32},{192,64},{224,... | collective-permute-start | bytes 356360 | tf_op jit(solution)/shard_map/ppermute | solution.py:505
  48.4 1.9 %collective-permute-start.8 = (f32[232,128]{1,0:T(8,128)S(1)}, f32[232,128]{1,0:T(8,128)S(1)}, u32[]{:S(2)}, u32[]{:S(2)}) collective-permute-start(f32[232,128]{1,0:T(8,128)S(1)} %get-tuple-element.50), channel_id=1, source_target_pairs={{0,64},{32,96},{64,128},{96,160},{128,192},{160,224},{192,0},{224,... | collective-permute-start | bytes 356360 | tf_op jit(solution)/shard_map/ppermute | solution.py:505
  50.3 1.7 %collective-permute-start.9 = (f32[232,128]{1,0:T(8,128)S(1)}, f32[232,128]{1,0:T(8,128)S(1)}, u32[]{:S(2)}, u32[]{:S(2)}) collective-permute-start(f32[232,128]{1,0:T(8,128)S(1)} %get-tuple-element.50), channel_id=1, source_target_pairs={{0,192},{32,224},{64,0},{96,32},{128,64},{160,96},{192,128},{224,1... | collective-permute-start | bytes 356360 | tf_op jit(solution)/shard_map/ppermute | solution.py:505
  52.0 2.5 %collective-permute-done.6 = f32[232,128]{1,0:T(8,128)S(1)} collective-permute-done((f32[232,128]{1,0:T(8,128)S(1)}, f32[232,128]{1,0:T(8,128)S(1)}, u32[]{:S(2)}, u32[]{:S(2)}) %collective-permute-start.6) | collective-permute-done | bytes 118816 | tf_op jit(solution)/shard_map/ppermute | solution.py:505
  54.6 7.0 %collective-permute-start.7 = (f32[2,232,128]{2,1,0:T(8,128)S(1)}, f32[2,232,128]{2,1,0:T(8,128)S(1)}, u32[]{:S(2)}, u32[]{:S(2)}) collective-permute-start(f32[2,232,128]{2,1,0:T(8,128)S(1)} %pad_maximum_fusion.same.early), channel_id=1, source_target_pairs={{0,32},{32,0},{64,96},{96,64},{128,160},{160,128},{192,224},{224,1... | collective-permute-start | bytes 712712 | tf_op jit(solution)/shard_map/ppermute | solution.py:534
  61.6 0.0 collective-permute-done.8
  61.6 0.1 collective-permute-done.9
  61.8 0.6 collective-permute-start.10
  62.3 0.4 collective-permute-done.7.other
  62.8 0.8 %early.1.begun = f32[1760,128]{1,0:T(8,128)} custom-call(s32[1]{0:T(128)} %bitcast.core, s32[1]{0:T(128)} %bitcast.1.place, f32[2,232,128]{2,1,0:T(8,128)S(1)} %pad_maximum_fusion.same.early, f32[2,232,128]{2,1,0:T(8,128)S(1)} %collective-permute-done.7.other), custom_call_target="tpu_custom_call" | custom-call | flops 1000000 | bytes 4000000 | tf_op jit(solution)/shard_map/early/pallas_call | solution.py:525
  63.6 0.0 collective-permute-done.10.other
  63.6 1.3 %late.1 = (f32[1760,128]{1,0:T(8,128)}, f32[1,1]{1,0:T(1,128)}) custom-call(s32[1]{0:T(128)} %bitcast.core, s32[1]{0:T(128)} %bitcast.1.place, f32[1760,128]{1,0:T(8,128)} %early.1.begun, f32[2,232,128]{2,1,0:T(8,128)S(1)} %pad_maximum_fusion.same.early, f32[2,232,128]{2,1,0:T(8,128)S(1)} %pad_maximum_fusion.1.same, ...), custom_call_target="tpu_custom_call", output_to_operand_aliasing={{0}: (2, {})} | custom-call | tf_op jit(solution)/shard_map/late/pallas_call | solution.py:536
  (8 shorter events, 0.2 us)
Async XLA Ops:
  0.6 9.1 %copy-start.1 = (f32[55,55]{1,0:T(8,128)S(1)}, f32[55,55]{1,0:T(8,128)}, u32[]{:S(2)}) copy-start(f32[55,55]{1,0:T(8,128)} %root.1) | copy-start | bytes 36304
  2.5 11.7 %collective-permute-start.1 = (f32[64,1024]{1,0:T(8,128)S(1)}, f32[64,1024]{1,0:T(8,128)S(1)}, u32[]{:S(2)}, u32[]{:S(2)}) collective-permute-start(f32[64,1024]{1,0:T(8,128)S(1)} %get-tuple-element.25.tail), channel_id=1, source_target_pairs={{0,1},{1,2},{2,3},{3,4},{4,5},{5,6},{6,7},{7,8},{8,9},{9,10},{10,1... | collective-permute-start | bytes 786440 | tf_op jit(solution)/shard_map/ppermute | solution.py:443
  4.6 12.9 %collective-permute-start = (f32[64,1024]{1,0:T(8,128)S(1)}, f32[64,1024]{1,0:T(8,128)S(1)}, u32[]{:S(2)}, u32[]{:S(2)}) collective-permute-start(f32[64,1024]{1,0:T(8,128)S(1)} %get-tuple-element.24.head), channel_id=1, source_target_pairs={{1,0},{2,1},{3,2},{4,3},{5,4},{6,5},{7,6},{8,7},{9,8},{10,9},{11,1... | collective-permute-start | bytes 786440 | tf_op jit(solution)/shard_map/ppermute | solution.py:444
  14.2 3.3 %copy-start = (f32[1,2,55,2048]{3,1,2,0:T(2,128)S(1)}, f32[1,2,55,2048]{3,1,2,0:T(2,128)}, u32[]{:S(2)}) copy-start(f32[1,2,55,2048]{3,1,2,0:T(2,128)} %param.5) | copy-start | bytes 2703364
  21.1 4.3 %collective-permute-start.2 = (f32[904,128]{1,0:T(8,128)S(1)}, f32[904,128]{1,0:T(8,128)S(1)}, u32[]{:S(2)}, u32[]{:S(2)}) collective-permute-start(f32[904,128]{1,0:T(8,128)S(1)} %get-tuple-element.39), channel_id=1, source_target_pairs={{0,32},{32,0},{64,96},{96,64},{128,160},{160,128},{192,224},{224,1... | collective-permute-start | bytes 1388552 | tf_op jit(solution)/shard_map/ppermute | solution.py:509
  25.4 21.1 %collective-permute-start.3 = (f32[224,128]{1,0:T(8,128)S(1)}, f32[224,128]{1,0:T(8,128)S(1)}, u32[]{:S(2)}, u32[]{:S(2)}) collective-permute-start(f32[224,128]{1,0:T(8,128)S(1)} %get-tuple-element.48), channel_id=1, source_target_pairs={{0,64},{32,96},{64,128},{96,160},{128,192},{160,224},{192,0},{224,... | collective-permute-start | bytes 344072 | tf_op jit(solution)/shard_map/ppermute | solution.py:505
  28.7 17.8 %collective-permute-start.4 = (f32[224,128]{1,0:T(8,128)S(1)}, f32[224,128]{1,0:T(8,128)S(1)}, u32[]{:S(2)}, u32[]{:S(2)}) collective-permute-start(f32[224,128]{1,0:T(8,128)S(1)} %get-tuple-element.47), channel_id=1, source_target_pairs={{0,128},{32,160},{64,192},{96,224},{128,0},{160,32},{192,64},{224,... | collective-permute-start | bytes 344072 | tf_op jit(solution)/shard_map/ppermute | solution.py:505
  33.2 13.3 %collective-permute-start.5 = (f32[224,128]{1,0:T(8,128)S(1)}, f32[224,128]{1,0:T(8,128)S(1)}, u32[]{:S(2)}, u32[]{:S(2)}) collective-permute-start(f32[224,128]{1,0:T(8,128)S(1)} %get-tuple-element.46), channel_id=1, source_target_pairs={{0,192},{32,224},{64,0},{96,32},{128,64},{160,96},{192,128},{224,1... | collective-permute-start | bytes 344072 | tf_op jit(solution)/shard_map/ppermute | solution.py:505
  46.7 7.9 %collective-permute-start.6 = (f32[232,128]{1,0:T(8,128)S(1)}, f32[232,128]{1,0:T(8,128)S(1)}, u32[]{:S(2)}, u32[]{:S(2)}) collective-permute-start(f32[232,128]{1,0:T(8,128)S(1)} %get-tuple-element.50), channel_id=1, source_target_pairs={{0,128},{32,160},{64,192},{96,224},{128,0},{160,32},{192,64},{224,... | collective-permute-start | bytes 356360 | tf_op jit(solution)/shard_map/ppermute | solution.py:505
  48.4 13.2 %collective-permute-start.8 = (f32[232,128]{1,0:T(8,128)S(1)}, f32[232,128]{1,0:T(8,128)S(1)}, u32[]{:S(2)}, u32[]{:S(2)}) collective-permute-start(f32[232,128]{1,0:T(8,128)S(1)} %get-tuple-element.50), channel_id=1, source_target_pairs={{0,64},{32,96},{64,128},{96,160},{128,192},{160,224},{192,0},{224,... | collective-permute-start | bytes 356360 | tf_op jit(solution)/shard_map/ppermute | solution.py:505
  50.3 11.4 %collective-permute-start.9 = (f32[232,128]{1,0:T(8,128)S(1)}, f32[232,128]{1,0:T(8,128)S(1)}, u32[]{:S(2)}, u32[]{:S(2)}) collective-permute-start(f32[232,128]{1,0:T(8,128)S(1)} %get-tuple-element.50), channel_id=1, source_target_pairs={{0,192},{32,224},{64,0},{96,32},{128,64},{160,96},{192,128},{224,1... | collective-permute-start | bytes 356360 | tf_op jit(solution)/shard_map/ppermute | solution.py:505
  54.6 8.2 %collective-permute-start.7 = (f32[2,232,128]{2,1,0:T(8,128)S(1)}, f32[2,232,128]{2,1,0:T(8,128)S(1)}, u32[]{:S(2)}, u32[]{:S(2)}) collective-permute-start(f32[2,232,128]{2,1,0:T(8,128)S(1)} %pad_maximum_fusion.same.early), channel_id=1, source_target_pairs={{0,32},{32,0},{64,96},{96,64},{128,160},{160,128},{192,224},{224,1... | collective-permute-start | bytes 712712 | tf_op jit(solution)/shard_map/ppermute | solution.py:534
  61.8 1.8 %collective-permute-start.10 = (f32[2,232,128]{2,1,0:T(8,128)S(1)}, f32[2,232,128]{2,1,0:T(8,128)S(1)}, u32[]{:S(2)}, u32[]{:S(2)}) collective-permute-start(f32[2,232,128]{2,1,0:T(8,128)S(1)} %pad_maximum_fusion.1.same), channel_id=1, source_target_pairs={{0,32},{32,0},{64,96},{96,64},{128,160},{160,128},{192,224},{224,1... | collective-permute-start | bytes 712712 | tf_op jit(solution)/shard_map/ppermute | solution.py:548
